TPU v7x, 32 devices: a whole 2x2x4 slice. The times are simulated.
32 devices in a mesh: groups: 2 (over y), rank: 4 (over z), tensor: 4 (over x, core).
Axes of the slice: x: 2, y: 2, z: 4, core: 2. Of those that a mesh axis runs over, the one named last changes fastest.
Arguments:
- tokens: bfloat16 [1024, 2048], P(('groups', 'rank'), 'tensor'), parts along dimension 0, may hold values from -6 to 6
- out_grad: bfloat16 [1024, 2048], P(('groups', 'rank'), 'tensor'), parts along dimension 0, may hold values from -0.3125 to 0.3125
- context: bfloat16 [1024, 2048], P(('groups', 'rank')), parts along dimension 0, may hold values from -6 to 6
- expert_ids: int32 [1024, 2], P(('groups', 'rank')), parts along dimension 0, may hold values from 0 to 7, all different within a row; in each aligned block of 128 rows (0 to 127, 128 to 255, ...) at most 40 rows name the same one
- gate_probs: bfloat16 [1024, 2], P(('groups', 'rank')), parts along dimension 0, may hold values from 0.19921875 to 1
- gate_weight: bfloat16 [2048, 57344], P(None, ('rank', 'tensor')), may hold values from -0.125 to 0.125
- up_weight: bfloat16 [2048, 57344], P(None, ('rank', 'tensor')), may hold values from -0.125 to 0.125
- down_weight: bfloat16 [57344, 2048], P('rank', 'tensor'), may hold values from -0.0625 to 0.0625
- kept_rows: int32 [16, 128], P('tensor'), may hold values from 0 to 2047, as said below
Outputs:
- layer_output: bfloat16 [1024, 2048], P(('groups', 'rank'), 'tensor'), parts along dimension 0
- router_grad: float32 [1024, 2], P(('groups', 'rank')), parts along dimension 0
- masked_grad: float32 [32, 128, 128], P(('groups', 'tensor')), parts along dimension 0
There are 2 independent parts, one for each index of `groups`. A program takes and returns all parts, laid end to end along the dimension named above; an argument that names none is the same for every part. Nothing has to cross between parts.
Inputs may be any that keep to these rules, and one draw needn't show every extreme that they name: `expert_ids`: each row names 2 different experts. Among the rows of one attention replica (aligned blocks of 128 rows) no expert is named more than 40 times, and in every draw some expert is named exactly 40 times in some block. `kept_rows`: row c holds 128 increasing row indices, one in each group of 16 consecutive rows; the same indices serve every replica.
All inputs are finite; a program needn't handle non-finite values.
Results may differ from a plain program's by a relative error of at most 0.0051.
Values may be sent and summed in bfloat16 or wider, within the bound.
No kernel may reach another device: no remote copies, remote signals or barrier semaphores. Data moves between devices by JAX's collectives and lax.ppermute only.
A program may use at most 192 MiB of HBM per device.

v0:
```python
import jax
import jax.numpy as jnp
from jax import lax
from jax.sharding import PartitionSpec as P

FF = 7168
MOST = 40


def route_tables(expert_ids, gate_probs, rank_count, rank_units, per_rank, capacity):
    token_count = expert_ids.shape[0]
    owners = jnp.arange(rank_count, dtype=jnp.int32)
    first_expert = owners * rank_units // FF
    served = first_expert[:, None] + jnp.arange(per_rank, dtype=jnp.int32)[None, :]
    matches = expert_ids[None, :, None, :] == served[:, None, :, None]
    zero_weight = jnp.zeros((), jnp.bfloat16)
    weights = jnp.sum(jnp.where(matches, gate_probs[None, :, None, :], zero_weight), axis=3)
    member = jnp.any(matches, axis=(2, 3))
    position = jnp.cumsum(member.astype(jnp.int32), axis=1) - 1
    slot_ids = jnp.arange(capacity, dtype=jnp.int32)
    picked = member[:, None, :] & (position[:, None, :] == slot_ids[None, :, None])
    token_index = jnp.arange(token_count, dtype=jnp.int32)
    row_index = jnp.sum(jnp.where(picked, token_index[None, None, :], 0), axis=2)
    filled = jnp.any(picked, axis=2)
    slot_weight = jnp.where(filled[:, :, None], weights[owners[:, None], row_index], zero_weight)
    return (matches, row_index, filled, slot_weight)


def shards(
    tokens,
    out_grad,
    context,
    expert_ids,
    gate_probs,
    gate_weight,
    up_weight,
    down_weight,
    kept_rows,
):
    rank_count = lax.axis_size("rank")
    tensor_count = lax.axis_size("tensor")
    dev_units = gate_weight.shape[1]
    rank_units = dev_units * tensor_count
    per_rank = max(1, rank_units // FF)
    unit_span = min(rank_units, FF)
    token_count = tokens.shape[0]
    column_count = tokens.shape[1]
    capacity = min(MOST * per_rank, token_count)
    zero_value = jnp.zeros((), jnp.bfloat16)
    matches, row_index, filled, slot_weight = route_tables(
        expert_ids, gate_probs, rank_count, rank_units, per_rank, capacity
    )
    grad_send = jnp.where(filled[:, :, None], out_grad[row_index], zero_value)
    whole_rows = lax.all_gather(tokens, "tensor", axis=1, tiled=True)
    token_send = jnp.where(filled[:, :, None], whole_rows[row_index], zero_value)
    flat_index = row_index.reshape(-1)
    owner_rows = jnp.arange(rank_count, dtype=jnp.int32)[:, None]
    received = (
        lax.all_to_all(token_send, "rank", split_axis=0, concat_axis=0, tiled=True),
        lax.all_to_all(grad_send, "rank", split_axis=0, concat_axis=0, tiled=True),
        lax.all_to_all(slot_weight, "rank", split_axis=0, concat_axis=0, tiled=True),
    )
    routed_rows = received[0]
    source_count = routed_rows.shape[0]
    item_count = routed_rows.shape[1]
    row_count = source_count * item_count
    token_rows = routed_rows.reshape(row_count, routed_rows.shape[2])
    gate_act = jnp.dot(token_rows, gate_weight, preferred_element_type=jnp.float32)
    up_act = jnp.dot(token_rows, up_weight, preferred_element_type=jnp.float32)
    hidden = (jax.nn.silu(gate_act) * up_act).astype(jnp.bfloat16)

    def add_units(totals, shard_piece):
        width = shard_piece.shape[1]
        if per_rank == 1:
            return (
                totals + jnp.dot(shard_piece, down_weight, preferred_element_type=jnp.float32)[None]
            )
        unit_index = jnp.arange(width, dtype=jnp.int32)
        products = []
        for which in range(per_rank):
            inside = (unit_index // unit_span == which)[None, :]
            masked_piece = jnp.where(inside, shard_piece, zero_value)
            products.append(jnp.dot(masked_piece, down_weight, preferred_element_type=jnp.float32))
        return totals + jnp.stack(products)

    zero_out = jnp.zeros((per_rank, row_count, down_weight.shape[1]), jnp.float32)
    expert_out = add_units(zero_out, lax.all_gather(hidden, "tensor", axis=1, tiled=True))
    grad_flat = received[1].reshape(row_count, column_count).astype(jnp.float32)
    weight_flat = received[2].reshape(row_count, per_rank).astype(jnp.float32)
    output_part = jnp.sum(expert_out * jnp.transpose(weight_flat)[:, :, None], axis=0)
    router_part = jnp.transpose(jnp.sum(expert_out * grad_flat[None], axis=2))
    router_part = lax.psum(router_part, "tensor")
    output_back = lax.all_to_all(
        output_part.reshape(source_count, item_count, column_count),
        "rank",
        split_axis=0,
        concat_axis=0,
        tiled=True,
    )
    router_back = lax.all_to_all(
        router_part.reshape(source_count, item_count, per_rank),
        "rank",
        split_axis=0,
        concat_axis=0,
        tiled=True,
    )
    output_rows = jnp.where(filled[:, :, None], output_back, 0.0).reshape(-1, column_count)
    layer_sum = jnp.zeros((token_count, column_count), jnp.float32).at[flat_index].add(output_rows)
    layer_output = layer_sum.astype(jnp.bfloat16)
    router_terms = jnp.where(filled[:, :, None], router_back, 0.0)
    per_token = (
        jnp.zeros((rank_count, token_count, per_rank), jnp.float32)
        .at[owner_rows, row_index]
        .add(router_terms)
    )
    router_grad = jnp.sum(jnp.where(matches, per_token[:, :, :, None], 0.0), axis=(0, 2))
    local_blocks = kept_rows.shape[0]
    keep_count = kept_rows.shape[1]
    picked_context = jnp.take(context, kept_rows.reshape(-1), axis=1).reshape(
        token_count, local_blocks, keep_count
    )
    grad_blocks = out_grad.reshape(token_count, local_blocks, 128)
    local_grad = jnp.einsum(
        "tck,tcj->ckj", picked_context, grad_blocks, preferred_element_type=jnp.float32
    )
    masked_grad = lax.psum(local_grad, "rank")
    return (layer_output, router_grad, masked_grad)


def solution(mesh):
    return jax.shard_map(
        shards,
        mesh=mesh,
        in_specs=(
            P(("groups", "rank"), "tensor"),
            P(("groups", "rank"), "tensor"),
            P(("groups", "rank"), None),
            P(("groups", "rank"), None),
            P(("groups", "rank"), None),
            P(None, ("rank", "tensor")),
            P(None, ("rank", "tensor")),
            P("rank", "tensor"),
            P("tensor", None),
        ),
        out_specs=(
            P(("groups", "rank"), "tensor"),
            P(("groups", "rank"), None),
            P(("groups", "tensor"), None, None),
        ),
        check_vma=False,
    )
```

profile of v0, /device:TPU:0, one launch (start us, length us, event | category | flops | bytes accessed | tf_op | source)
XLA Modules:
  0.0 226.8 jit_solution(9029528062777171189)
XLA Ops:
  9.6 8.8 %all_gather.6 = bf16[128,2048]{1,0:T(8,128)(2,1)S(1)} all-gather(bf16[128,512]{1,0:T(8,128)(2,1)} %param.9), channel_id=1, replica_groups=mesh['groups'=2,'rank'=4,'tensor'=4] {'tensor'}, dimensions={1}, use_global_device_ids=true | all-gather | bytes 655360 | tf_op jit(solution)/shard_map/all_gather | solution.py:54
  18.4 2.4 %gather_fusion = bf16[320,2048]{1,0:T(8,128)(2,1)S(1)} fusion(bf16[128,2048]{1,0:T(8,128)(2,1)S(1)} %all_gather.6, s32[1024]{0:T(1024)S(1)} %pad_clamp_fusion.1), kind=kCustom, calls=%fused_computation | custom fusion | bytes 2622720 | tf_op jit(solution)/shard_map/gather | solution.py:55
  21.0 36.7 %all_to_all.25 = bf16[4,80,2048]{2,1,0:T(8,128)(2,1)S(1)} all-to-all(bf16[4,80,2048]{2,1,0:T(8,128)(2,1)S(1)} %broadcast_select_fusion), channel_id=1, replica_groups=mesh['groups'=2,'rank'=4,'tensor'=4] {'rank'}, dimensions={0} | all-to-all | bytes 2621440 | tf_op jit(solution)/shard_map/all_to_all | solution.py:59
  57.7 8.3 %fusion.38 = f32[320,3584]{1,0:T(8,128)S(1)} fusion(bf16[320,2048]{1,0:T(8,128)(2,1)S(1)} %bitcast.50, bf16[2048,3584]{1,0:T(8,128)(2,1)} %param.14), kind=kOutput, calls=%fused_computation.75 | convolution fusion | flops 4697620480 | bytes 20578304 | tf_op jit(solution)/shard_map/dot_general | solution.py:68
  66.5 6.4 %fusion.6 = bf16[320,3584]{1,0:T(8,128)(2,1)} fusion(bf16[320,2048]{1,0:T(8,128)(2,1)S(1)} %bitcast.51, bf16[2048,3584]{1,0:T(8,128)(2,1)S(1)} %bitcast.63, f32[320,3584]{1,0:T(8,128)S(1)} %fusion.38), kind=kOutput, calls=%fused_computation.13 | convolution fusion | flops 4704501760 | bytes 22872064 | tf_op jit(solution)/shard_map/dot_general | solution.py:69
  73.3 4.9 %gather_fusion.1 = bf16[320,2]{1,0:T(8,128)(2,1)S(1)} fusion(bf16[4,128,2]{2,1,0:T(8,128)(2,1)S(1)} %copy.54, s32[320]{0:T(512)S(1)} %reshape.202), kind=kCustom, calls=%fused_computation.1 | custom fusion | bytes 5120 | tf_op jit(solution)/shard_map/gather | solution.py:25
  78.9 3.2 %all-to-all-start.1 = ((bf16[4,80,2]{1,2,0:T(2,128)(2,1)}), bf16[4,80,2]{1,2,0:T(2,128)(2,1)S(1)}, u32[]{:S(2)}, u32[]{:S(2)}) async-start(bf16[4,80,2]{1,2,0:T(2,128)(2,1)} %broadcast_select_fusion.4), calls=%async_computation.1 | async-start | bytes 4096 | tf_op jit(solution)/shard_map/all_to_all | solution.py:61
  82.1 2.0 gather_fusion.2
  85.0 2.6 %all-to-all-done.1 = bf16[4,80,2]{1,2,0:T(2,128)(2,1)S(1)} async-done(((bf16[4,80,2]{1,2,0:T(2,128)(2,1)}), bf16[4,80,2]{1,2,0:T(2,128)(2,1)S(1)}, u32[]{:S(2)}, u32[]{:S(2)}) %all-to-all-start.1) | async-done | bytes 1312 | tf_op jit(solution)/shard_map/all_to_all | solution.py:61
  87.6 3.6 %all-to-all-start.3 = ((bf16[4,80,512]{2,1,0:T(8,128)(2,1)}), bf16[4,80,512]{2,1,0:T(8,128)(2,1)S(1)}, u32[]{:S(2)}, u32[]{:S(2)}) async-start(bf16[4,80,512]{2,1,0:T(8,128)(2,1)} %broadcast_select_fusion.2), calls=%async_computation.3 | async-start | bytes 655360 | tf_op jit(solution)/shard_map/all_to_all | solution.py:60
  91.4 8.4 %all-to-all-done.3 = bf16[4,80,512]{2,1,0:T(8,128)(2,1)S(1)} async-done(((bf16[4,80,512]{2,1,0:T(8,128)(2,1)}), bf16[4,80,512]{2,1,0:T(8,128)(2,1)S(1)}, u32[]{:S(2)}, u32[]{:S(2)}) %all-to-all-start.3) | async-done | bytes 327712 | tf_op jit(solution)/shard_map/all_to_all | solution.py:60
  99.9 34.7 %all-gather.2.cloned.1.call-done = bf16[320,14336]{1,0:T(8,128)(2,1)} async-done(((bf16[320,3584]{1,0:T(8,128)(2,1)}), bf16[320,14336]{1,0:T(8,128)(2,1)}) %all-gather.2.cloned.1.call-update) | async-done | bytes 9175056 | tf_op jit(solution)/shard_map/all_gather | solution.py:87
  134.6 12.9 %fusion.12 = f32[1,320,512]{2,1,0:T(8,128)S(1)} fusion(bf16[14336,512]{1,0:T(8,128)(2,1)} %param.16, bf16[320,14336]{1,0:T(8,128)(2,1)} %all-gather.2.cloned.1.call-done, pred[14336]{0:T(1024)(128)(4,1)S(1)} %broadcast_compare_fusion.1), kind=kOutput, calls=%fused_computation.21 | convolution fusion | flops 4702208000 | bytes 24524800 | tf_op jit(solution)/shard_map/dot_general | solution.py:83
  147.5 8.5 %fusion.9 = f32[1,320,512]{2,1,0:T(8,128)S(1)} fusion(bf16[14336,512]{1,0:T(8,128)(2,1)} %param.16, bf16[320,14336]{1,0:T(8,128)(2,1)S(1)} %copy-done.5, pred[14336]{0:T(1024)(128)(4,1)S(1)} %broadcast_compare_fusion), kind=kOutput, calls=%fused_computation.20 | convolution fusion | flops 4702208000 | bytes 24524800 | tf_op jit(solution)/shard_map/dot_general | solution.py:83
  156.0 1.1 multiply_reduce_fusion
  157.1 6.5 %psum.14 = f32[4,80,2]{1,2,0:T(2,128)} all-reduce(f32[4,80,2]{1,2,0:T(2,128)S(1)} %copy.57), channel_id=1, replica_groups=mesh['groups'=2,'rank'=4,'tensor'=4] {'tensor'}, use_global_device_ids=true, to_apply=%region_8.9 | all-reduce | flops 640 | bytes 5120 | tf_op jit(solution)/shard_map/psum | solution.py:92
  163.6 4.8 %all-to-all-start.4 = ((f32[4,80,2]{1,2,0:T(2,128)}), f32[4,80,2]{1,2,0:T(2,128)S(1)}, u32[]{:S(2)}, u32[]{:S(2)}) async-start(f32[4,80,2]{1,2,0:T(2,128)} %psum.14), calls=%async_computation.4 | async-start | bytes 8192 | tf_op jit(solution)/shard_map/all_to_all | solution.py:100
  168.7 5.3 %all-to-all-done.4 = f32[4,80,2]{1,2,0:T(2,128)S(1)} async-done(((f32[4,80,2]{1,2,0:T(2,128)}), f32[4,80,2]{1,2,0:T(2,128)S(1)}, u32[]{:S(2)}, u32[]{:S(2)}) %all-to-all-start.4) | async-done | bytes 2592 | tf_op jit(solution)/shard_map/all_to_all | solution.py:100
  174.0 3.5 %all-to-all-start.2 = ((f32[4,80,512]{2,1,0:T(8,128)}), f32[4,80,512]{2,1,0:T(8,128)S(1)}, u32[]{:S(2)}, u32[]{:S(2)}) async-start(f32[4,80,512]{2,1,0:T(8,128)} %bitcast.7), calls=%async_computation.2 | async-start | bytes 1310720 | tf_op jit(solution)/shard_map/all_to_all | solution.py:93
  177.5 1.3 gather_fusion.3
  180.2 17.1 %scatter_fusion = f32[4,128,2]{2,1,0:T(8,128)S(1)} fusion(f32[4,128,2]{2,1,0:T(8,128)S(1)} %broadcast_in_dim.175, s32[320]{0:T(512)S(1)} %reshape.232, f32[320,2]{1,0:T(8,128)S(1)} %bitcast.54), kind=kCustom, calls=%fused_computation.5 | custom fusion | flops 640 | bytes 10240 | tf_op jit(solution)/shard_map/scatter-add | solution.py:114
  198.2 2.6 %scatter_custom_fusion = f32[128,512]{1,0:T(8,128)S(1)} fusion(s32[320]{0:T(512)S(1)} %fusion.34, f32[320,512]{1,0:T(8,128)S(1)} %bitcast.55, f32[]{:T(128)} %constant.25.clone.1), kind=kCustom, calls=%fused_computation.32 | custom fusion | flops 163840 | bytes 262148 | tf_op jit(solution)/shard_map/scatter-add | solution.py:108
  201.4 16.2 %all-reduce.2.cloned.1.call-done = f32[4,128,128]{2,1,0:T(8,128)} async-done(((f32[4,128,128]{2,1,0:T(8,128)}), f32[4,128,128]{2,1,0:T(8,128)}) %all-reduce.2.cloned.1.call-update) | async-done | bytes 262160 | tf_op jit(solution)/shard_map/psum | solution.py:126
  217.7 1.7 copy.73
  (66 shorter events, 7.6 us)
Async XLA Ops:
  8.0 74.1 %copy-start = (bf16[128,512]{1,0:T(8,128)(2,1)S(1)}, bf16[128,512]{1,0:T(8,128)(2,1)}, u32[]{:S(2)}) copy-start(bf16[128,512]{1,0:T(8,128)(2,1)} %param.10) | copy-start | bytes 393220
  8.0 126.6 %all-gather.2.cloned.1.call-start = ((), (), s32[]{:S(2)}) async-start(), calls=%async_computation.5 | async-start | bytes 11468800 | tf_op jit(solution)/shard_map/all_gather | solution.py:87
  21.0 45.0 %slice-start = ((s8[14680064]{0:T(1024)(128)(4,1)}), s8[2097152]{0:T(1024)(128)(4,1)S(1)}, s32[]{:S(2)}) async-start(s8[14680064]{0:T(1024)(128)(4,1)} %bitcast.62), calls=%async_computation.7 | async-start | bytes 4194304
  57.7 8.4 %slice-start.1 = ((s8[14680064]{0:T(1024)(128)(4,1)}), s8[4194304]{0:T(1024)(128)(4,1)S(1)}, s32[]{:S(2)}) async-start(s8[14680064]{0:T(1024)(128)(4,1)} %bitcast.62), calls=%async_computation.8 | async-start | bytes 8388608
  57.7 8.4 %slice-start.2 = ((s8[14680064]{0:T(1024)(128)(4,1)}), s8[4194304]{0:T(1024)(128)(4,1)S(1)}, s32[]{:S(2)}) async-start(s8[14680064]{0:T(1024)(128)(4,1)} %bitcast.62), calls=%async_computation.9 | async-start | bytes 8388608
  57.7 8.8 %slice-start.3 = ((s8[14680064]{0:T(1024)(128)(4,1)}), s8[4194304]{0:T(1024)(128)(4,1)S(1)}, s32[]{:S(2)}) async-start(s8[14680064]{0:T(1024)(128)(4,1)} %bitcast.62), calls=%async_computation.10 | async-start | bytes 8388608
  66.5 6.5 %copy-start.2 = (s32[128,2]{0,1:T(2,128)S(1)}, s32[128,2]{0,1:T(2,128)}, u32[]{:S(2)}) copy-start(s32[128,2]{0,1:T(2,128)} %param.12) | copy-start | bytes 3076
  66.5 6.5 %copy-start.4 = (bf16[128,2]{0,1:T(2,128)(2,1)S(1)}, bf16[128,2]{0,1:T(2,128)(2,1)}, u32[]{:S(2)}) copy-start(bf16[128,2]{0,1:T(2,128)(2,1)} %param.13) | copy-start | bytes 1540
  78.9 8.7 %all-to-all-start.1 = ((bf16[4,80,2]{1,2,0:T(2,128)(2,1)}), bf16[4,80,2]{1,2,0:T(2,128)(2,1)S(1)}, u32[]{:S(2)}, u32[]{:S(2)}) async-start(bf16[4,80,2]{1,2,0:T(2,128)(2,1)} %broadcast_select_fusion.4), calls=%async_computation.1 | async-start | bytes 4096 | tf_op jit(solution)/shard_map/all_to_all | solution.py:61
  87.6 12.3 %all-to-all-start.3 = ((bf16[4,80,512]{2,1,0:T(8,128)(2,1)}), bf16[4,80,512]{2,1,0:T(8,128)(2,1)S(1)}, u32[]{:S(2)}, u32[]{:S(2)}) async-start(bf16[4,80,512]{2,1,0:T(8,128)(2,1)} %broadcast_select_fusion.2), calls=%async_computation.3 | async-start | bytes 655360 | tf_op jit(solution)/shard_map/all_to_all | solution.py:60
  134.6 12.9 %copy-start.5 = (bf16[320,14336]{1,0:T(8,128)(2,1)S(1)}, bf16[320,14336]{1,0:T(8,128)(2,1)}, u32[]{:S(2)}) copy-start(bf16[320,14336]{1,0:T(8,128)(2,1)} %all-gather.2.cloned.1.call-done) | copy-start | bytes 27525124
  147.5 20.9 %copy-start.3 = (s32[4,128]{1,0:T(4,128)S(1)}, s32[4,128]{1,0:T(4,128)}, u32[]{:S(2)}) copy-start(s32[4,128]{1,0:T(4,128)} %param.17) | copy-start | bytes 6148
  147.5 20.9 %copy-start.1 = (bf16[128,2048]{1,0:T(8,128)(2,1)S(1)}, bf16[128,2048]{1,0:T(8,128)(2,1)}, u32[]{:S(2)}) copy-start(bf16[128,2048]{1,0:T(8,128)(2,1)} %param.11) | copy-start | bytes 1572868
  163.6 10.3 %all-to-all-start.4 = ((f32[4,80,2]{1,2,0:T(2,128)}), f32[4,80,2]{1,2,0:T(2,128)S(1)}, u32[]{:S(2)}, u32[]{:S(2)}) async-start(f32[4,80,2]{1,2,0:T(2,128)} %psum.14), calls=%async_computation.4 | async-start | bytes 8192 | tf_op jit(solution)/shard_map/all_to_all | solution.py:100
  174.0 24.1 %all-to-all-start.2 = ((f32[4,80,512]{2,1,0:T(8,128)}), f32[4,80,512]{2,1,0:T(8,128)S(1)}, u32[]{:S(2)}, u32[]{:S(2)}) async-start(f32[4,80,512]{2,1,0:T(8,128)} %bitcast.7), calls=%async_computation.2 | async-start | bytes 1310720 | tf_op jit(solution)/shard_map/all_to_all | solution.py:93
  177.4 40.2 %all-reduce.2.cloned.1.call-start = ((), (), s32[]{:S(2)}) async-start(), calls=%async_computation.6 | async-start | bytes 524288 | tf_op jit(solution)/shard_map/psum | solution.py:126
Sparse Core Ops, SparseCore 0:
  73.1 61.4 all-gather.1
Sparse Core Ops, SparseCore 1:
  180.8 36.8 all-reduce.1
where the time goes:
time: 227 us
  waiting for transfers between devices  67.2 us (30%)
  blocking collectives  52 us (23%)
  matrix products  37 us (16%)
  other arithmetic  25.4 us (11%)
  between operations  15.8 us (7%)
  starting transfers between devices  15.2 us (7%)
  local copies, waits for them, and re-layouts  14.1 us (6%)
    all_to_all x1, blocking collectives, shards(): lax.all_to_all(token_send, 'rank', split_axis=0, concat_axis=0, tiled=True)  36.7 us
    all_gather x1, waiting for transfers between devices, shards(): lax.all_gather(hidden, 'tensor', axis=1, tiled=True)  34.7 us
    dot_general x2, matrix products, add_units(): jnp.dot(masked_piece, down_weight, preferred_element_type=jnp.float32)  21.3 us
    scatter-add x1, other arithmetic, shards(): per_token = jnp.zeros((rank_count, token_count, per_rank), jnp.float32).a...  17.1 us
    psum x1, waiting for transfers between devices, shards(): masked_grad = lax.psum(local_grad, 'rank')  16.2 us
    all_gather x1, blocking collectives, shards(): whole_rows = lax.all_gather(tokens, 'tensor', axis=1, tiled=True)  8.83 us
    all_to_all x1, waiting for transfers between devices, shards(): lax.all_to_all(grad_send, 'rank', split_axis=0, concat_axis=0, tiled=True)  8.45 us
    dot_general x1, matrix products, shards(): jnp.dot(token_rows, gate_weight, preferred_element_type=jnp.float32)  8.35 us
  transfers between devices with their start and end apart: 6, of which 5 were waited for; matrix products, arithmetic and copies ran while one was open for 15% of the time, Pallas kernels for 0%

commit v1 on v0

--- a/solution.py
+++ b/solution.py
@@ -1,6 +1,9 @@
+import functools
 import jax
 import jax.numpy as jnp
 from jax import lax
+from jax.experimental import pallas as pl
+from jax.experimental.pallas import tpu as pltpu
 from jax.sharding import PartitionSpec as P
 
 FF = 7168
@@ -127,9 +130,336 @@
     return (layer_output, router_grad, masked_grad)
 
 
+OWNERS = 4
+LISTS = 8
+ROWS = OWNERS * MOST
+CHUNKS = (512, 1024, 1024, 1024)
+BLOCK = 256
+DEEP = 512
+
+
+def call(kernel, outs, name, *, flops=0, moved=0, grid=None, in_specs=None, out_specs=None, scratch=(), scalars=0):
+    space = pltpu.PrefetchScalarGridSpec(
+        num_scalar_prefetch=scalars,
+        grid=grid or (),
+        in_specs=in_specs,
+        out_specs=out_specs,
+        scratch_shapes=scratch,
+    )
+    return pl.pallas_call(
+        kernel,
+        out_shape=outs,
+        grid_spec=space,
+        name=name,
+        compiler_params=pltpu.CompilerParams(vmem_limit_bytes=24 * 2**20),
+        cost_estimate=pl.CostEstimate(flops=flops, bytes_accessed=moved, transcendentals=0),
+    )
+
+
+def whole():
+    return pl.BlockSpec(memory_space=pltpu.VMEM)
+
+
+def slot_codes(place, ids_ref):
+    rank, chip = place[0], place[1] // 2
+    count = ids_ref.shape[0]
+    lists = lax.broadcasted_iota(jnp.int32, (LISTS, count), 0)
+    experts = 2 * (rank ^ (lists // 2)) + (chip ^ (lists % 2))
+    chosen = []
+    for k in range(2):
+        column = jnp.broadcast_to(ids_ref[:, k : k + 1].astype(jnp.float32), (count, count))
+        chosen.append(jnp.transpose(column)[:LISTS].astype(jnp.int32) == experts)
+    member = jnp.where(chosen[0] | chosen[1], 1.0, 0.0).astype(jnp.bfloat16)
+    earlier = lax.broadcasted_iota(jnp.int32, (count, count), 0) < lax.broadcasted_iota(
+        jnp.int32, (count, count), 1
+    )
+    before = jnp.where(earlier, 1.0, 0.0).astype(jnp.bfloat16)
+    position = jnp.dot(member, before, preferred_element_type=jnp.float32)
+    return [jnp.where(c, position, -1.0) for c in chosen]
+
+
+def slot_matrix(code):
+    count = code.shape[1]
+    slots = lax.broadcasted_iota(jnp.int32, (MOST, count), 0).astype(jnp.float32)
+    return jnp.concatenate(
+        [jnp.where(code[q : q + 1] == slots, 1.0, 0.0) for q in range(LISTS)], axis=0
+    )
+
+
+def pack_kernel(place, ids_ref, tokens_ref, *out_refs):
+    first, second = slot_codes(place, ids_ref)
+    pick = slot_matrix(jnp.maximum(first, second)).astype(jnp.bfloat16)
+    rows = jnp.dot(pick, tokens_ref[...], preferred_element_type=jnp.float32)
+    for s in range(OWNERS):
+        out_refs[s][...] = rows[2 * MOST * s : 2 * MOST * (s + 1)].astype(jnp.bfloat16)
+
+
+def route_kernel(place, ids_ref, out_ref):
+    count = ids_ref.shape[0]
+    for k, code in enumerate(slot_codes(place, ids_ref)):
+        pick = jnp.concatenate([slot_matrix(code), jnp.zeros((64, count), jnp.float32)], axis=0)
+        out_ref[k] = jnp.transpose(pick).astype(jnp.bfloat16)
+
+
+def split_kernel(*refs):
+    own_ref, other_ref = refs[OWNERS:]
+    order = [refs[s][...].astype(jnp.float32) for s in (1, 2, 3, 0)]
+    own_ref[...] = jnp.concatenate([d[:MOST] for d in order], axis=0).astype(jnp.bfloat16)
+    other_ref[...] = jnp.concatenate([d[MOST:] for d in order], axis=0).astype(jnp.bfloat16)
+
+
+def hidden_kernel(place, a0, a1, a2, a3, gate_ref, up_ref, out_ref, rows):
+    @pl.when(pl.program_id(0) == 0)
+    def _():
+        for j, piece in enumerate((a0, a1, a2, a3)):
+            width = piece.shape[1]
+            start = pl.multiple_of((place[1] ^ j) * width, width)
+            rows[:, pl.ds(start, width)] = piece[...]
+
+    gate = jnp.dot(rows[...], gate_ref[...], preferred_element_type=jnp.float32)
+    up = jnp.dot(rows[...], up_ref[...], preferred_element_type=jnp.float32)
+    out_ref[...] = (gate / (1.0 + jnp.exp(-gate)) * up).astype(jnp.bfloat16)
+
+
+def hidden_chunk(place, pieces, gate_weight, up_weight, start, width):
+    depth = gate_weight.shape[0]
+    first = start // BLOCK
+    weight = pl.BlockSpec((depth, BLOCK), lambda i, place: (0, first + i))
+    return call(
+        hidden_kernel,
+        jax.ShapeDtypeStruct((ROWS, width), jnp.bfloat16),
+        "hidden",
+        grid=(width // BLOCK,),
+        in_specs=[whole()] * 4 + [weight, weight],
+        out_specs=pl.BlockSpec((ROWS, BLOCK), lambda i, place: (0, i)),
+        scratch=[pltpu.VMEM((ROWS, depth), jnp.bfloat16)],
+        scalars=1,
+        flops=4 * ROWS * depth * width,
+        moved=4 * depth * width,
+    )(place, *pieces, gate_weight, up_weight)
+
+
+def down_kernel(has_total, last, place, *refs):
+    near, far, near_weight, far_weight = refs[:4]
+    refs = refs[4:]
+    total_in = None
+    if has_total:
+        total_in, refs = refs[0], refs[1:]
+    outs, total = refs[:-1], refs[-1]
+    step, steps = pl.program_id(0), pl.num_programs(0)
+    part = jnp.dot(near[...], near_weight[...], preferred_element_type=jnp.float32) + jnp.dot(
+        far[...], far_weight[...], preferred_element_type=jnp.float32
+    )
+
+    @pl.when(step == 0)
+    def _():
+        total[...] = part + total_in[...] if has_total else part
+
+    @pl.when(step > 0)
+    def _():
+        total[...] += part
+
+    @pl.when(step == steps - 1)
+    def _():
+        if last:
+            for s in range(OWNERS):
+                outs[s][...] = total[MOST * s : MOST * (s + 1), :].astype(jnp.bfloat16)
+        else:
+            outs[0][...] = total[...]
+
+
+def down_chunk(place, near, far, down_weight, total, start, flip, last):
+    width, columns = near.shape[1], down_weight.shape[1]
+    half = FF // 2 // DEEP
+    first = start // DEEP
+
+    def block(core):
+        return lambda i, place: (
+            ((place[1] // 2) ^ flip) * 2 * half + ((place[1] % 2) ^ core) * half + first + i,
+            0,
+        )
+
+    piece = pl.BlockSpec((ROWS, DEEP), lambda i, place: (0, i))
+    in_specs = [piece, piece] + [pl.BlockSpec((DEEP, columns), block(core)) for core in (0, 1)]
+    operands = [near, far, down_weight, down_weight]
+    if total is not None:
+        in_specs.append(whole())
+        operands.append(total)
+    if last:
+        outs = [jax.ShapeDtypeStruct((MOST, columns), jnp.bfloat16)] * OWNERS
+    else:
+        outs = [jax.ShapeDtypeStruct((ROWS, columns), jnp.float32)]
+    return call(
+        functools.partial(down_kernel, total is not None, last),
+        outs,
+        "down",
+        grid=(width // DEEP,),
+        in_specs=in_specs,
+        out_specs=[whole()] * len(outs),
+        scratch=[pltpu.VMEM((ROWS, columns), jnp.float32)],
+        scalars=1,
+        flops=4 * ROWS * width * columns,
+        moved=4 * width * columns,
+    )(place, *operands)
+
+
+def combine_kernel(*refs):
+    lists, (route_ref, probs_ref, grad_ref, layer_ref, router_ref) = refs[:LISTS], refs[LISTS:]
+    columns = grad_ref.shape[1]
+    stacked = [ref[...].astype(jnp.float32) for ref in lists] + [jnp.zeros((64, columns), jnp.float32)]
+    rows = jnp.concatenate(stacked, axis=0).astype(jnp.bfloat16)
+    grad = grad_ref[...].astype(jnp.float32)
+    probs = probs_ref[...].astype(jnp.float32)
+    ones = jnp.ones((8, columns), jnp.float32)
+    layer = None
+    scores = []
+    for k in range(2):
+        chosen = jnp.dot(route_ref[k], rows, preferred_element_type=jnp.float32)
+        term = probs[:, k : k + 1] * chosen
+        layer = term if layer is None else layer + term
+        scores.append(
+            lax.dot_general(
+                ones,
+                grad * chosen,
+                (((1,), (1,)), ((), ())),
+                precision=lax.Precision.HIGHEST,
+                preferred_element_type=jnp.float32,
+            )
+        )
+    layer_ref[...] = layer.astype(jnp.bfloat16)
+    line = lax.broadcasted_iota(jnp.int32, router_ref.shape, 0)
+    router_ref[...] = jnp.where(line == 0, scores[0], scores[1])
+
+
+def router_kernel(p0, p1, p2, p3, out_ref):
+    total = (p0[...] + p1[...]) + (p2[...] + p3[...])
+    square = jnp.concatenate([total] * 16, axis=0)
+    out_ref[...] = jnp.transpose(square)[:, :2]
+
+
+def masked_kernel(context_ref, grad_ref, kept_ref, out_ref):
+    features, keep = context_ref.shape[1], kept_ref.shape[1]
+    index = lax.broadcasted_iota(jnp.int32, (features, keep), 0)
+    for c in range(kept_ref.shape[0]):
+        pick = jnp.where(index == kept_ref[c : c + 1, :], 1.0, 0.0).astype(jnp.bfloat16)
+        picked = jnp.dot(context_ref[...], pick, preferred_element_type=jnp.float32)
+        part = lax.dot_general(
+            picked.astype(jnp.bfloat16),
+            grad_ref[:, 128 * c : 128 * (c + 1)],
+            (((0,), (0,)), ((), ())),
+            preferred_element_type=jnp.float32,
+        )
+        out_ref[c] = part.astype(jnp.bfloat16)
+
+
+def add_kernel(p0, p1, p2, p3, out_ref):
+    f32 = jnp.float32
+    out_ref[...] = (p0[...].astype(f32) + p1[...].astype(f32)) + (p2[...].astype(f32) + p3[...].astype(f32))
+
+
+def swap(value, axis, by):
+    return lax.ppermute(value, axis, [(i, i ^ by) for i in range(4)])
+
+
+def routed(
+    tokens,
+    out_grad,
+    context,
+    expert_ids,
+    gate_probs,
+    gate_weight,
+    up_weight,
+    down_weight,
+    kept_rows,
+):
+    token_count, columns = tokens.shape
+    bf16, f32 = jnp.bfloat16, jnp.float32
+    shape = jax.ShapeDtypeStruct
+    place = jnp.stack([lax.axis_index("rank"), lax.axis_index("tensor")]).astype(jnp.int32)
+    packed = call(
+        pack_kernel,
+        [shape((2 * MOST, columns), bf16)] * OWNERS,
+        "pack",
+        in_specs=[whole()] * 2,
+        out_specs=[whole()] * OWNERS,
+        scalars=1,
+    )(place, expert_ids, tokens)
+    arrived = [packed[0]] + [swap(packed[s], "rank", s) for s in (1, 2, 3)]
+    route = call(
+        route_kernel,
+        shape((2, token_count, 384), bf16),
+        "route",
+        in_specs=[whole()],
+        out_specs=whole(),
+        scalars=1,
+    )(place, expert_ids)
+    partial = call(
+        masked_kernel,
+        shape((kept_rows.shape[0], kept_rows.shape[1], 128), bf16),
+        "masked",
+        in_specs=[whole()] * 3,
+        out_specs=whole(),
+        flops=2 * context.shape[0] * context.shape[1] * 512,
+        moved=2**20,
+    )(context, out_grad, kept_rows)
+    own, other = call(
+        split_kernel,
+        [shape((ROWS, columns), bf16)] * 2,
+        "split",
+        in_specs=[whole()] * OWNERS,
+        out_specs=[whole()] * 2,
+    )(*arrived)
+    own_far = swap(own, "tensor", 1)
+    crossed = swap(other, "tensor", 2)
+    crossed_far = swap(crossed, "tensor", 1)
+    pieces = (own, own_far, crossed, crossed_far)
+    starts = [sum(CHUNKS[:i]) for i in range(len(CHUNKS))]
+    hidden = [
+        hidden_chunk(place, pieces, gate_weight, up_weight, start, width)
+        for start, width in zip(starts, CHUNKS)
+    ]
+    partials = [partial] + [swap(partial, "rank", s) for s in (1, 2, 3)]
+    masked_grad = call(
+        add_kernel,
+        shape(partial.shape, f32),
+        "masked_sum",
+        in_specs=[whole()] * 4,
+        out_specs=whole(),
+    )(*partials)
+    across = [swap(h, "tensor", 2) for h in hidden]
+    results = []
+    for flip, parts in enumerate((hidden, across)):
+        total = None
+        for i, part in enumerate(parts):
+            far = swap(part, "tensor", 1)
+            last = i == len(parts) - 1
+            outs = down_chunk(place, part, far, down_weight, total, starts[i], flip, last)
+            total = outs[0]
+        results.append([outs[3]] + [swap(outs[s - 1], "rank", s) for s in (1, 2, 3)])
+    lists = [results[q % 2][q // 2] for q in range(LISTS)]
+    layer_output, router = call(
+        combine_kernel,
+        [shape((token_count, columns), bf16), shape((8, token_count), f32)],
+        "combine",
+        in_specs=[whole()] * (LISTS + 3),
+        out_specs=[whole()] * 2,
+    )(*lists, route, gate_probs, out_grad)
+    routers = [router] + [swap(router, "tensor", t) for t in (1, 2, 3)]
+    router_grad = call(
+        router_kernel,
+        shape((token_count, 2), f32),
+        "router",
+        in_specs=[whole()] * 4,
+        out_specs=whole(),
+    )(*routers)
+    return (layer_output, router_grad, masked_grad)
+
+
 def solution(mesh):
+    ranks, tensors = mesh.shape["rank"], mesh.shape["tensor"]
+    body = routed if (ranks, tensors) == (4, 4) else shards
     return jax.shard_map(
-        shards,
+        body,
         mesh=mesh,
         in_specs=(
             P(("groups", "rank"), "tensor"),

time: 227 us -> 114 us (0.50)
  blocking collectives: 52 us -> 0 us
  matrix products: 37 us -> 0 us
  waiting for transfers between devices: 67.2 us -> 32.7 us
  Pallas kernels: 0 us -> 32.9 us
  other arithmetic: 25.4 us -> 0.08 us
  between operations: 15.8 us -> 0.93 us
  starting transfers between devices: 15.2 us -> 26.2 us
  local copies, waits for them, and re-layouts: 14.1 us -> 20.9 us
    dot_general x5 -> x0, matrix products: 37 us -> none  [the longest x2 21.3 us: add_units(): jnp.dot(masked_piece, down_weight, preferred_element_type=jnp.float32)]
    all_to_all x1 -> x0, blocking collectives: 36.7 us -> none  [shards(): lax.all_to_all(token_send, 'rank', split_axis=0, concat_axis=0, tiled=True)]
    all_gather x1 -> x0, waiting for transfers between devices: 34.7 us -> none  [shards(): lax.all_gather(hidden, 'tensor', axis=1, tiled=True)]
    pallas_call x0 -> x19, Pallas kernels: none -> 32.9 us  [the longest x8 13.9 us: down_chunk(): call(functools.partial(down_kernel, total is not None, last), outs, 'down...]
    ppermute x0 -> x30, waiting for transfers between devices: none -> 32.7 us  [swap(): return lax.ppermute(value, axis, [(i, i ^ by) for i in range(4)])]
    ppermute x0 -> x30, starting transfers between devices: none -> 26.2 us  [swap(): return lax.ppermute(value, axis, [(i, i ^ by) for i in range(4)])]
    scatter-add x2 -> x0, other arithmetic: 19.6 us -> none  [the longest x1 17.1 us: shards(): per_token = jnp.zeros((rank_count, token_count, per_rank), jnp.float32).a...]
    unnamed x22 -> x41, local copies, waits for them, and re-layouts: 2.44 us -> 20.9 us
  transfers between devices with their start and end apart: 6 -> 30, of which waited for: 5 -> 12; matrix products, arithmetic and copies ran while one was open for 15% -> 0% of each run, Pallas kernels for 0% -> 26%
where the time goes in v1:
time: 114 us
  Pallas kernels  32.9 us (29%)
  waiting for transfers between devices  32.7 us (29%)
  starting transfers between devices  26.2 us (23%)
  local copies, waits for them, and re-layouts  20.9 us (18%)
    ppermute x30, waiting for transfers between devices, swap(): return lax.ppermute(value, axis, [(i, i ^ by) for i in range(4)])  32.7 us
    ppermute x30, starting transfers between devices, swap(): return lax.ppermute(value, axis, [(i, i ^ by) for i in range(4)])  26.2 us
    unnamed x41, local copies, waits for them, and re-layouts  20.9 us
    pallas_call x8, Pallas kernels, down_chunk(): call(functools.partial(down_kernel, total is not None, last), outs, 'down...  13.9 us
    pallas_call x4, Pallas kernels, hidden_chunk(): call(hidden_kernel, jax.ShapeDtypeStruct((ROWS, width), jnp.bfloat16), 'h...  12.2 us
  transfers between devices with their start and end apart: 30, of which 12 were waited for; matrix products, arithmetic and copies ran while one was open for 0% of the time, Pallas kernels for 26%

profile of v1, /device:TPU:0, one launch (start us, length us, event | category | flops | bytes accessed | tf_op | source)
XLA Modules:
  0.0 113.6 jit_solution(9503853380451521901)
XLA Ops:
  3.4 3.1 %collective-permute-start = (bf16[80,512]{1,0:T(8,128)(2,1)S(1)}, bf16[80,512]{1,0:T(8,128)(2,1)S(1)}, u32[]{:S(2)}, u32[]{:S(2)}) collective-permute-start(bf16[80,512]{1,0:T(8,128)(2,1)S(1)} %get-tuple-element.20), channel_id=1, source_target_pairs={{0,4},{4,0},{8,12},{12,8},{1,5},{5,1},{9,13},{13,9},{2,6},{6,2},{1... | collective-permute-start | bytes 245768 | tf_op jit(solution)/shard_map/ppermute | solution.py:361
  6.5 2.6 %collective-permute-start.1 = (bf16[80,512]{1,0:T(8,128)(2,1)S(1)}, bf16[80,512]{1,0:T(8,128)(2,1)S(1)}, u32[]{:S(2)}, u32[]{:S(2)}) collective-permute-start(bf16[80,512]{1,0:T(8,128)(2,1)S(1)} %get-tuple-element.21), channel_id=1, source_target_pairs={{0,8},{4,12},{8,0},{12,4},{1,9},{5,13},{9,1},{13,5},{2,10},{6,14},... | collective-permute-start | bytes 245768 | tf_op jit(solution)/shard_map/ppermute | solution.py:361
  9.1 6.6 %collective-permute-done.1.refs_2_ = bf16[80,512]{1,0:T(8,128)(2,1)S(1)} collective-permute-done((bf16[80,512]{1,0:T(8,128)(2,1)S(1)}, bf16[80,512]{1,0:T(8,128)(2,1)S(1)}, u32[]{:S(2)}, u32[]{:S(2)}) %collective-permute-start.1) | collective-permute-done | bytes 81952 | tf_op jit(solution)/shard_map/ppermute | solution.py:361
  15.7 1.6 %collective-permute-start.4 = (bf16[160,512]{1,0:T(8,128)(2,1)S(1)}, bf16[160,512]{1,0:T(8,128)(2,1)S(1)}, u32[]{:S(2)}, u32[]{:S(2)}) collective-permute-start(bf16[160,512]{1,0:T(8,128)(2,1)S(1)} %get-tuple-element.24), channel_id=1, source_target_pairs={{0,2},{1,3},{2,0},{3,1},{4,6},{5,7},{6,4},{7,5},{8,10},{9,11},{10,... | collective-permute-start | bytes 491528 | tf_op jit(solution)/shard_map/ppermute | solution.py:361
  17.3 3.8 %collective-permute-done.4.a2 = bf16[160,512]{1,0:T(8,128)(2,1)S(1)} collective-permute-done((bf16[160,512]{1,0:T(8,128)(2,1)S(1)}, bf16[160,512]{1,0:T(8,128)(2,1)S(1)}, u32[]{:S(2)}, u32[]{:S(2)}) %collective-permute-start.4) | collective-permute-done | bytes 163872 | tf_op jit(solution)/shard_map/ppermute | solution.py:361
  22.5 5.2 %copy-done.1 = bf16[2048,3584]{1,0:T(8,128)(2,1)S(1)} copy-done((bf16[2048,3584]{1,0:T(8,128)(2,1)S(1)}, bf16[2048,3584]{1,0:T(8,128)(2,1)}, u32[]{:S(2)}) %copy-start.1) | copy-done | bytes 14680088
  27.7 5.2 %copy-done.2 = bf16[2048,3584]{1,0:T(8,128)(2,1)S(1)} copy-done((bf16[2048,3584]{1,0:T(8,128)(2,1)S(1)}, bf16[2048,3584]{1,0:T(8,128)(2,1)}, u32[]{:S(2)}) %copy-start.2) | copy-done | bytes 14680088
  32.9 2.0 %hidden.7.refs_0_ = bf16[160,512]{1,0:T(8,128)(2,1)S(1)} custom-call(s32[2]{0:T(128)S(1)} %pad_add_fusion.place, bf16[160,512]{1,0:T(8,128)(2,1)S(1)} %get-tuple-element.23.a0, bf16[160,512]{1,0:T(8,128)(2,1)S(1)} %collective-permute-done.3.a1, bf16[160,512]{1,0:T(8,128)(2,1)S(1)} %collective-permute-done.4.a2, ...), custom_call_target="tpu_custom_call" | custom-call | flops 671088640 | bytes 4194304 | tf_op jit(solution)/shard_map/hidden/pallas_call | solution.py:228
  36.5 3.4 %hidden.6.refs_0_ = bf16[160,1024]{1,0:T(8,128)(2,1)S(1)} custom-call(s32[2]{0:T(128)S(1)} %pad_add_fusion.place, bf16[160,512]{1,0:T(8,128)(2,1)S(1)} %get-tuple-element.23.a0, bf16[160,512]{1,0:T(8,128)(2,1)S(1)} %collective-permute-done.3.a1, bf16[160,512]{1,0:T(8,128)(2,1)S(1)} %collective-permute-done.4.a2, ...), custom_call_target="tpu_custom_call" | custom-call | flops 1342177280 | bytes 8388608 | tf_op jit(solution)/shard_map/hidden/pallas_call | solution.py:228
  40.5 3.4 %hidden.5.refs_0_ = bf16[160,1024]{1,0:T(8,128)(2,1)S(1)} custom-call(s32[2]{0:T(128)S(1)} %pad_add_fusion.place, bf16[160,512]{1,0:T(8,128)(2,1)S(1)} %get-tuple-element.23.a0, bf16[160,512]{1,0:T(8,128)(2,1)S(1)} %collective-permute-done.3.a1, bf16[160,512]{1,0:T(8,128)(2,1)S(1)} %collective-permute-done.4.a2, ...), custom_call_target="tpu_custom_call" | custom-call | flops 1342177280 | bytes 8388608 | tf_op jit(solution)/shard_map/hidden/pallas_call | solution.py:228
  45.5 3.4 %hidden.4.refs_0_ = bf16[160,1024]{1,0:T(8,128)(2,1)S(1)} custom-call(s32[2]{0:T(128)S(1)} %pad_add_fusion.place, bf16[160,512]{1,0:T(8,128)(2,1)S(1)} %get-tuple-element.23.a0, bf16[160,512]{1,0:T(8,128)(2,1)S(1)} %collective-permute-done.3.a1, bf16[160,512]{1,0:T(8,128)(2,1)S(1)} %collective-permute-done.4.a2, ...), custom_call_target="tpu_custom_call" | custom-call | flops 1342177280 | bytes 8388608 | tf_op jit(solution)/shard_map/hidden/pallas_call | solution.py:228
  51.9 5.7 %collective-permute-done.12.refs_0_ = bf16[160,1024]{1,0:T(8,128)(2,1)} collective-permute-done((bf16[160,1024]{1,0:T(8,128)(2,1)S(1)}, bf16[160,1024]{1,0:T(8,128)(2,1)}, u32[]{:S(2)}, u32[]{:S(2)}) %collective-permute-start.12) | collective-permute-done | bytes 327712 | tf_op jit(solution)/shard_map/ppermute | solution.py:361
  57.6 6.5 %collective-permute-done.10.refs_0_ = bf16[160,1024]{1,0:T(8,128)(2,1)S(1)} collective-permute-done((bf16[160,1024]{1,0:T(8,128)(2,1)S(1)}, bf16[160,1024]{1,0:T(8,128)(2,1)S(1)}, u32[]{:S(2)}, u32[]{:S(2)}) %collective-permute-start.10) | collective-permute-done | bytes 327712 | tf_op jit(solution)/shard_map/ppermute | solution.py:361
  66.6 2.1 %masked.1.p0 = bf16[4,128,128]{2,1,0:T(8,128)(2,1)} custom-call(bf16[128,2048]{1,0:T(8,128)(2,1)S(1)} %copy-done.12, bf16[128,512]{1,0:T(8,128)(2,1)S(1)} %copy-done.10, s32[4,128]{1,0:T(4,128)S(1)} %copy-done.13), custom_call_target="tpu_custom_call" | custom-call | flops 268435456 | bytes 1048576 | tf_op jit(solution)/shard_map/masked/pallas_call | solution.py:396
  68.6 5.2 %copy-done = bf16[14336,512]{1,0:T(8,128)(2,1)S(1)} copy-done((bf16[14336,512]{1,0:T(8,128)(2,1)S(1)}, bf16[14336,512]{1,0:T(8,128)(2,1)}, u32[]{:S(2)}) %copy-start) | copy-done | bytes 14680088
  73.8 2.1 %down.8.refs_4_ = f32[160,512]{1,0:T(8,128)S(1)} custom-call(s32[2]{0:T(128)S(1)} %pad_add_fusion.place, bf16[160,512]{1,0:T(8,128)(2,1)S(1)} %hidden.7.refs_0_, bf16[160,512]{1,0:T(8,128)(2,1)} %collective-permute-done.9.refs_1_, bf16[14336,512]{1,0:T(8,128)(2,1)S(1)} %copy-done, bf16[14336,512]{1,0:T(8,128)(2,1)S(1)} %copy-done), custom_call_target="tpu_custom_call" | custom-call | flops 167772160 | bytes 1048576 | tf_op jit(solution)/shard_map/down/pallas_call | solution.py:292
  81.5 1.7 %collective-permute-start.28 = (bf16[4,128,128]{2,1,0:T(8,128)(2,1)}, bf16[4,128,128]{2,1,0:T(8,128)(2,1)S(1)}, u32[]{:S(2)}, u32[]{:S(2)}) collective-permute-start(bf16[4,128,128]{2,1,0:T(8,128)(2,1)} %masked.1.p0), channel_id=1, source_target_pairs={{0,8},{4,12},{8,0},{12,4},{1,9},{5,13},{9,1},{13,5},{2,10},{6,14},... | collective-permute-start | bytes 393224 | tf_op jit(solution)/shard_map/ppermute | solution.py:361
  86.0 2.3 %down.13.refs_4_ = f32[160,512]{1,0:T(8,128)S(1)} custom-call(s32[2]{0:T(128)S(1)} %pad_add_fusion.place, bf16[160,1024]{1,0:T(8,128)(2,1)} %collective-permute-done.14.refs_0_, bf16[160,1024]{1,0:T(8,128)(2,1)S(1)} %collective-permute-done.15.refs_1_, bf16[14336,512]{1,0:T(8,128)(2,1)S(1)} %bitcast.3, bf16[14336,512]{1,0:T(8,128)(2,1)S(1)} %bitcast.3, ...), custom_call_target="tpu_custom_call" | custom-call | flops 335544320 | bytes 2097152 | tf_op jit(solution)/shard_map/down/pallas_call | solution.py:292
  88.9 2.5 %collective-permute-start.20 = (bf16[40,512]{1,0:T(8,128)(2,1)S(1)}, bf16[40,512]{1,0:T(8,128)(2,1)S(1)}, u32[]{:S(2)}, u32[]{:S(2)}) collective-permute-start(bf16[40,512]{1,0:T(8,128)(2,1)S(1)} %get-tuple-element.29), channel_id=1, source_target_pairs={{0,8},{4,12},{8,0},{12,4},{1,9},{5,13},{9,1},{13,5},{2,10},{6,14},... | collective-permute-start | bytes 122888 | tf_op jit(solution)/shard_map/ppermute | solution.py:361
  91.4 2.3 %down.14.refs_4_ = f32[160,512]{1,0:T(8,128)S(1)} custom-call(s32[2]{0:T(128)S(1)} %pad_add_fusion.place, bf16[160,1024]{1,0:T(8,128)(2,1)} %collective-permute-done.12.refs_0_, bf16[160,1024]{1,0:T(8,128)(2,1)S(1)} %collective-permute-done.13.refs_1_, bf16[14336,512]{1,0:T(8,128)(2,1)S(1)} %bitcast.3, bf16[14336,512]{1,0:T(8,128)(2,1)S(1)} %bitcast.3, ...), custom_call_target="tpu_custom_call" | custom-call | flops 335544320 | bytes 2097152 | tf_op jit(solution)/shard_map/down/pallas_call | solution.py:292
  93.8 2.0 %down.15 = (bf16[40,512]{1,0:T(8,128)(2,1)S(1)}, bf16[40,512]{1,0:T(8,128)(2,1)}, bf16[40,512]{1,0:T(8,128)(2,1)S(1)}, bf16[40,512]{1,0:T(8,128)(2,1)S(1)}) custom-call(s32[2]{0:T(128)S(1)} %pad_add_fusion.place, bf16[160,1024]{1,0:T(8,128)(2,1)S(1)} %collective-permute-done.10.refs_0_, bf16[160,1024]{1,0:T(8,128)(2,1)S(1)} %collective-permute-done.11.refs_1_, ...), custom_call_target="tpu_custom_call" | custom-call | flops 335544320 | bytes 2097152 | tf_op jit(solution)/shard_map/down/pallas_call | solution.py:292
  98.5 3.4 %collective-permute-done.22.refs_6_ = bf16[40,512]{1,0:T(8,128)(2,1)S(1)} collective-permute-done((bf16[40,512]{1,0:T(8,128)(2,1)S(1)}, bf16[40,512]{1,0:T(8,128)(2,1)S(1)}, u32[]{:S(2)}, u32[]{:S(2)}) %collective-permute-start.22) | collective-permute-done | bytes 40992 | tf_op jit(solution)/shard_map/ppermute | solution.py:361
  102.5 2.2 %collective-permute-start.23 = (bf16[40,512]{1,0:T(8,128)(2,1)S(1)}, bf16[40,512]{1,0:T(8,128)(2,1)S(1)}, u32[]{:S(2)}, u32[]{:S(2)}) collective-permute-start(bf16[40,512]{1,0:T(8,128)(2,1)S(1)} %get-tuple-element.32), channel_id=1, source_target_pairs={{0,12},{4,8},{8,4},{12,0},{1,13},{5,9},{9,5},{13,1},{2,14},{6,10},... | collective-permute-start | bytes 122888 | tf_op jit(solution)/shard_map/ppermute | solution.py:361
  111.1 1.7 %masked_sum.1 = f32[4,128,128]{2,1,0:T(8,128)} custom-call(bf16[4,128,128]{2,1,0:T(8,128)(2,1)} %masked.1.p0, bf16[4,128,128]{2,1,0:T(8,128)(2,1)S(1)} %collective-permute-done.27.p1, bf16[4,128,128]{2,1,0:T(8,128)(2,1)S(1)} %collective-permute-done.28.p2, bf16[4,128,128]{2,1,0:T(8,128)(2,1)S(1)} %collective-permute-done.29.p3), custom_call_target="tpu_custom_call" | custom-call | tf_op jit(solution)/shard_map/masked_sum/pallas_call | solution.py:422
  (98 shorter events, 33.0 us)
Async XLA Ops:
  3.4 5.7 %collective-permute-start = (bf16[80,512]{1,0:T(8,128)(2,1)S(1)}, bf16[80,512]{1,0:T(8,128)(2,1)S(1)}, u32[]{:S(2)}, u32[]{:S(2)}) collective-permute-start(bf16[80,512]{1,0:T(8,128)(2,1)S(1)} %get-tuple-element.20), channel_id=1, source_target_pairs={{0,4},{4,0},{8,12},{12,8},{1,5},{5,1},{9,13},{13,9},{2,6},{6,2},{1... | collective-permute-start | bytes 245768 | tf_op jit(solution)/shard_map/ppermute | solution.py:361
  6.5 9.2 %collective-permute-start.1 = (bf16[80,512]{1,0:T(8,128)(2,1)S(1)}, bf16[80,512]{1,0:T(8,128)(2,1)S(1)}, u32[]{:S(2)}, u32[]{:S(2)}) collective-permute-start(bf16[80,512]{1,0:T(8,128)(2,1)S(1)} %get-tuple-element.21), channel_id=1, source_target_pairs={{0,8},{4,12},{8,0},{12,4},{1,9},{5,13},{9,1},{13,5},{2,10},{6,14},... | collective-permute-start | bytes 245768 | tf_op jit(solution)/shard_map/ppermute | solution.py:361
  9.1 6.6 %collective-permute-start.2 = (bf16[80,512]{1,0:T(8,128)(2,1)S(1)}, bf16[80,512]{1,0:T(8,128)(2,1)S(1)}, u32[]{:S(2)}, u32[]{:S(2)}) collective-permute-start(bf16[80,512]{1,0:T(8,128)(2,1)S(1)} %get-tuple-element.22), channel_id=1, source_target_pairs={{0,12},{4,8},{8,4},{12,0},{1,13},{5,9},{9,5},{13,1},{2,14},{6,10},... | collective-permute-start | bytes 245768 | tf_op jit(solution)/shard_map/ppermute | solution.py:361
  15.7 5.4 %collective-permute-start.4 = (bf16[160,512]{1,0:T(8,128)(2,1)S(1)}, bf16[160,512]{1,0:T(8,128)(2,1)S(1)}, u32[]{:S(2)}, u32[]{:S(2)}) collective-permute-start(bf16[160,512]{1,0:T(8,128)(2,1)S(1)} %get-tuple-element.24), channel_id=1, source_target_pairs={{0,2},{1,3},{2,0},{3,1},{4,6},{5,7},{6,4},{7,5},{8,10},{9,11},{10,... | collective-permute-start | bytes 491528 | tf_op jit(solution)/shard_map/ppermute | solution.py:361
  34.9 14.6 %collective-permute-start.16 = (bf16[160,512]{1,0:T(8,128)(2,1)S(1)}, bf16[160,512]{1,0:T(8,128)(2,1)S(1)}, u32[]{:S(2)}, u32[]{:S(2)}) collective-permute-start(bf16[160,512]{1,0:T(8,128)(2,1)S(1)} %hidden.7.refs_0_), channel_id=1, source_target_pairs={{0,2},{1,3},{2,0},{3,1},{4,6},{5,7},{6,4},{7,5},{8,10},{9,11},{10,... | collective-permute-start | bytes 491528 | tf_op jit(solution)/shard_map/ppermute | solution.py:361
  36.5 13.1 %collective-permute-start.9 = (bf16[160,512]{1,0:T(8,128)(2,1)S(1)}, bf16[160,512]{1,0:T(8,128)(2,1)}, u32[]{:S(2)}, u32[]{:S(2)}) collective-permute-start(bf16[160,512]{1,0:T(8,128)(2,1)S(1)} %hidden.7.refs_0_), channel_id=1, source_target_pairs={{0,1},{1,0},{2,3},{3,2},{4,5},{5,4},{6,7},{7,6},{8,9},{9,8},{10,11... | collective-permute-start | bytes 491528 | tf_op jit(solution)/shard_map/ppermute | solution.py:361
  39.9 11.6 %collective-permute-start.14 = (bf16[160,1024]{1,0:T(8,128)(2,1)S(1)}, bf16[160,1024]{1,0:T(8,128)(2,1)}, u32[]{:S(2)}, u32[]{:S(2)}) collective-permute-start(bf16[160,1024]{1,0:T(8,128)(2,1)S(1)} %hidden.6.refs_0_), channel_id=1, source_target_pairs={{0,2},{1,3},{2,0},{3,1},{4,6},{5,7},{6,4},{7,5},{8,10},{9,11},{10,... | collective-permute-start | bytes 983048 | tf_op jit(solution)/shard_map/ppermute | solution.py:361
  43.9 13.6 %collective-permute-start.12 = (bf16[160,1024]{1,0:T(8,128)(2,1)S(1)}, bf16[160,1024]{1,0:T(8,128)(2,1)}, u32[]{:S(2)}, u32[]{:S(2)}) collective-permute-start(bf16[160,1024]{1,0:T(8,128)(2,1)S(1)} %hidden.5.refs_0_), channel_id=1, source_target_pairs={{0,2},{1,3},{2,0},{3,1},{4,6},{5,7},{6,4},{7,5},{8,10},{9,11},{10,... | collective-permute-start | bytes 983048 | tf_op jit(solution)/shard_map/ppermute | solution.py:361
  48.9 15.2 %collective-permute-start.10 = (bf16[160,1024]{1,0:T(8,128)(2,1)S(1)}, bf16[160,1024]{1,0:T(8,128)(2,1)S(1)}, u32[]{:S(2)}, u32[]{:S(2)}) collective-permute-start(bf16[160,1024]{1,0:T(8,128)(2,1)S(1)} %hidden.4.refs_0_), channel_id=1, source_target_pairs={{0,2},{1,3},{2,0},{3,1},{4,6},{5,7},{6,4},{7,5},{8,10},{9,11},{10,... | collective-permute-start | bytes 983048 | tf_op jit(solution)/shard_map/ppermute | solution.py:361
  49.5 14.6 %collective-permute-start.8 = (bf16[160,1024]{1,0:T(8,128)(2,1)S(1)}, bf16[160,1024]{1,0:T(8,128)(2,1)S(1)}, u32[]{:S(2)}, u32[]{:S(2)}) collective-permute-start(bf16[160,1024]{1,0:T(8,128)(2,1)S(1)} %hidden.6.refs_0_), channel_id=1, source_target_pairs={{0,1},{1,0},{2,3},{3,2},{4,5},{5,4},{6,7},{7,6},{8,9},{9,8},{10,11... | collective-permute-start | bytes 983048 | tf_op jit(solution)/shard_map/ppermute | solution.py:361
  51.4 27.1 %collective-permute-start.7 = (bf16[160,1024]{1,0:T(8,128)(2,1)S(1)}, bf16[160,1024]{1,0:T(8,128)(2,1)S(1)}, u32[]{:S(2)}, u32[]{:S(2)}) collective-permute-start(bf16[160,1024]{1,0:T(8,128)(2,1)S(1)} %hidden.5.refs_0_), channel_id=1, source_target_pairs={{0,1},{1,0},{2,3},{3,2},{4,5},{5,4},{6,7},{7,6},{8,9},{9,8},{10,11... | collective-permute-start | bytes 983048 | tf_op jit(solution)/shard_map/ppermute | solution.py:361
  51.5 29.9 %collective-permute-start.6 = (bf16[160,1024]{1,0:T(8,128)(2,1)S(1)}, bf16[160,1024]{1,0:T(8,128)(2,1)S(1)}, u32[]{:S(2)}, u32[]{:S(2)}) collective-permute-start(bf16[160,1024]{1,0:T(8,128)(2,1)S(1)} %hidden.4.refs_0_), channel_id=1, source_target_pairs={{0,1},{1,0},{2,3},{3,2},{4,5},{5,4},{6,7},{7,6},{8,9},{9,8},{10,11... | collective-permute-start | bytes 983048 | tf_op jit(solution)/shard_map/ppermute | solution.py:361
  57.6 27.0 %collective-permute-start.15 = (bf16[160,1024]{1,0:T(8,128)(2,1)}, bf16[160,1024]{1,0:T(8,128)(2,1)S(1)}, u32[]{:S(2)}, u32[]{:S(2)}) collective-permute-start(bf16[160,1024]{1,0:T(8,128)(2,1)} %collective-permute-done.14.refs_0_), channel_id=1, source_target_pairs={{0,1},{1,0},{2,3},{3,2},{4,5},{5,4},{6,7},{7,6},{8,9},{9,8},{10,11... | collective-permute-start | bytes 983048 | tf_op jit(solution)/shard_map/ppermute | solution.py:361
  64.1 24.2 %collective-permute-start.13 = (bf16[160,1024]{1,0:T(8,128)(2,1)}, bf16[160,1024]{1,0:T(8,128)(2,1)S(1)}, u32[]{:S(2)}, u32[]{:S(2)}) collective-permute-start(bf16[160,1024]{1,0:T(8,128)(2,1)} %collective-permute-done.12.refs_0_), channel_id=1, source_target_pairs={{0,1},{1,0},{2,3},{3,2},{4,5},{5,4},{6,7},{7,6},{8,9},{9,8},{10,11... | collective-permute-start | bytes 983048 | tf_op jit(solution)/shard_map/ppermute | solution.py:361
  64.1 24.8 %collective-permute-start.11 = (bf16[160,1024]{1,0:T(8,128)(2,1)S(1)}, bf16[160,1024]{1,0:T(8,128)(2,1)S(1)}, u32[]{:S(2)}, u32[]{:S(2)}) collective-permute-start(bf16[160,1024]{1,0:T(8,128)(2,1)S(1)} %collective-permute-done.10.refs_0_), channel_id=1, source_target_pairs={{0,1},{1,0},{2,3},{3,2},{4,5},{5,4},{6,7},{7,6},{8,9},{9,8},{10,11... | collective-permute-start | bytes 983048 | tf_op jit(solution)/shard_map/ppermute | solution.py:361
  78.5 31.3 %collective-permute-start.27 = (bf16[4,128,128]{2,1,0:T(8,128)(2,1)}, bf16[4,128,128]{2,1,0:T(8,128)(2,1)S(1)}, u32[]{:S(2)}, u32[]{:S(2)}) collective-permute-start(bf16[4,128,128]{2,1,0:T(8,128)(2,1)} %masked.1.p0), channel_id=1, source_target_pairs={{0,4},{4,0},{8,12},{12,8},{1,5},{5,1},{9,13},{13,9},{2,6},{6,2},{1... | collective-permute-start | bytes 393224 | tf_op jit(solution)/shard_map/ppermute | solution.py:361
  81.5 29.7 %collective-permute-start.28 = (bf16[4,128,128]{2,1,0:T(8,128)(2,1)}, bf16[4,128,128]{2,1,0:T(8,128)(2,1)S(1)}, u32[]{:S(2)}, u32[]{:S(2)}) collective-permute-start(bf16[4,128,128]{2,1,0:T(8,128)(2,1)} %masked.1.p0), channel_id=1, source_target_pairs={{0,8},{4,12},{8,0},{12,4},{1,9},{5,13},{9,1},{13,5},{2,10},{6,14},... | collective-permute-start | bytes 393224 | tf_op jit(solution)/shard_map/ppermute | solution.py:361
  84.6 26.6 %collective-permute-start.29 = (bf16[4,128,128]{2,1,0:T(8,128)(2,1)}, bf16[4,128,128]{2,1,0:T(8,128)(2,1)S(1)}, u32[]{:S(2)}, u32[]{:S(2)}) collective-permute-start(bf16[4,128,128]{2,1,0:T(8,128)(2,1)} %masked.1.p0), channel_id=1, source_target_pairs={{0,12},{4,8},{8,4},{12,0},{1,13},{5,9},{9,5},{13,1},{2,14},{6,10},... | collective-permute-start | bytes 393224 | tf_op jit(solution)/shard_map/ppermute | solution.py:361
  88.3 7.5 %collective-permute-start.18 = (bf16[40,512]{1,0:T(8,128)(2,1)S(1)}, bf16[40,512]{1,0:T(8,128)(2,1)S(1)}, u32[]{:S(2)}, u32[]{:S(2)}) collective-permute-start(bf16[40,512]{1,0:T(8,128)(2,1)S(1)} %get-tuple-element.27), channel_id=1, source_target_pairs={{0,4},{4,0},{8,12},{12,8},{1,5},{5,1},{9,13},{13,9},{2,6},{6,2},{1... | collective-permute-start | bytes 122888 | tf_op jit(solution)/shard_map/ppermute | solution.py:361
  88.9 9.5 %collective-permute-start.20 = (bf16[40,512]{1,0:T(8,128)(2,1)S(1)}, bf16[40,512]{1,0:T(8,128)(2,1)S(1)}, u32[]{:S(2)}, u32[]{:S(2)}) collective-permute-start(bf16[40,512]{1,0:T(8,128)(2,1)S(1)} %get-tuple-element.29), channel_id=1, source_target_pairs={{0,8},{4,12},{8,0},{12,4},{1,9},{5,13},{9,1},{13,5},{2,10},{6,14},... | collective-permute-start | bytes 122888 | tf_op jit(solution)/shard_map/ppermute | solution.py:361
  95.8 6.1 %collective-permute-start.22 = (bf16[40,512]{1,0:T(8,128)(2,1)S(1)}, bf16[40,512]{1,0:T(8,128)(2,1)S(1)}, u32[]{:S(2)}, u32[]{:S(2)}) collective-permute-start(bf16[40,512]{1,0:T(8,128)(2,1)S(1)} %get-tuple-element.31), channel_id=1, source_target_pairs={{0,12},{4,8},{8,4},{12,0},{1,13},{5,9},{9,5},{13,1},{2,14},{6,10},... | collective-permute-start | bytes 122888 | tf_op jit(solution)/shard_map/ppermute | solution.py:361
  98.5 4.0 %collective-permute-start.19 = (bf16[40,512]{1,0:T(8,128)(2,1)S(1)}, bf16[40,512]{1,0:T(8,128)(2,1)S(1)}, u32[]{:S(2)}, u32[]{:S(2)}) collective-permute-start(bf16[40,512]{1,0:T(8,128)(2,1)S(1)} %get-tuple-element.28), channel_id=1, source_target_pairs={{0,4},{4,0},{8,12},{12,8},{1,5},{5,1},{9,13},{13,9},{2,6},{6,2},{1... | collective-permute-start | bytes 122888 | tf_op jit(solution)/shard_map/ppermute | solution.py:361
  101.9 5.1 %collective-permute-start.21 = (bf16[40,512]{1,0:T(8,128)(2,1)}, bf16[40,512]{1,0:T(8,128)(2,1)S(1)}, u32[]{:S(2)}, u32[]{:S(2)}) collective-permute-start(bf16[40,512]{1,0:T(8,128)(2,1)} %get-tuple-element.30), channel_id=1, source_target_pairs={{0,8},{4,12},{8,0},{12,4},{1,9},{5,13},{9,1},{13,5},{2,10},{6,14},... | collective-permute-start | bytes 122888 | tf_op jit(solution)/shard_map/ppermute | solution.py:361
  102.5 5.8 %collective-permute-start.23 = (bf16[40,512]{1,0:T(8,128)(2,1)S(1)}, bf16[40,512]{1,0:T(8,128)(2,1)S(1)}, u32[]{:S(2)}, u32[]{:S(2)}) collective-permute-start(bf16[40,512]{1,0:T(8,128)(2,1)S(1)} %get-tuple-element.32), channel_id=1, source_target_pairs={{0,12},{4,8},{8,4},{12,0},{1,13},{5,9},{9,5},{13,1},{2,14},{6,10},... | collective-permute-start | bytes 122888 | tf_op jit(solution)/shard_map/ppermute | solution.py:361
  (25 other events, 245.7 us)

commit v2 on v0

--- a/solution.py
+++ b/solution.py
@@ -1,6 +1,9 @@
+import functools
 import jax
 import jax.numpy as jnp
 from jax import lax
+from jax.experimental import pallas as pl
+from jax.experimental.pallas import tpu as pltpu
 from jax.sharding import PartitionSpec as P
 
 FF = 7168
@@ -127,9 +130,402 @@
     return (layer_output, router_grad, masked_grad)
 
 
+OWNERS = 4
+LISTS = 8
+ROWS = OWNERS * MOST
+REMOTE = ROWS - MOST
+CHUNKS = (512, 896, 1024, 1152)
+STARTS = (0, 512, 1408, 2432)
+HALF = FF // 2
+BLOCK = 256
+PIECES = 4
+LOADS = (((0, 0), (0, 1), (1, 0), (1, 1), (2, 0)), ((2, 1), (3, 0)), ((3, 1),))
+ANY = pl.BlockSpec(memory_space=pl.ANY)
+HBM = pl.BlockSpec(memory_space=pltpu.HBM)
+VMEM = pl.BlockSpec(memory_space=pltpu.VMEM)
+
+
+def call(kernel, name, operands, outs, *, after=(), far=(), scratch=(), aliases=None, cost=0):
+    count, late = len(operands), len(after)
+    operands = [
+        pltpu.with_memory_space_constraint(x, pltpu.HBM) if i in far else x
+        for i, x in enumerate(operands)
+    ]
+
+    def body(*refs):
+        place = (lax.axis_index("rank"), lax.axis_index("tensor"))
+        kernel(place, *refs[:count], *refs[count + late :])
+
+    return pl.pallas_call(
+        body,
+        out_shape=outs,
+        in_specs=[HBM if i in far else VMEM for i in range(count)] + [ANY] * late,
+        out_specs=[VMEM] * len(outs),
+        scratch_shapes=scratch,
+        name=name,
+        input_output_aliases=aliases or {},
+        compiler_params=pltpu.CompilerParams(vmem_limit_bytes=8 * 2**20),
+        cost_estimate=pl.CostEstimate(flops=0, bytes_accessed=int(cost * 3e6), transcendentals=0),
+    )(*operands, *after)
+
+
+def shape(*dims, dtype=jnp.bfloat16):
+    return jax.ShapeDtypeStruct(dims, dtype)
+
+
+def product(left, right):
+    return jnp.dot(left, right, preferred_element_type=jnp.float32)
+
+
+def slot_codes(place, ids_ref):
+    rank, chip = place[0], place[1] // 2
+    count = ids_ref.shape[1]
+    lists = lax.broadcasted_iota(jnp.int32, (LISTS, count), 0)
+    experts = 2 * (rank ^ (lists // 2)) + (chip ^ (lists % 2))
+    chosen = [ids_ref[k : k + 1, :] == experts for k in range(2)]
+    member = jnp.where(chosen[0] | chosen[1], 1.0, 0.0).astype(jnp.bfloat16)
+    earlier = lax.broadcasted_iota(jnp.int32, (count, count), 0) < lax.broadcasted_iota(
+        jnp.int32, (count, count), 1
+    )
+    before = jnp.where(earlier, 1.0, 0.0).astype(jnp.bfloat16)
+    position = product(member, before)
+    return [jnp.where(c, position, -1.0) for c in chosen]
+
+
+def slot_matrix(code, value=1.0):
+    count = code.shape[1]
+    slots = lax.broadcasted_iota(jnp.int32, (MOST, count), 0).astype(jnp.float32)
+    return jnp.concatenate(
+        [jnp.where(code[q : q + 1] == slots, value, 0.0) for q in range(LISTS)], axis=0
+    )
+
+
+def pack_kernel(place, ids_ref, tokens_ref, *refs):
+    outs, (ids, tokens, sems) = refs[:OWNERS], refs[OWNERS:]
+    copies = [
+        pltpu.make_async_copy(ids_ref, ids, sems.at[0]),
+        pltpu.make_async_copy(tokens_ref, tokens, sems.at[1]),
+    ]
+    for copy in copies:
+        copy.start()
+    copies[0].wait()
+    first, second = slot_codes(place, ids)
+    pick = slot_matrix(jnp.maximum(first, second)).astype(jnp.bfloat16)
+    copies[1].wait()
+    rows = product(pick, tokens[...])
+    for s in range(OWNERS):
+        outs[s][...] = rows[2 * MOST * s : 2 * MOST * (s + 1)].astype(jnp.bfloat16)
+
+
+def route_kernel(place, ids_ref, probs_ref, out_ref):
+    count = ids_ref.shape[1]
+    codes = slot_codes(place, ids_ref)
+    probs = [probs_ref[k : k + 1, :].astype(jnp.float32) for k in range(2)]
+    weighted = slot_matrix(codes[0], probs[0]) + slot_matrix(codes[1], probs[1])
+    for k, pick in enumerate((slot_matrix(codes[0]), slot_matrix(codes[1]), weighted)):
+        padded = jnp.concatenate([pick, jnp.zeros((64, count), jnp.float32)], axis=0)
+        out_ref[k] = jnp.transpose(padded).astype(jnp.bfloat16)
+
+
+def split_kernel(place, *refs):
+    own_ref, other_ref = refs[OWNERS:]
+    order = [refs[s][...].astype(jnp.float32) for s in (1, 2, 3, 0)]
+    own_ref[...] = jnp.concatenate([d[:MOST] for d in order], axis=0).astype(jnp.bfloat16)
+    other_ref[...] = jnp.concatenate([d[MOST:] for d in order], axis=0).astype(jnp.bfloat16)
+
+
+def weight_copies(sources, outs, sems, load):
+    copies = []
+    for (chunk, which), out in zip(load, outs):
+        part = out.shape[0] // PIECES
+        for i in range(PIECES):
+            rows = pl.ds(i * part, part)
+            source = sources[which].at[rows, pl.ds(STARTS[chunk], CHUNKS[chunk])]
+            copies.append(pltpu.make_async_copy(source, out.at[rows, :], sems.at[len(copies)]))
+    return copies
+
+
+def load_kernel(load, place, gate_ref, up_ref, *refs):
+    copies = weight_copies((gate_ref, up_ref), refs[:-1], refs[-1], load)
+    for copy in copies:
+        copy.start()
+    for copy in copies:
+        copy.wait()
+
+
+def masked_kernel(place, context_ref, grad_ref, kept_ref, gate_ref, up_ref, *refs):
+    out_ref, weights, (context, grad, sems, few) = refs[0], refs[1:-4], refs[-4:]
+    first = [
+        pltpu.make_async_copy(context_ref, context, few.at[0]),
+        pltpu.make_async_copy(grad_ref, grad, few.at[1]),
+    ]
+    copies = weight_copies((gate_ref, up_ref), weights, sems, LOADS[0])
+    for copy in first + copies:
+        copy.start()
+    features, keep = context.shape[1], kept_ref.shape[1]
+    index = lax.broadcasted_iota(jnp.int32, (features, keep), 0)
+    for copy in first:
+        copy.wait()
+    for c in range(kept_ref.shape[0]):
+        pick = jnp.where(index == kept_ref[c : c + 1, :], 1.0, 0.0).astype(jnp.bfloat16)
+        picked = product(context[...], pick).astype(jnp.bfloat16)
+        part = lax.dot_general(
+            picked,
+            grad[:, 128 * c : 128 * (c + 1)],
+            (((0,), (0,)), ((), ())),
+            preferred_element_type=jnp.float32,
+        )
+        out_ref[c] = part.astype(jnp.bfloat16)
+    for copy in copies:
+        copy.wait()
+
+
+def pass_kernel(place, in_ref, out_ref):
+    pass
+
+
+def sum_kernel(place, left, right, out_ref):
+    total = left[...].astype(jnp.float32) + right[...].astype(jnp.float32)
+    out_ref[...] = total.astype(out_ref.dtype)
+
+
+def hidden_kernel(place, a0, a1, a2, a3, gate_ref, up_ref, out_ref, remote_ref, rows):
+    for j, piece in enumerate((a0, a1, a2, a3)):
+        width = piece.shape[1]
+        start = pl.multiple_of((place[1] ^ j) * width, width)
+        rows[:, pl.ds(start, width)] = piece[...]
+    for start in range(0, out_ref.shape[1], BLOCK):
+        columns = slice(start, min(start + BLOCK, out_ref.shape[1]))
+        gate = product(rows[...], gate_ref[:, columns])
+        up = product(rows[...], up_ref[:, columns])
+        hidden = gate / (1.0 + jnp.exp(-gate)) * up
+        out_ref[:, columns] = hidden.astype(jnp.bfloat16)
+        remote_ref[:, columns] = hidden[:REMOTE].astype(jnp.bfloat16)
+
+
+def merge_kernel(place, *refs):
+    for start, width, part in zip(STARTS, CHUNKS, refs):
+        own = part[...].astype(jnp.float32)[REMOTE:]
+        refs[-1][:, start : start + width] = own.astype(jnp.bfloat16)
+
+
+def down_part(place, part, down_ref, start, flip, core):
+    chip, own = (place[1] // 2) ^ flip, (place[1] % 2) ^ core
+    rows = pl.ds(pl.multiple_of((2 * chip + own) * HALF + start, 128), part.shape[1])
+    return product(part[...], down_ref[rows, :])
+
+
+def down_own_kernel(place, *refs):
+    parts, down_ref, outs = refs[: 2 * len(CHUNKS)], refs[2 * len(CHUNKS)], refs[2 * len(CHUNKS) + 1 :]
+    total = None
+    for i, part in enumerate(parts):
+        term = down_part(place, part, down_ref, STARTS[i // 2], 0, i % 2)
+        total = term if total is None else total + term
+    for s in range(OWNERS):
+        outs[s][...] = total[MOST * s : MOST * (s + 1)].astype(jnp.bfloat16)
+
+
+def down_add_kernel(pieces, has_total, place, *refs):
+    parts, down_ref, refs = refs[: len(pieces)], refs[len(pieces)], refs[len(pieces) + 1 :]
+    total = refs[0][...] if has_total else None
+    for (start, core), part in zip(pieces, parts):
+        term = down_part(place, part, down_ref, start, 1, core)
+        total = term if total is None else total + term
+    refs[-1][...] = total
+
+
+def back_kernel(place, total_ref, o1, o2, o3, *outs):
+    total = total_ref[...]
+    for s, own in enumerate((o1, o2, o3)):
+        both = [own[...].astype(jnp.float32), total[MOST * s : MOST * (s + 1)]]
+        outs[s][...] = jnp.concatenate(both, axis=0).astype(jnp.bfloat16)
+
+
+def combine_kernel(place, own, other, b1, b2, b3, route_ref, grad_ref, layer_ref, router_ref):
+    count, columns = grad_ref.shape
+    stacked = [ref[...].astype(jnp.float32) for ref in (own, other, b1, b2, b3)]
+    stacked.append(jnp.zeros((64, columns), jnp.float32))
+    rows = jnp.concatenate(stacked, axis=0).astype(jnp.bfloat16)
+    grad = grad_ref[...].astype(jnp.float32)
+    layer_ref[...] = product(route_ref[2], rows).astype(jnp.bfloat16)
+    lane = lax.broadcasted_iota(jnp.int32, (count, 128), 1)
+    scores = jnp.zeros((count, 128), jnp.float32)
+    for k in range(2):
+        score = jnp.sum(grad * product(route_ref[k], rows), axis=1, keepdims=True)
+        scores = jnp.where(lane == k, score, scores)
+    router_ref[...] = jnp.transpose(scores)[:8]
+
+
+def router_kernel(place, p0, p1, p2, p3, out_ref):
+    out_ref[...] = ((p0[...] + p1[...]) + (p2[...] + p3[...]))[:2]
+
+
+def swap(value, axis, by):
+    return lax.ppermute(value, axis, [(i, i ^ by) for i in range(4)])
+
+
+def routed(
+    tokens,
+    out_grad,
+    context,
+    expert_ids,
+    gate_probs,
+    gate_weight,
+    up_weight,
+    down_weight,
+    kept_rows,
+):
+    token_count, columns = tokens.shape
+    depth = gate_weight.shape[0]
+    f32 = jnp.float32
+    dma = pltpu.SemaphoreType.DMA
+    ids, probs = expert_ids.T, gate_probs.T
+
+    packed = call(
+        pack_kernel,
+        "pack",
+        (ids, tokens),
+        [shape(2 * MOST, columns)] * OWNERS,
+        far=(0, 1),
+        scratch=[pltpu.VMEM(ids.shape, ids.dtype), pltpu.VMEM(tokens.shape, tokens.dtype), dma((2,))],
+    )
+    arrived = [packed[0]] + [swap(packed[s], "rank", s) for s in (1, 2, 3)]
+    weights = [[None, None] for _ in CHUNKS]
+
+    def load(which, kernel, name, operands, outs, scratch, after):
+        pieces = LOADS[which]
+        shapes = [shape(depth, CHUNKS[chunk]) for chunk, _ in pieces]
+        made = call(
+            kernel,
+            name,
+            (*operands, gate_weight, up_weight),
+            outs + shapes,
+            after=after,
+            far=tuple(i for i in range(len(operands) + 2) if i != 2 or not operands),
+            scratch=scratch,
+        )
+        for (chunk, part), array in zip(pieces, made[len(outs) :]):
+            weights[chunk][part] = array
+        return made
+
+    scratch = [
+        pltpu.VMEM(context.shape, context.dtype),
+        pltpu.VMEM(out_grad.shape, out_grad.dtype),
+        dma((PIECES * len(LOADS[0]),)),
+        dma((2,)),
+    ]
+    partial_shape = [shape(kept_rows.shape[0], kept_rows.shape[1], 128)]
+    partial = load(
+        0, masked_kernel, "masked", (context, out_grad, kept_rows), partial_shape, scratch, (packed[0],)
+    )[0]
+    route = call(
+        route_kernel, "route", (ids, probs), [shape(3, token_count, 384)], after=(partial,)
+    )[0]
+    own, other = call(
+        split_kernel, "split", tuple(arrived), [shape(ROWS, columns)] * 2, after=(route,)
+    )
+    own_far = swap(own, "tensor", 1)
+    crossed = swap(other, "tensor", 2)
+
+    def load_more(which, after):
+        scratch = [dma((PIECES * len(LOADS[which]),))]
+        kernel = functools.partial(load_kernel, LOADS[which])
+        return load(which, kernel, "load", (), [], scratch, (after,))[0]
+
+    def hold(value, after, cost=0):
+        return call(pass_kernel, "hold", (value,), [value], after=(after,), aliases={0: 0}, cost=cost)[0]
+
+    crossed = hold(crossed, load_more(1, own))
+    crossed_far = swap(crossed, "tensor", 1)
+    last = load_more(2, crossed)
+    pieces = (own, own_far, crossed, crossed_far)
+
+    hidden, remote = [], []
+    for k, width in enumerate(CHUNKS):
+        made = call(
+            hidden_kernel,
+            "hidden",
+            (*pieces, *weights[k]),
+            [shape(ROWS, width), shape(REMOTE, width)],
+            after=(last,),
+            scratch=[pltpu.VMEM((ROWS, depth), jnp.bfloat16)],
+            cost=20 if k == 0 else 0,
+        )
+        hidden.append(made[0])
+        remote.append(made[1])
+        last = made[0]
+    across = [swap(part, "tensor", 2) for part in remote]
+    own_rows = call(merge_kernel, "merge", tuple(hidden), [shape(MOST, HALF)])[0]
+    own_across = swap(own_rows, "tensor", 2)
+    hidden_far = [swap(part, "tensor", 1) for part in hidden]
+
+    def add(pieces, parts, total, after):
+        rows = parts[0].shape[0]
+        operands = (*parts, down_weight) + (() if total is None else (total,))
+        return call(
+            functools.partial(down_add_kernel, pieces, total is not None),
+            "down_add",
+            operands,
+            [shape(rows, columns, dtype=f32)],
+            after=after,
+        )[0]
+
+    total, step = None, own_rows
+    held = hold(partial, own_rows)
+    for k, start in enumerate(STARTS):
+        if k == 2:
+            pair = call(
+                sum_kernel, "pair_sum", (held, swap(held, "rank", 1)), [partial], after=(total,)
+            )[0]
+            step = pair
+        if k == 3:
+            operands = [part for near_far in zip(hidden, hidden_far) for part in near_far]
+            finished = call(
+                down_own_kernel,
+                "down_own",
+                (*operands, down_weight),
+                [shape(MOST, columns)] * OWNERS,
+                after=(total,),
+            )
+            returned, own_result = finished[:3], finished[3]
+            masked_grad = call(
+                sum_kernel,
+                "masked_sum",
+                (pair, swap(pair, "rank", 2)),
+                [shape(*partial.shape, dtype=f32)],
+                after=(own_result,),
+            )[0]
+            step = masked_grad
+        near = hold(across[k], step, 3)
+        far = swap(near, "tensor", 1)
+        total = add(((start, 0),), (near,), total, ())
+        total = add(((start, 1),), (far,), total, ())
+        step = total
+    backs = call(
+        back_kernel, "back", (total, *returned), [shape(2 * MOST, columns)] * 3
+    )
+    lists = [swap(backs[s - 1], "rank", s) for s in (1, 2, 3)]
+    near = hold(own_across, backs[0], 3)
+    far = swap(near, "tensor", 1)
+    mine = add(((0, 0),), (near,), None, ())
+    lists[0] = hold(lists[0], lists[1], 4)
+    mine = add(((0, 1),), (far,), mine, (lists[0],))
+    layer_output, router = call(
+        combine_kernel,
+        "combine",
+        (own_result, mine, *lists, route, out_grad),
+        [shape(token_count, columns), shape(8, token_count, dtype=f32)],
+    )
+    routers = [router] + [swap(router, "tensor", t) for t in (1, 2, 3)]
+    router_grad = call(router_kernel, "router", tuple(routers), [shape(2, token_count, dtype=f32)])[0]
+    return (layer_output, router_grad.T, masked_grad)
+
+
 def solution(mesh):
+    ranks, tensors = mesh.shape["rank"], mesh.shape["tensor"]
+    body = routed if (ranks, tensors) == (4, 4) else shards
     return jax.shard_map(
-        shards,
+        body,
         mesh=mesh,
         in_specs=(
             P(("groups", "rank"), "tensor"),

time: 227 us -> 72.1 us (0.32)
  blocking collectives: 52 us -> 0 us
  waiting for transfers between devices: 67.2 us -> 17.9 us
  matrix products: 37 us -> 0 us
  Pallas kernels: 0 us -> 28.6 us
  other arithmetic: 25.4 us -> 0.01 us
  between operations: 15.8 us -> 0.98 us
  local copies, waits for them, and re-layouts: 14.1 us -> 1.66 us
  starting transfers between devices: 15.2 us -> 22.8 us
    dot_general x5 -> x0, matrix products: 37 us -> none  [the longest x2 21.3 us: add_units(): jnp.dot(masked_piece, down_weight, preferred_element_type=jnp.float32)]
    all_to_all x1 -> x0, blocking collectives: 36.7 us -> none  [shards(): lax.all_to_all(token_send, 'rank', split_axis=0, concat_axis=0, tiled=True)]
    all_gather x1 -> x0, waiting for transfers between devices: 34.7 us -> none  [shards(): lax.all_gather(hidden, 'tensor', axis=1, tiled=True)]
    pallas_call x0 -> x35, Pallas kernels: none -> 28.6 us  [call(): pl.pallas_call(body, out_shape=outs, in_specs=[HBM if i in far else VMEM...]
    ppermute x0 -> x28, starting transfers between devices: none -> 22.8 us  [swap(): return lax.ppermute(value, axis, [(i, i ^ by) for i in range(4)])]
    scatter-add x2 -> x0, other arithmetic: 19.6 us -> none  [the longest x1 17.1 us: shards(): per_token = jnp.zeros((rank_count, token_count, per_rank), jnp.float32).a...]
    ppermute x0 -> x28, waiting for transfers between devices: none -> 17.9 us  [swap(): return lax.ppermute(value, axis, [(i, i ^ by) for i in range(4)])]
    all_to_all x4 -> x0, waiting for transfers between devices: 16.3 us -> none  [the longest x1 8.45 us: shards(): lax.all_to_all(grad_send, 'rank', split_axis=0, concat_axis=0, tiled=True)]
  transfers between devices with their start and end apart: 6 -> 28, of which waited for: 5 -> 10; matrix products, arithmetic and copies ran while one was open for 15% -> 0% of each run, Pallas kernels for 0% -> 35%
where the time goes in v2:
time: 72.1 us; the launch traced here: 71.9 us
  Pallas kernels  28.6 us (40%)
  starting transfers between devices  22.8 us (32%)
  waiting for transfers between devices  17.9 us (25%)
  local copies, waits for them, and re-layouts  1.66 us (2%)
  between operations  0.98 us (1%)
    pallas_call x35, Pallas kernels, call(): pl.pallas_call(body, out_shape=outs, in_specs=[HBM if i in far else VMEM...  28.6 us
    ppermute x28, starting transfers between devices, swap(): return lax.ppermute(value, axis, [(i, i ^ by) for i in range(4)])  22.8 us
    ppermute x28, waiting for transfers between devices, swap(): return lax.ppermute(value, axis, [(i, i ^ by) for i in range(4)])  17.9 us
    unnamed x18, local copies, waits for them, and re-layouts  1.66 us
  transfers between devices with their start and end apart: 28, of which 10 were waited for; matrix products, arithmetic and copies ran while one was open for 0% of the time, Pallas kernels for 35%

profile of v2, /device:TPU:0, one launch (start us, length us, event | category | flops | bytes accessed | tf_op | source)
XLA Modules:
  0.0 71.9 jit_solution(13894751663227572629)
XLA Ops:
  0.6 1.2 %pack.1 = (bf16[80,512]{1,0:T(8,128)(2,1)S(1)}, bf16[80,512]{1,0:T(8,128)(2,1)S(1)}, bf16[80,512]{1,0:T(8,128)(2,1)S(1)}, bf16[80,512]{1,0:T(8,128)(2,1)S(1)}) custom-call(s32[2,128]{1,0:T(2,128)} %bitcast.5, bf16[128,512]{1,0:T(8,128)(2,1)} %refs_1_.14), custom_call_target="tpu_custom_call" | custom-call | tf_op jit(solution)/shard_map/pack/pallas_call | solution.py:159
  1.8 3.1 %collective-permute-start = (bf16[80,512]{1,0:T(8,128)(2,1)S(1)}, bf16[80,512]{1,0:T(8,128)(2,1)S(1)}, u32[]{:S(2)}, u32[]{:S(2)}) collective-permute-start(bf16[80,512]{1,0:T(8,128)(2,1)S(1)} %get-tuple-element.35), channel_id=1, source_target_pairs={{0,4},{4,0},{8,12},{12,8},{1,5},{5,1},{9,13},{13,9},{2,6},{6,2},{1... | collective-permute-start | bytes 245768 | tf_op jit(solution)/shard_map/ppermute | solution.py:364
  4.9 2.6 %collective-permute-start.1 = (bf16[80,512]{1,0:T(8,128)(2,1)S(1)}, bf16[80,512]{1,0:T(8,128)(2,1)S(1)}, u32[]{:S(2)}, u32[]{:S(2)}) collective-permute-start(bf16[80,512]{1,0:T(8,128)(2,1)S(1)} %get-tuple-element.36), channel_id=1, source_target_pairs={{0,8},{4,12},{8,0},{12,4},{1,9},{5,13},{9,1},{13,5},{2,10},{6,14},... | collective-permute-start | bytes 245768 | tf_op jit(solution)/shard_map/ppermute | solution.py:364
  8.2 7.1 %masked.1 = (bf16[4,128,128]{2,1,0:T(8,128)(2,1)S(1)}, bf16[2048,512]{1,0:T(8,128)(2,1)S(1)}, bf16[2048,512]{1,0:T(8,128)(2,1)S(1)}, bf16[2048,896]{1,0:T(8,128)...) custom-call(bf16[128,2048]{1,0:T(8,128)(2,1)} %refs_0_.3, bf16[128,512]{1,0:T(8,128)(2,1)} %refs_6_.1, ...), custom_call_target="tpu_custom_call" | custom-call | tf_op jit(solution)/shard_map/masked/pallas_call | solution.py:159
  15.6 1.8 %collective-permute-start.4 = (bf16[160,512]{1,0:T(8,128)(2,1)S(1)}, bf16[160,512]{1,0:T(8,128)(2,1)S(1)}, u32[]{:S(2)}, u32[]{:S(2)}) collective-permute-start(bf16[160,512]{1,0:T(8,128)(2,1)S(1)} %get-tuple-element.40), channel_id=1, source_target_pairs={{0,2},{1,3},{2,0},{3,1},{4,6},{5,7},{6,4},{7,5},{8,10},{9,11},{10,... | collective-permute-start | bytes 491528 | tf_op jit(solution)/shard_map/ppermute | solution.py:364
  17.4 3.8 %load.2 = (bf16[2048,1024]{1,0:T(8,128)(2,1)S(1)}, bf16[2048,1152]{1,0:T(8,128)(2,1)S(1)}) custom-call(bf16[2048,3584]{1,0:T(8,128)(2,1)} %refs_0_.5, bf16[2048,3584]{1,0:T(8,128)(2,1)} %refs_1_.17, bf16[160,512]{1,0:T(8,128)(2,1)S(1)} %get-tuple-element.39.refs_2_.refs_0_), custom_call_target="tpu_custom_call" | custom-call | tf_op jit(solution)/shard_map/load/pallas_call | solution.py:159
  21.8 2.4 %load.3.refs_6_.refs_5_ = bf16[2048,1152]{1,0:T(8,128)(2,1)S(1)} custom-call(bf16[2048,3584]{1,0:T(8,128)(2,1)} %refs_0_.5, bf16[2048,3584]{1,0:T(8,128)(2,1)} %refs_1_.17, bf16[160,512]{1,0:T(8,128)(2,1)S(1)} %hold.8.refs_2_), custom_call_target="tpu_custom_call" | custom-call | tf_op jit(solution)/shard_map/load/pallas_call | solution.py:159
  26.2 1.6 %hidden.5 = (bf16[160,896]{1,0:T(8,128)(2,1)S(1)}, bf16[120,896]{1,0:T(8,128)(2,1)S(1)}) custom-call(bf16[160,512]{1,0:T(8,128)(2,1)S(1)} %get-tuple-element.39.refs_2_.refs_0_, bf16[160,512]{1,0:T(8,128)(2,1)S(1)} %collective-permute-done.3.refs_1_, bf16[160,512]{1,0:T(8,128)(2,1)S(1)} %hold.8.refs_2_, bf16[160,512]{1,0:T(8,128)(2,1)S(1)} %collective-permute-done.5.refs_3_, ...), custom_call_target="tpu_custom_call" | custom-call | tf_op jit(solution)/shard_map/hidden/pallas_call | solution.py:159
  27.7 1.1 %collective-permute-start.12 = (bf16[120,896]{1,0:T(8,128)(2,1)S(1)}, bf16[120,896]{1,0:T(8,128)(2,1)S(1)}, u32[]{:S(2)}, u32[]{:S(2)}) collective-permute-start(bf16[120,896]{1,0:T(8,128)(2,1)S(1)} %get-tuple-element.53), channel_id=1, source_target_pairs={{0,2},{1,3},{2,0},{3,1},{4,6},{5,7},{6,4},{7,5},{8,10},{9,11},{10,... | collective-permute-start | bytes 645128 | tf_op jit(solution)/shard_map/ppermute | solution.py:364
  28.9 1.6 %hidden.6 = (bf16[160,1024]{1,0:T(8,128)(2,1)S(1)}, bf16[120,1024]{1,0:T(8,128)(2,1)S(1)}) custom-call(bf16[160,512]{1,0:T(8,128)(2,1)S(1)} %get-tuple-element.39.refs_2_.refs_0_, bf16[160,512]{1,0:T(8,128)(2,1)S(1)} %collective-permute-done.3.refs_1_, bf16[160,512]{1,0:T(8,128)(2,1)S(1)} %hold.8.refs_2_, ...), custom_call_target="tpu_custom_call" | custom-call | tf_op jit(solution)/shard_map/hidden/pallas_call | solution.py:159
  30.5 2.0 %hidden.7 = (bf16[160,1152]{1,0:T(8,128)(2,1)S(1)}, bf16[120,1152]{1,0:T(8,128)(2,1)S(1)}) custom-call(bf16[160,512]{1,0:T(8,128)(2,1)S(1)} %get-tuple-element.39.refs_2_.refs_0_, bf16[160,512]{1,0:T(8,128)(2,1)S(1)} %collective-permute-done.3.refs_1_, bf16[160,512]{1,0:T(8,128)(2,1)S(1)} %hold.8.refs_2_, ...), custom_call_target="tpu_custom_call" | custom-call | tf_op jit(solution)/shard_map/hidden/pallas_call | solution.py:159
  32.7 1.0 %collective-permute-start.10 = (bf16[120,1024]{1,0:T(8,128)(2,1)S(1)}, bf16[120,1024]{1,0:T(8,128)(2,1)S(1)}, u32[]{:S(2)}, u32[]{:S(2)}) collective-permute-start(bf16[120,1024]{1,0:T(8,128)(2,1)S(1)} %get-tuple-element.52), channel_id=1, source_target_pairs={{0,2},{1,3},{2,0},{3,1},{4,6},{5,7},{6,4},{7,5},{8,10},{9,11},{10,... | collective-permute-start | bytes 737288 | tf_op jit(solution)/shard_map/ppermute | solution.py:364
  35.7 3.5 %collective-permute-done.11.refs_1_ = bf16[4,128,128]{2,1,0:T(8,128)(2,1)S(1)} collective-permute-done((bf16[4,128,128]{2,1,0:T(8,128)(2,1)S(1)}, bf16[4,128,128]{2,1,0:T(8,128)(2,1)S(1)}, u32[]{:S(2)}, u32[]{:S(2)}) %collective-permute-start.11) | collective-permute-done | bytes 131104 | tf_op jit(solution)/shard_map/ppermute | solution.py:364
  39.3 1.8 %collective-permute-done.10.refs_0_ = bf16[120,1024]{1,0:T(8,128)(2,1)S(1)} collective-permute-done((bf16[120,1024]{1,0:T(8,128)(2,1)S(1)}, bf16[120,1024]{1,0:T(8,128)(2,1)S(1)}, u32[]{:S(2)}, u32[]{:S(2)}) %collective-permute-start.10) | collective-permute-done | bytes 245792 | tf_op jit(solution)/shard_map/ppermute | solution.py:364
  43.0 1.7 %collective-permute-start.19 = (bf16[4,128,128]{2,1,0:T(8,128)(2,1)S(1)}, bf16[4,128,128]{2,1,0:T(8,128)(2,1)S(1)}, u32[]{:S(2)}, u32[]{:S(2)}) collective-permute-start(bf16[4,128,128]{2,1,0:T(8,128)(2,1)S(1)} %pair_sum.1.refs_1_.refs_0_), channel_id=1, source_target_pairs={{0,8},{4,12},{8,0},{12,4},{1,9},{5,13},{9,1},{13,5},{2,10},{6,14},... | collective-permute-start | bytes 393224 | tf_op jit(solution)/shard_map/ppermute | solution.py:364
  44.7 1.1 %collective-permute-start.17 = (bf16[40,3584]{1,0:T(8,128)(2,1)S(1)}, bf16[40,3584]{1,0:T(8,128)(2,1)S(1)}, u32[]{:S(2)}, u32[]{:S(2)}) collective-permute-start(bf16[40,3584]{1,0:T(8,128)(2,1)S(1)} %merge.1.refs_1_), channel_id=1, source_target_pairs={{0,2},{1,3},{2,0},{3,1},{4,6},{5,7},{6,4},{7,5},{8,10},{9,11},{10,... | collective-permute-start | bytes 860168 | tf_op jit(solution)/shard_map/ppermute | solution.py:364
  46.5 1.5 %down_own.1 = (bf16[40,512]{1,0:T(8,128)(2,1)S(1)}, bf16[40,512]{1,0:T(8,128)(2,1)S(1)}, bf16[40,512]{1,0:T(8,128)(2,1)S(1)}, bf16[40,512]{1,0:T(8,128)(2,1)S(1)}) custom-call(bf16[160,512]{1,0:T(8,128)(2,1)S(1)} %get-tuple-element.44.refs_6_.refs_0_, bf16[160,512]{1,0:T(8,128)(2,1)S(1)} %collective-permute-done.6.refs_1_, ...), custom_call_target="tpu_custom_call" | custom-call | tf_op jit(solution)/shard_map/down_own/pallas_call | solution.py:159
  48.0 4.5 %collective-permute-done.19.refs_1_ = bf16[4,128,128]{2,1,0:T(8,128)(2,1)S(1)} collective-permute-done((bf16[4,128,128]{2,1,0:T(8,128)(2,1)S(1)}, bf16[4,128,128]{2,1,0:T(8,128)(2,1)S(1)}, u32[]{:S(2)}, u32[]{:S(2)}) %collective-permute-start.19) | collective-permute-done | bytes 131104 | tf_op jit(solution)/shard_map/ppermute | solution.py:364
  54.5 1.2 %collective-permute-done.20.refs_0_ = bf16[120,1152]{1,0:T(8,128)(2,1)S(1)} collective-permute-done((bf16[120,1152]{1,0:T(8,128)(2,1)S(1)}, bf16[120,1152]{1,0:T(8,128)(2,1)S(1)}, u32[]{:S(2)}, u32[]{:S(2)}) %collective-permute-start.20) | collective-permute-done | bytes 276512 | tf_op jit(solution)/shard_map/ppermute | solution.py:364
  56.3 1.7 %collective-permute-start.23 = (bf16[80,512]{1,0:T(8,128)(2,1)S(1)}, bf16[80,512]{1,0:T(8,128)(2,1)S(1)}, u32[]{:S(2)}, u32[]{:S(2)}) collective-permute-start(bf16[80,512]{1,0:T(8,128)(2,1)S(1)} %get-tuple-element.61), channel_id=1, source_target_pairs={{0,8},{4,12},{8,0},{12,4},{1,9},{5,13},{9,1},{13,5},{2,10},{6,14},... | collective-permute-start | bytes 245768 | tf_op jit(solution)/shard_map/ppermute | solution.py:364
  58.0 2.5 %collective-permute-start.22 = (bf16[80,512]{1,0:T(8,128)(2,1)S(1)}, bf16[80,512]{1,0:T(8,128)(2,1)S(1)}, u32[]{:S(2)}, u32[]{:S(2)}) collective-permute-start(bf16[80,512]{1,0:T(8,128)(2,1)S(1)} %get-tuple-element.60.refs_1_), channel_id=1, source_target_pairs={{0,4},{4,0},{8,12},{12,8},{1,5},{5,1},{9,13},{13,9},{2,6},{6,2},{1... | collective-permute-start | bytes 245768 | tf_op jit(solution)/shard_map/ppermute | solution.py:364
  61.4 2.8 %collective-permute-done.23.refs_1_.refs_3_ = bf16[80,512]{1,0:T(8,128)(2,1)S(1)} collective-permute-done((bf16[80,512]{1,0:T(8,128)(2,1)S(1)}, bf16[80,512]{1,0:T(8,128)(2,1)S(1)}, u32[]{:S(2)}, u32[]{:S(2)}) %collective-permute-start.23) | collective-permute-done | bytes 81952 | tf_op jit(solution)/shard_map/ppermute | solution.py:364
  64.9 1.8 %collective-permute-done.24.refs_4_ = bf16[80,512]{1,0:T(8,128)(2,1)S(1)} collective-permute-done((bf16[80,512]{1,0:T(8,128)(2,1)S(1)}, bf16[80,512]{1,0:T(8,128)(2,1)S(1)}, u32[]{:S(2)}, u32[]{:S(2)}) %collective-permute-start.24) | collective-permute-done | bytes 81952 | tf_op jit(solution)/shard_map/ppermute | solution.py:364
  69.5 1.2 %collective-permute-done.27.refs_3_ = f32[8,128]{1,0:T(8,128)S(1)} collective-permute-done((f32[8,128]{1,0:T(8,128)S(1)}, f32[8,128]{1,0:T(8,128)S(1)}, u32[]{:S(2)}, u32[]{:S(2)}) %collective-permute-start.27) | collective-permute-done | bytes 4128 | tf_op jit(solution)/shard_map/ppermute | solution.py:364
  (86 shorter events, 16.6 us)
Async XLA Ops:
  1.8 13.8 %collective-permute-start = (bf16[80,512]{1,0:T(8,128)(2,1)S(1)}, bf16[80,512]{1,0:T(8,128)(2,1)S(1)}, u32[]{:S(2)}, u32[]{:S(2)}) collective-permute-start(bf16[80,512]{1,0:T(8,128)(2,1)S(1)} %get-tuple-element.35), channel_id=1, source_target_pairs={{0,4},{4,0},{8,12},{12,8},{1,5},{5,1},{9,13},{13,9},{2,6},{6,2},{1... | collective-permute-start | bytes 245768 | tf_op jit(solution)/shard_map/ppermute | solution.py:364
  4.9 10.7 %collective-permute-start.1 = (bf16[80,512]{1,0:T(8,128)(2,1)S(1)}, bf16[80,512]{1,0:T(8,128)(2,1)S(1)}, u32[]{:S(2)}, u32[]{:S(2)}) collective-permute-start(bf16[80,512]{1,0:T(8,128)(2,1)S(1)} %get-tuple-element.36), channel_id=1, source_target_pairs={{0,8},{4,12},{8,0},{12,4},{1,9},{5,13},{9,1},{13,5},{2,10},{6,14},... | collective-permute-start | bytes 245768 | tf_op jit(solution)/shard_map/ppermute | solution.py:364
  7.5 8.1 %collective-permute-start.2 = (bf16[80,512]{1,0:T(8,128)(2,1)S(1)}, bf16[80,512]{1,0:T(8,128)(2,1)S(1)}, u32[]{:S(2)}, u32[]{:S(2)}) collective-permute-start(bf16[80,512]{1,0:T(8,128)(2,1)S(1)} %get-tuple-element.37), channel_id=1, source_target_pairs={{0,12},{4,8},{8,4},{12,0},{1,13},{5,9},{9,5},{13,1},{2,14},{6,10},... | collective-permute-start | bytes 245768 | tf_op jit(solution)/shard_map/ppermute | solution.py:364
  15.6 5.6 %collective-permute-start.4 = (bf16[160,512]{1,0:T(8,128)(2,1)S(1)}, bf16[160,512]{1,0:T(8,128)(2,1)S(1)}, u32[]{:S(2)}, u32[]{:S(2)}) collective-permute-start(bf16[160,512]{1,0:T(8,128)(2,1)S(1)} %get-tuple-element.40), channel_id=1, source_target_pairs={{0,2},{1,3},{2,0},{3,1},{4,6},{5,7},{6,4},{7,5},{8,10},{9,11},{10,... | collective-permute-start | bytes 491528 | tf_op jit(solution)/shard_map/ppermute | solution.py:364
  17.4 6.8 %collective-permute-start.3 = (bf16[160,512]{1,0:T(8,128)(2,1)S(1)}, bf16[160,512]{1,0:T(8,128)(2,1)S(1)}, u32[]{:S(2)}, u32[]{:S(2)}) collective-permute-start(bf16[160,512]{1,0:T(8,128)(2,1)S(1)} %get-tuple-element.39.refs_2_.refs_0_), channel_id=1, source_target_pairs={{0,1},{1,0},{2,3},{3,2},{4,5},{5,4},{6,7},{7,6},{8,9},{9,8},{10,11... | collective-permute-start | bytes 491528 | tf_op jit(solution)/shard_map/ppermute | solution.py:364
  21.2 3.0 %collective-permute-start.5 = (bf16[160,512]{1,0:T(8,128)(2,1)S(1)}, bf16[160,512]{1,0:T(8,128)(2,1)S(1)}, u32[]{:S(2)}, u32[]{:S(2)}) collective-permute-start(bf16[160,512]{1,0:T(8,128)(2,1)S(1)} %hold.8.refs_2_), channel_id=1, source_target_pairs={{0,1},{1,0},{2,3},{3,2},{4,5},{5,4},{6,7},{7,6},{8,9},{9,8},{10,11... | collective-permute-start | bytes 491528 | tf_op jit(solution)/shard_map/ppermute | solution.py:364
  25.1 7.4 %collective-permute-start.13 = (bf16[120,512]{1,0:T(8,128)(2,1)S(1)}, bf16[120,512]{1,0:T(8,128)(2,1)S(1)}, u32[]{:S(2)}, u32[]{:S(2)}) collective-permute-start(bf16[120,512]{1,0:T(8,128)(2,1)S(1)} %get-tuple-element.54), channel_id=1, source_target_pairs={{0,2},{1,3},{2,0},{3,1},{4,6},{5,7},{6,4},{7,5},{8,10},{9,11},{10,... | collective-permute-start | bytes 368648 | tf_op jit(solution)/shard_map/ppermute | solution.py:364
  27.7 7.5 %collective-permute-start.12 = (bf16[120,896]{1,0:T(8,128)(2,1)S(1)}, bf16[120,896]{1,0:T(8,128)(2,1)S(1)}, u32[]{:S(2)}, u32[]{:S(2)}) collective-permute-start(bf16[120,896]{1,0:T(8,128)(2,1)S(1)} %get-tuple-element.53), channel_id=1, source_target_pairs={{0,2},{1,3},{2,0},{3,1},{4,6},{5,7},{6,4},{7,5},{8,10},{9,11},{10,... | collective-permute-start | bytes 645128 | tf_op jit(solution)/shard_map/ppermute | solution.py:364
  32.7 8.4 %collective-permute-start.10 = (bf16[120,1024]{1,0:T(8,128)(2,1)S(1)}, bf16[120,1024]{1,0:T(8,128)(2,1)S(1)}, u32[]{:S(2)}, u32[]{:S(2)}) collective-permute-start(bf16[120,1024]{1,0:T(8,128)(2,1)S(1)} %get-tuple-element.52), channel_id=1, source_target_pairs={{0,2},{1,3},{2,0},{3,1},{4,6},{5,7},{6,4},{7,5},{8,10},{9,11},{10,... | collective-permute-start | bytes 737288 | tf_op jit(solution)/shard_map/ppermute | solution.py:364
  33.7 5.6 %collective-permute-start.11 = (bf16[4,128,128]{2,1,0:T(8,128)(2,1)S(1)}, bf16[4,128,128]{2,1,0:T(8,128)(2,1)S(1)}, u32[]{:S(2)}, u32[]{:S(2)}) collective-permute-start(bf16[4,128,128]{2,1,0:T(8,128)(2,1)S(1)} %hold.9.refs_0_), channel_id=1, source_target_pairs={{0,4},{4,0},{8,12},{12,8},{1,5},{5,1},{9,13},{13,9},{2,6},{6,2},{1... | collective-permute-start | bytes 393224 | tf_op jit(solution)/shard_map/ppermute | solution.py:364
  35.2 5.8 %collective-permute-start.15 = (bf16[120,896]{1,0:T(8,128)(2,1)S(1)}, bf16[120,896]{1,0:T(8,128)(2,1)S(1)}, u32[]{:S(2)}, u32[]{:S(2)}) collective-permute-start(bf16[120,896]{1,0:T(8,128)(2,1)S(1)} %hold.11.refs_0_), channel_id=1, source_target_pairs={{0,1},{1,0},{2,3},{3,2},{4,5},{5,4},{6,7},{7,6},{8,9},{9,8},{10,11... | collective-permute-start | bytes 645128 | tf_op jit(solution)/shard_map/ppermute | solution.py:364
  35.2 7.5 %collective-permute-start.6 = (bf16[160,512]{1,0:T(8,128)(2,1)S(1)}, bf16[160,512]{1,0:T(8,128)(2,1)S(1)}, u32[]{:S(2)}, u32[]{:S(2)}) collective-permute-start(bf16[160,512]{1,0:T(8,128)(2,1)S(1)} %get-tuple-element.44.refs_6_.refs_0_), channel_id=1, source_target_pairs={{0,1},{1,0},{2,3},{3,2},{4,5},{5,4},{6,7},{7,6},{8,9},{9,8},{10,11... | collective-permute-start | bytes 491528 | tf_op jit(solution)/shard_map/ppermute | solution.py:364
  35.7 7.3 %collective-permute-start.7 = (bf16[160,896]{1,0:T(8,128)(2,1)S(1)}, bf16[160,896]{1,0:T(8,128)(2,1)S(1)}, u32[]{:S(2)}, u32[]{:S(2)}) collective-permute-start(bf16[160,896]{1,0:T(8,128)(2,1)S(1)} %get-tuple-element.47.refs_6_.refs_1_.refs_2_), channel_id=1, source_target_pairs={{0,1},{1,0},{2,3},{3,2},{4,5},{5,4},{6,7},{7,6},{8,9},{9,8},{10,11... | collective-permute-start | bytes 860168 | tf_op jit(solution)/shard_map/ppermute | solution.py:364
  39.3 7.2 %collective-permute-start.9 = (bf16[160,1152]{1,0:T(8,128)(2,1)S(1)}, bf16[160,1152]{1,0:T(8,128)(2,1)S(1)}, u32[]{:S(2)}, u32[]{:S(2)}) collective-permute-start(bf16[160,1152]{1,0:T(8,128)(2,1)S(1)} %get-tuple-element.51.refs_3_.refs_6_), channel_id=1, source_target_pairs={{0,1},{1,0},{2,3},{3,2},{4,5},{5,4},{6,7},{7,6},{8,9},{9,8},{10,11... | collective-permute-start | bytes 1105928 | tf_op jit(solution)/shard_map/ppermute | solution.py:364
  41.1 5.4 %collective-permute-start.8 = (bf16[160,1024]{1,0:T(8,128)(2,1)S(1)}, bf16[160,1024]{1,0:T(8,128)(2,1)S(1)}, u32[]{:S(2)}, u32[]{:S(2)}) collective-permute-start(bf16[160,1024]{1,0:T(8,128)(2,1)S(1)} %get-tuple-element.49.refs_6_.refs_2_.refs_4_), channel_id=1, source_target_pairs={{0,1},{1,0},{2,3},{3,2},{4,5},{5,4},{6,7},{7,6},{8,9},{9,8},{10,11... | collective-permute-start | bytes 983048 | tf_op jit(solution)/shard_map/ppermute | solution.py:364
  41.1 12.1 %collective-permute-start.18 = (bf16[120,1152]{1,0:T(8,128)(2,1)S(1)}, bf16[120,1152]{1,0:T(8,128)(2,1)S(1)}, u32[]{:S(2)}, u32[]{:S(2)}) collective-permute-start(bf16[120,1152]{1,0:T(8,128)(2,1)S(1)} %get-tuple-element.56), channel_id=1, source_target_pairs={{0,2},{1,3},{2,0},{3,1},{4,6},{5,7},{6,4},{7,5},{8,10},{9,11},{10,... | collective-permute-start | bytes 829448 | tf_op jit(solution)/shard_map/ppermute | solution.py:364
  43.0 9.4 %collective-permute-start.19 = (bf16[4,128,128]{2,1,0:T(8,128)(2,1)S(1)}, bf16[4,128,128]{2,1,0:T(8,128)(2,1)S(1)}, u32[]{:S(2)}, u32[]{:S(2)}) collective-permute-start(bf16[4,128,128]{2,1,0:T(8,128)(2,1)S(1)} %pair_sum.1.refs_1_.refs_0_), channel_id=1, source_target_pairs={{0,8},{4,12},{8,0},{12,4},{1,9},{5,13},{9,1},{13,5},{2,10},{6,14},... | collective-permute-start | bytes 393224 | tf_op jit(solution)/shard_map/ppermute | solution.py:364
  44.7 11.5 %collective-permute-start.17 = (bf16[40,3584]{1,0:T(8,128)(2,1)S(1)}, bf16[40,3584]{1,0:T(8,128)(2,1)S(1)}, u32[]{:S(2)}, u32[]{:S(2)}) collective-permute-start(bf16[40,3584]{1,0:T(8,128)(2,1)S(1)} %merge.1.refs_1_), channel_id=1, source_target_pairs={{0,2},{1,3},{2,0},{3,1},{4,6},{5,7},{6,4},{7,5},{8,10},{9,11},{10,... | collective-permute-start | bytes 860168 | tf_op jit(solution)/shard_map/ppermute | solution.py:364
  56.2 7.9 %collective-permute-start.21 = (bf16[40,3584]{1,0:T(8,128)(2,1)S(1)}, bf16[40,3584]{1,0:T(8,128)(2,1)S(1)}, u32[]{:S(2)}, u32[]{:S(2)}) collective-permute-start(bf16[40,3584]{1,0:T(8,128)(2,1)S(1)} %hold.14.refs_0_), channel_id=1, source_target_pairs={{0,1},{1,0},{2,3},{3,2},{4,5},{5,4},{6,7},{7,6},{8,9},{9,8},{10,11... | collective-permute-start | bytes 860168 | tf_op jit(solution)/shard_map/ppermute | solution.py:364
  56.3 7.9 %collective-permute-start.23 = (bf16[80,512]{1,0:T(8,128)(2,1)S(1)}, bf16[80,512]{1,0:T(8,128)(2,1)S(1)}, u32[]{:S(2)}, u32[]{:S(2)}) collective-permute-start(bf16[80,512]{1,0:T(8,128)(2,1)S(1)} %get-tuple-element.61), channel_id=1, source_target_pairs={{0,8},{4,12},{8,0},{12,4},{1,9},{5,13},{9,1},{13,5},{2,10},{6,14},... | collective-permute-start | bytes 245768 | tf_op jit(solution)/shard_map/ppermute | solution.py:364
  58.0 6.2 %collective-permute-start.22 = (bf16[80,512]{1,0:T(8,128)(2,1)S(1)}, bf16[80,512]{1,0:T(8,128)(2,1)S(1)}, u32[]{:S(2)}, u32[]{:S(2)}) collective-permute-start(bf16[80,512]{1,0:T(8,128)(2,1)S(1)} %get-tuple-element.60.refs_1_), channel_id=1, source_target_pairs={{0,4},{4,0},{8,12},{12,8},{1,5},{5,1},{9,13},{13,9},{2,6},{6,2},{1... | collective-permute-start | bytes 245768 | tf_op jit(solution)/shard_map/ppermute | solution.py:364
  60.4 6.3 %collective-permute-start.24 = (bf16[80,512]{1,0:T(8,128)(2,1)S(1)}, bf16[80,512]{1,0:T(8,128)(2,1)S(1)}, u32[]{:S(2)}, u32[]{:S(2)}) collective-permute-start(bf16[80,512]{1,0:T(8,128)(2,1)S(1)} %get-tuple-element.62), channel_id=1, source_target_pairs={{0,12},{4,8},{8,4},{12,0},{1,13},{5,9},{9,5},{13,1},{2,14},{6,10},... | collective-permute-start | bytes 245768 | tf_op jit(solution)/shard_map/ppermute | solution.py:364
  67.7 3.0 %collective-permute-start.27 = (f32[8,128]{1,0:T(8,128)S(1)}, f32[8,128]{1,0:T(8,128)S(1)}, u32[]{:S(2)}, u32[]{:S(2)}) collective-permute-start(f32[8,128]{1,0:T(8,128)S(1)} %get-tuple-element.64.refs_0_), channel_id=1, source_target_pairs={{0,3},{1,2},{2,1},{3,0},{4,7},{5,6},{6,5},{7,4},{8,11},{9,10},{10,... | collective-permute-start | bytes 12296 | tf_op jit(solution)/shard_map/ppermute | solution.py:364
  67.7 3.6 %collective-permute-start.26 = (f32[8,128]{1,0:T(8,128)S(1)}, f32[8,128]{1,0:T(8,128)S(1)}, u32[]{:S(2)}, u32[]{:S(2)}) collective-permute-start(f32[8,128]{1,0:T(8,128)S(1)} %get-tuple-element.64.refs_0_), channel_id=1, source_target_pairs={{0,2},{1,3},{2,0},{3,1},{4,6},{5,7},{6,4},{7,5},{8,10},{9,11},{10,... | collective-permute-start | bytes 12296 | tf_op jit(solution)/shard_map/ppermute | solution.py:364
  (13 other events, 52.3 us)

commit v3 on v2

--- a/solution.py
+++ b/solution.py
@@ -134,18 +134,19 @@
 LISTS = 8
 ROWS = OWNERS * MOST
 REMOTE = ROWS - MOST
-CHUNKS = (512, 896, 1024, 1152)
-STARTS = (0, 512, 1408, 2432)
+CHUNKS = (1408, 1024, 1152)
+STARTS = (0, 1408, 2432)
 HALF = FF // 2
 BLOCK = 256
-PIECES = 4
-LOADS = (((0, 0), (0, 1), (1, 0), (1, 1), (2, 0)), ((2, 1), (3, 0)), ((3, 1),))
+FLUSH = ((), (1,), (0, 2))
+OWN_NEAR = ((0, 0, 0), (HALF // 2, 0, 0))
+OWN_FAR = ((0, 0, 1), (HALF // 2, 0, 1))
 ANY = pl.BlockSpec(memory_space=pl.ANY)
 HBM = pl.BlockSpec(memory_space=pltpu.HBM)
 VMEM = pl.BlockSpec(memory_space=pltpu.VMEM)
 
 
-def call(kernel, name, operands, outs, *, after=(), far=(), scratch=(), aliases=None, cost=0):
+def call(kernel, name, operands, outs, *, after=(), far=(), scratch=(), aliases=None, cost=0, limit=3):
     count, late = len(operands), len(after)
     operands = [
         pltpu.with_memory_space_constraint(x, pltpu.HBM) if i in far else x
@@ -164,7 +165,7 @@
         scratch_shapes=scratch,
         name=name,
         input_output_aliases=aliases or {},
-        compiler_params=pltpu.CompilerParams(vmem_limit_bytes=8 * 2**20),
+        compiler_params=pltpu.CompilerParams(vmem_limit_bytes=limit * 2**20),
         cost_estimate=pl.CostEstimate(flops=0, bytes_accessed=int(cost * 3e6), transcendentals=0),
     )(*operands, *after)
 
@@ -234,37 +235,15 @@
     other_ref[...] = jnp.concatenate([d[MOST:] for d in order], axis=0).astype(jnp.bfloat16)
 
 
-def weight_copies(sources, outs, sems, load):
-    copies = []
-    for (chunk, which), out in zip(load, outs):
-        part = out.shape[0] // PIECES
-        for i in range(PIECES):
-            rows = pl.ds(i * part, part)
-            source = sources[which].at[rows, pl.ds(STARTS[chunk], CHUNKS[chunk])]
-            copies.append(pltpu.make_async_copy(source, out.at[rows, :], sems.at[len(copies)]))
-    return copies
-
-
-def load_kernel(load, place, gate_ref, up_ref, *refs):
-    copies = weight_copies((gate_ref, up_ref), refs[:-1], refs[-1], load)
+def masked_kernel(place, context_hbm, grad_hbm, kept_hbm, gate_hbm, up_hbm, out_ref, *scratch):
+    context, grad, kept_ref, sems = scratch
+    pairs = ((context_hbm, context), (grad_hbm, grad), (kept_hbm, kept_ref))
+    copies = [pltpu.make_async_copy(*pair, sems.at[i]) for i, pair in enumerate(pairs)]
     for copy in copies:
-        copy.start()
-    for copy in copies:
-        copy.wait()
-
-
-def masked_kernel(place, context_ref, grad_ref, kept_ref, gate_ref, up_ref, *refs):
-    out_ref, weights, (context, grad, sems, few) = refs[0], refs[1:-4], refs[-4:]
-    first = [
-        pltpu.make_async_copy(context_ref, context, few.at[0]),
-        pltpu.make_async_copy(grad_ref, grad, few.at[1]),
-    ]
-    copies = weight_copies((gate_ref, up_ref), weights, sems, LOADS[0])
-    for copy in first + copies:
         copy.start()
     features, keep = context.shape[1], kept_ref.shape[1]
     index = lax.broadcasted_iota(jnp.int32, (features, keep), 0)
-    for copy in first:
+    for copy in copies:
         copy.wait()
     for c in range(kept_ref.shape[0]):
         pick = jnp.where(index == kept_ref[c : c + 1, :], 1.0, 0.0).astype(jnp.bfloat16)
@@ -275,9 +254,7 @@
             (((0,), (0,)), ((), ())),
             preferred_element_type=jnp.float32,
         )
-        out_ref[c] = part.astype(jnp.bfloat16)
-    for copy in copies:
-        copy.wait()
+        out_ref[c] = part
 
 
 def pass_kernel(place, in_ref, out_ref):
@@ -289,24 +266,35 @@
     out_ref[...] = total.astype(out_ref.dtype)
 
 
-def hidden_kernel(place, a0, a1, a2, a3, gate_ref, up_ref, out_ref, remote_ref, rows):
+def masked_sum_kernel(place, left, right, out_ref, token_ref):
+    sum_kernel(place, left, right, out_ref)
+    token_ref[...] = jnp.zeros_like(token_ref)
+
+
+def hidden_kernel(first, place, a0, a1, a2, a3, gate_ref, up_ref, out_ref, remote_ref, rows):
     for j, piece in enumerate((a0, a1, a2, a3)):
         width = piece.shape[1]
         start = pl.multiple_of((place[1] ^ j) * width, width)
         rows[:, pl.ds(start, width)] = piece[...]
     for start in range(0, out_ref.shape[1], BLOCK):
         columns = slice(start, min(start + BLOCK, out_ref.shape[1]))
-        gate = product(rows[...], gate_ref[:, columns])
-        up = product(rows[...], up_ref[:, columns])
+        units = slice(first + columns.start, first + columns.stop)
+        gate = product(rows[...], gate_ref[:, units])
+        up = product(rows[...], up_ref[:, units])
         hidden = gate / (1.0 + jnp.exp(-gate)) * up
         out_ref[:, columns] = hidden.astype(jnp.bfloat16)
         remote_ref[:, columns] = hidden[:REMOTE].astype(jnp.bfloat16)
 
 
 def merge_kernel(place, *refs):
-    for start, width, part in zip(STARTS, CHUNKS, refs):
+    parts, (first_ref, second_ref, own_ref) = refs[: len(CHUNKS)], refs[len(CHUNKS) :]
+    for start, width, part in zip(STARTS, CHUNKS, parts):
         own = part[...].astype(jnp.float32)[REMOTE:]
-        refs[-1][:, start : start + width] = own.astype(jnp.bfloat16)
+        own_ref[:, start : start + width] = own.astype(jnp.bfloat16)
+        for half_ref, begin in ((first_ref, 0), (second_ref, HALF // 2)):
+            low, high = max(start, begin), min(start + width, begin + HALF // 2)
+            if low < high:
+                half_ref[:, low - begin : high - begin] = part[:, low - start : high - start]
 
 
 def down_part(place, part, down_ref, start, flip, core):
@@ -315,30 +303,20 @@
     return product(part[...], down_ref[rows, :])
 
 
-def down_own_kernel(place, *refs):
-    parts, down_ref, outs = refs[: 2 * len(CHUNKS)], refs[2 * len(CHUNKS)], refs[2 * len(CHUNKS) + 1 :]
-    total = None
-    for i, part in enumerate(parts):
-        term = down_part(place, part, down_ref, STARTS[i // 2], 0, i % 2)
-        total = term if total is None else total + term
-    for s in range(OWNERS):
-        outs[s][...] = total[MOST * s : MOST * (s + 1)].astype(jnp.bfloat16)
-
-
 def down_add_kernel(pieces, has_total, place, *refs):
     parts, down_ref, refs = refs[: len(pieces)], refs[len(pieces)], refs[len(pieces) + 1 :]
     total = refs[0][...] if has_total else None
-    for (start, core), part in zip(pieces, parts):
-        term = down_part(place, part, down_ref, start, 1, core)
+    for (start, flip, core), part in zip(pieces, parts):
+        term = down_part(place, part, down_ref, start, flip, core)
         total = term if total is None else total + term
     refs[-1][...] = total
 
 
-def back_kernel(place, total_ref, o1, o2, o3, *outs):
-    total = total_ref[...]
-    for s, own in enumerate((o1, o2, o3)):
-        both = [own[...].astype(jnp.float32), total[MOST * s : MOST * (s + 1)]]
+def back_kernel(place, total_ref, mine_ref, *outs):
+    for s in range(OWNERS - 1):
+        both = [ref[MOST * s : MOST * (s + 1), :] for ref in (mine_ref, total_ref)]
         outs[s][...] = jnp.concatenate(both, axis=0).astype(jnp.bfloat16)
+    outs[-1][...] = mine_ref[REMOTE:, :].astype(jnp.bfloat16)
 
 
 def combine_kernel(place, own, other, b1, b2, b3, route_ref, grad_ref, layer_ref, router_ref):
@@ -390,33 +368,21 @@
         scratch=[pltpu.VMEM(ids.shape, ids.dtype), pltpu.VMEM(tokens.shape, tokens.dtype), dma((2,))],
     )
     arrived = [packed[0]] + [swap(packed[s], "rank", s) for s in (1, 2, 3)]
-    weights = [[None, None] for _ in CHUNKS]
-
-    def load(which, kernel, name, operands, outs, scratch, after):
-        pieces = LOADS[which]
-        shapes = [shape(depth, CHUNKS[chunk]) for chunk, _ in pieces]
-        made = call(
-            kernel,
-            name,
-            (*operands, gate_weight, up_weight),
-            outs + shapes,
-            after=after,
-            far=tuple(i for i in range(len(operands) + 2) if i != 2 or not operands),
-            scratch=scratch,
-        )
-        for (chunk, part), array in zip(pieces, made[len(outs) :]):
-            weights[chunk][part] = array
-        return made
-
-    scratch = [
-        pltpu.VMEM(context.shape, context.dtype),
-        pltpu.VMEM(out_grad.shape, out_grad.dtype),
-        dma((PIECES * len(LOADS[0]),)),
-        dma((2,)),
-    ]
-    partial_shape = [shape(kept_rows.shape[0], kept_rows.shape[1], 128)]
-    partial = load(
-        0, masked_kernel, "masked", (context, out_grad, kept_rows), partial_shape, scratch, (packed[0],)
+    blocks = (kept_rows.shape[0], kept_rows.shape[1], 128)
+    partial = call(
+        masked_kernel,
+        "masked",
+        (context, out_grad, kept_rows, gate_weight, up_weight),
+        [shape(*blocks, dtype=f32)],
+        after=(packed[0],),
+        far=(0, 1, 2, 3, 4),
+        limit=4,
+        scratch=[
+            pltpu.VMEM(context.shape, context.dtype),
+            pltpu.VMEM(out_grad.shape, out_grad.dtype),
+            pltpu.VMEM(kept_rows.shape, kept_rows.dtype),
+            dma((3,)),
+        ],
     )[0]
     route = call(
         route_kernel, "route", (ids, probs), [shape(3, token_count, 384)], after=(partial,)
@@ -427,25 +393,20 @@
     own_far = swap(own, "tensor", 1)
     crossed = swap(other, "tensor", 2)
 
-    def load_more(which, after):
-        scratch = [dma((PIECES * len(LOADS[which]),))]
-        kernel = functools.partial(load_kernel, LOADS[which])
-        return load(which, kernel, "load", (), [], scratch, (after,))[0]
-
-    def hold(value, after, cost=0):
-        return call(pass_kernel, "hold", (value,), [value], after=(after,), aliases={0: 0}, cost=cost)[0]
-
-    crossed = hold(crossed, load_more(1, own))
+    def hold(value, *after):
+        return call(pass_kernel, "hold", (value,), [value], after=after, aliases={0: 0})[0]
+
+    held = hold(partial, own)
+    crossed = hold(crossed, own)
     crossed_far = swap(crossed, "tensor", 1)
-    last = load_more(2, crossed)
     pieces = (own, own_far, crossed, crossed_far)
 
-    hidden, remote = [], []
+    hidden, remote, last = [], [], route
     for k, width in enumerate(CHUNKS):
         made = call(
-            hidden_kernel,
+            functools.partial(hidden_kernel, STARTS[k]),
             "hidden",
-            (*pieces, *weights[k]),
+            (*pieces, gate_weight, up_weight),
             [shape(ROWS, width), shape(REMOTE, width)],
             after=(last,),
             scratch=[pltpu.VMEM((ROWS, depth), jnp.bfloat16)],
@@ -454,12 +415,21 @@
         hidden.append(made[0])
         remote.append(made[1])
         last = made[0]
+        if k == 0:
+            last = pair = call(
+                sum_kernel, "pair_sum", (held, swap(held, "rank", 1)), [shape(*blocks)], after=(last,)
+            )[0]
     across = [swap(part, "tensor", 2) for part in remote]
-    own_rows = call(merge_kernel, "merge", tuple(hidden), [shape(MOST, HALF)])[0]
+    *full, own_rows = call(
+        merge_kernel,
+        "merge",
+        tuple(hidden),
+        [shape(ROWS, HALF // 2)] * 2 + [shape(MOST, HALF)],
+    )
+    full_far = [swap(part, "tensor", 1) for part in full]
     own_across = swap(own_rows, "tensor", 2)
-    hidden_far = [swap(part, "tensor", 1) for part in hidden]
-
-    def add(pieces, parts, total, after):
+
+    def add(pieces, parts, total, after=()):
         rows = parts[0].shape[0]
         operands = (*parts, down_weight) + (() if total is None else (total,))
         return call(
@@ -471,49 +441,48 @@
         )[0]
 
     total, step = None, own_rows
-    held = hold(partial, own_rows)
+    fars = []
     for k, start in enumerate(STARTS):
-        if k == 2:
-            pair = call(
-                sum_kernel, "pair_sum", (held, swap(held, "rank", 1)), [partial], after=(total,)
-            )[0]
-            step = pair
-        if k == 3:
-            operands = [part for near_far in zip(hidden, hidden_far) for part in near_far]
-            finished = call(
-                down_own_kernel,
-                "down_own",
-                (*operands, down_weight),
-                [shape(MOST, columns)] * OWNERS,
+        if k == 1:
+            masked_grad, step = call(
+                masked_sum_kernel,
+                "masked_sum",
+                (pair, swap(pair, "rank", 2)),
+                [shape(*blocks, dtype=f32), shape(8, 128, dtype=f32)],
                 after=(total,),
             )
-            returned, own_result = finished[:3], finished[3]
-            masked_grad = call(
-                sum_kernel,
-                "masked_sum",
-                (pair, swap(pair, "rank", 2)),
-                [shape(*partial.shape, dtype=f32)],
-                after=(own_result,),
+        if k == 2:
+            mine = call(
+                functools.partial(down_add_kernel, OWN_NEAR, False),
+                "down_add",
+                (*full, down_weight),
+                [shape(ROWS, columns, dtype=f32)],
+                after=(total,),
             )[0]
-            step = masked_grad
-        near = hold(across[k], step, 3)
+            step = mine
+        near = hold(across[k], step)
         far = swap(near, "tensor", 1)
-        total = add(((start, 0),), (near,), total, ())
-        total = add(((start, 1),), (far,), total, ())
+        total = add(((start, 1, 0),), (near,), total)
+        fars.append(((start, 1, 1), far))
+        for j in FLUSH[k]:
+            total = add((fars[j][0],), (fars[j][1],), total)
         step = total
-    backs = call(
-        back_kernel, "back", (total, *returned), [shape(2 * MOST, columns)] * 3
+    mine = add(OWN_FAR, full_far, mine, (total,))
+    *backs, own = call(
+        back_kernel,
+        "back",
+        (total, mine),
+        [shape(2 * MOST, columns)] * 3 + [shape(MOST, columns)],
     )
     lists = [swap(backs[s - 1], "rank", s) for s in (1, 2, 3)]
-    near = hold(own_across, backs[0], 3)
+    near = hold(own_across, *lists)
     far = swap(near, "tensor", 1)
-    mine = add(((0, 0),), (near,), None, ())
-    lists[0] = hold(lists[0], lists[1], 4)
-    mine = add(((0, 1),), (far,), mine, (lists[0],))
+    last = add(((0, 1, 0),), (near,), None)
+    last = add(((0, 1, 1),), (far,), last)
     layer_output, router = call(
         combine_kernel,
         "combine",
-        (own_result, mine, *lists, route, out_grad),
+        (own, last, *lists, route, out_grad),
         [shape(token_count, columns), shape(8, token_count, dtype=f32)],
     )
     routers = [router] + [swap(router, "tensor", t) for t in (1, 2, 3)]

time: 72.1 us -> 66.8 us (0.926)
  Pallas kernels: 28.6 us -> 17.4 us
  waiting for transfers between devices: 17.9 us -> 25.2 us
  local copies, waits for them, and re-layouts: 1.66 us -> 0.04 us
    pallas_call x35 -> x29, Pallas kernels: 28.6 us -> 17.4 us  [call(): pl.pallas_call(body, out_shape=outs, in_specs=[HBM if i in far else VMEM...]
    ppermute x28 -> x24, waiting for transfers between devices: 17.9 us -> 25.2 us  [swap(): return lax.ppermute(value, axis, [(i, i ^ by) for i in range(4)])]
    unnamed x18, local copies, waits for them, and re-layouts: 1.66 us -> 0.04 us
    ppermute x28 -> x24, starting transfers between devices: 22.8 us -> 23.1 us  [swap(): return lax.ppermute(value, axis, [(i, i ^ by) for i in range(4)])]
  transfers between devices with their start and end apart: 28 -> 24, of which waited for: 10 -> 11; matrix products, arithmetic and copies ran while one was open for 0% -> 0% of each run, Pallas kernels for 35% -> 21%
where the time goes in v3:
time: 66.8 us; the launch traced here: 66.7 us
  waiting for transfers between devices  25.2 us (38%)
  starting transfers between devices  23.1 us (35%)
  Pallas kernels  17.4 us (26%)
  between operations  0.92 us (1%)
    ppermute x24, waiting for transfers between devices, swap(): return lax.ppermute(value, axis, [(i, i ^ by) for i in range(4)])  25.2 us
    ppermute x24, starting transfers between devices, swap(): return lax.ppermute(value, axis, [(i, i ^ by) for i in range(4)])  23.1 us
    pallas_call x29, Pallas kernels, call(): pl.pallas_call(body, out_shape=outs, in_specs=[HBM if i in far else VMEM...  17.4 us
  transfers between devices with their start and end apart: 24, of which 11 were waited for; matrix products, arithmetic and copies ran while one was open for 0% of the time, Pallas kernels for 21%

profile of v3, /device:TPU:0, one launch (start us, length us, event | category | flops | bytes accessed | tf_op | source)
XLA Modules:
  0.0 66.7 jit_solution(5747251378351370280)
XLA Ops:
  0.6 1.2 %pack.1 = (bf16[80,512]{1,0:T(8,128)(2,1)S(1)}, bf16[80,512]{1,0:T(8,128)(2,1)S(1)}, bf16[80,512]{1,0:T(8,128)(2,1)S(1)}, bf16[80,512]{1,0:T(8,128)(2,1)S(1)}) custom-call(s32[2,128]{1,0:T(2,128)} %bitcast.5, bf16[128,512]{1,0:T(8,128)(2,1)} %refs_1_.10), custom_call_target="tpu_custom_call" | custom-call | tf_op jit(solution)/shard_map/pack/pallas_call | solution.py:160
  1.8 3.1 %collective-permute-start = (bf16[80,512]{1,0:T(8,128)(2,1)S(1)}, bf16[80,512]{1,0:T(8,128)(2,1)S(1)}, u32[]{:S(2)}, u32[]{:S(2)}) collective-permute-start(bf16[80,512]{1,0:T(8,128)(2,1)S(1)} %get-tuple-element.27), channel_id=1, source_target_pairs={{0,4},{4,0},{8,12},{12,8},{1,5},{5,1},{9,13},{13,9},{2,6},{6,2},{1... | collective-permute-start | bytes 245768 | tf_op jit(solution)/shard_map/ppermute | solution.py:342
  4.9 2.6 %collective-permute-start.1 = (bf16[80,512]{1,0:T(8,128)(2,1)S(1)}, bf16[80,512]{1,0:T(8,128)(2,1)S(1)}, u32[]{:S(2)}, u32[]{:S(2)}) collective-permute-start(bf16[80,512]{1,0:T(8,128)(2,1)S(1)} %get-tuple-element.28), channel_id=1, source_target_pairs={{0,8},{4,12},{8,0},{12,4},{1,9},{5,13},{9,1},{13,5},{2,10},{6,14},... | collective-permute-start | bytes 245768 | tf_op jit(solution)/shard_map/ppermute | solution.py:342
  7.5 2.6 %masked.1.refs_2_.refs_0_ = f32[4,128,128]{2,1,0:T(8,128)S(1)} custom-call(bf16[128,2048]{1,0:T(8,128)(2,1)} %refs_0_.1, bf16[128,512]{1,0:T(8,128)(2,1)} %refs_6_.1, s32[4,128]{1,0:T(4,128)} %refs_2_.3, bf16[2048,3584]{1,0:T(8,128)(2,1)} %refs_4_.7, bf16[2048,3584]{1,0:T(8,128)(2,1)} %refs_5_.5, bf16[80,512]{1,0:T(8,128)(2,1)S(1)} %get-tuple-element.26.refs_5_.refs_0_), custom_call_target="tpu_custom_call" | custom-call | tf_op jit(solution)/shard_map/masked/pallas_call | solution.py:160
  10.5 3.6 %collective-permute-done.1.refs_2_ = bf16[80,512]{1,0:T(8,128)(2,1)S(1)} collective-permute-done((bf16[80,512]{1,0:T(8,128)(2,1)S(1)}, bf16[80,512]{1,0:T(8,128)(2,1)S(1)}, u32[]{:S(2)}, u32[]{:S(2)}) %collective-permute-start.1) | collective-permute-done | bytes 81952 | tf_op jit(solution)/shard_map/ppermute | solution.py:342
  14.1 1.6 %collective-permute-start.4 = (bf16[160,512]{1,0:T(8,128)(2,1)S(1)}, bf16[160,512]{1,0:T(8,128)(2,1)S(1)}, u32[]{:S(2)}, u32[]{:S(2)}) collective-permute-start(bf16[160,512]{1,0:T(8,128)(2,1)S(1)} %get-tuple-element.31), channel_id=1, source_target_pairs={{0,2},{1,3},{2,0},{3,1},{4,6},{5,7},{6,4},{7,5},{8,10},{9,11},{10,... | collective-permute-start | bytes 491528 | tf_op jit(solution)/shard_map/ppermute | solution.py:342
  15.7 3.8 %collective-permute-done.4.refs_0_ = bf16[160,512]{1,0:T(8,128)(2,1)S(1)} collective-permute-done((bf16[160,512]{1,0:T(8,128)(2,1)S(1)}, bf16[160,512]{1,0:T(8,128)(2,1)S(1)}, u32[]{:S(2)}, u32[]{:S(2)}) %collective-permute-start.4) | collective-permute-done | bytes 163872 | tf_op jit(solution)/shard_map/ppermute | solution.py:342
  19.5 1.4 %collective-permute-start.6 = (f32[4,128,128]{2,1,0:T(8,128)S(1)}, f32[4,128,128]{2,1,0:T(8,128)S(1)}, u32[]{:S(2)}, u32[]{:S(2)}) collective-permute-start(f32[4,128,128]{2,1,0:T(8,128)S(1)} %hold.7.refs_0_), channel_id=1, source_target_pairs={{0,4},{4,0},{8,12},{12,8},{1,5},{5,1},{9,13},{13,9},{2,6},{6,2},{1... | collective-permute-start | bytes 786440 | tf_op jit(solution)/shard_map/ppermute | solution.py:342
  21.0 2.3 %hidden.3 = (bf16[160,1408]{1,0:T(8,128)(2,1)S(1)}, bf16[120,1408]{1,0:T(8,128)(2,1)S(1)}) custom-call(bf16[160,512]{1,0:T(8,128)(2,1)S(1)} %get-tuple-element.30.refs_1_.refs_0_, bf16[160,512]{1,0:T(8,128)(2,1)S(1)} %collective-permute-done.3.refs_1_, bf16[160,512]{1,0:T(8,128)(2,1)S(1)} %hold.6.refs_2_, ...), custom_call_target="tpu_custom_call" | custom-call | bytes 60000000 | tf_op jit(solution)/shard_map/hidden/pallas_call | solution.py:160
  23.2 1.6 %collective-permute-start.10 = (bf16[120,1408]{1,0:T(8,128)(2,1)S(1)}, bf16[120,1408]{1,0:T(8,128)(2,1)S(1)}, u32[]{:S(2)}, u32[]{:S(2)}) collective-permute-start(bf16[120,1408]{1,0:T(8,128)(2,1)S(1)} %get-tuple-element.39), channel_id=1, source_target_pairs={{0,2},{1,3},{2,0},{3,1},{4,6},{5,7},{6,4},{7,5},{8,10},{9,11},{10,... | collective-permute-start | bytes 1013768 | tf_op jit(solution)/shard_map/ppermute | solution.py:342
  24.8 3.5 %collective-permute-done.6.refs_1_ = f32[4,128,128]{2,1,0:T(8,128)S(1)} collective-permute-done((f32[4,128,128]{2,1,0:T(8,128)S(1)}, f32[4,128,128]{2,1,0:T(8,128)S(1)}, u32[]{:S(2)}, u32[]{:S(2)}) %collective-permute-start.6) | collective-permute-done | bytes 262176 | tf_op jit(solution)/shard_map/ppermute | solution.py:342
  28.3 1.6 %hidden.4 = (bf16[160,1024]{1,0:T(8,128)(2,1)S(1)}, bf16[120,1024]{1,0:T(8,128)(2,1)S(1)}) custom-call(bf16[160,512]{1,0:T(8,128)(2,1)S(1)} %get-tuple-element.30.refs_1_.refs_0_, bf16[160,512]{1,0:T(8,128)(2,1)S(1)} %collective-permute-done.3.refs_1_, bf16[160,512]{1,0:T(8,128)(2,1)S(1)} %hold.6.refs_2_, ...), custom_call_target="tpu_custom_call" | custom-call | tf_op jit(solution)/shard_map/hidden/pallas_call | solution.py:160
  29.9 1.6 %collective-permute-start.8 = (bf16[120,1024]{1,0:T(8,128)(2,1)S(1)}, bf16[120,1024]{1,0:T(8,128)(2,1)S(1)}, u32[]{:S(2)}, u32[]{:S(2)}) collective-permute-start(bf16[120,1024]{1,0:T(8,128)(2,1)S(1)} %get-tuple-element.38), channel_id=1, source_target_pairs={{0,2},{1,3},{2,0},{3,1},{4,6},{5,7},{6,4},{7,5},{8,10},{9,11},{10,... | collective-permute-start | bytes 737288 | tf_op jit(solution)/shard_map/ppermute | solution.py:342
  31.4 2.5 %collective-permute-start.9 = (bf16[4,128,128]{2,1,0:T(8,128)(2,1)S(1)}, bf16[4,128,128]{2,1,0:T(8,128)(2,1)S(1)}, u32[]{:S(2)}, u32[]{:S(2)}) collective-permute-start(bf16[4,128,128]{2,1,0:T(8,128)(2,1)S(1)} %pair_sum.1.refs_6_.refs_0_), channel_id=1, source_target_pairs={{0,8},{4,12},{8,0},{12,4},{1,9},{5,13},{9,1},{13,5},{2,10},{6,14},... | collective-permute-start | bytes 393224 | tf_op jit(solution)/shard_map/ppermute | solution.py:342
  33.9 1.9 %hidden.5 = (bf16[160,1152]{1,0:T(8,128)(2,1)S(1)}, bf16[120,1152]{1,0:T(8,128)(2,1)S(1)}) custom-call(bf16[160,512]{1,0:T(8,128)(2,1)S(1)} %get-tuple-element.30.refs_1_.refs_0_, bf16[160,512]{1,0:T(8,128)(2,1)S(1)} %collective-permute-done.3.refs_1_, bf16[160,512]{1,0:T(8,128)(2,1)S(1)} %hold.6.refs_2_, ...), custom_call_target="tpu_custom_call" | custom-call | tf_op jit(solution)/shard_map/hidden/pallas_call | solution.py:160
  37.5 2.5 %collective-permute-done.9.refs_1_ = bf16[4,128,128]{2,1,0:T(8,128)(2,1)S(1)} collective-permute-done((bf16[4,128,128]{2,1,0:T(8,128)(2,1)S(1)}, bf16[4,128,128]{2,1,0:T(8,128)(2,1)S(1)}, u32[]{:S(2)}, u32[]{:S(2)}) %collective-permute-start.9) | collective-permute-done | bytes 131104 | tf_op jit(solution)/shard_map/ppermute | solution.py:342
  43.3 1.8 %collective-permute-done.7.refs_0_ = bf16[120,1152]{1,0:T(8,128)(2,1)S(1)} collective-permute-done((bf16[120,1152]{1,0:T(8,128)(2,1)S(1)}, bf16[120,1152]{1,0:T(8,128)(2,1)S(1)}, u32[]{:S(2)}, u32[]{:S(2)}) %collective-permute-start.7) | collective-permute-done | bytes 276512 | tf_op jit(solution)/shard_map/ppermute | solution.py:342
  48.0 1.4 %collective-permute-start.17 = (bf16[80,512]{1,0:T(8,128)(2,1)S(1)}, bf16[80,512]{1,0:T(8,128)(2,1)S(1)}, u32[]{:S(2)}, u32[]{:S(2)}) collective-permute-start(bf16[80,512]{1,0:T(8,128)(2,1)S(1)} %get-tuple-element.43), channel_id=1, source_target_pairs={{0,4},{4,0},{8,12},{12,8},{1,5},{5,1},{9,13},{13,9},{2,6},{6,2},{1... | collective-permute-start | bytes 245768 | tf_op jit(solution)/shard_map/ppermute | solution.py:342
  49.4 1.8 %collective-permute-start.18 = (bf16[80,512]{1,0:T(8,128)(2,1)S(1)}, bf16[80,512]{1,0:T(8,128)(2,1)S(1)}, u32[]{:S(2)}, u32[]{:S(2)}) collective-permute-start(bf16[80,512]{1,0:T(8,128)(2,1)S(1)} %get-tuple-element.44), channel_id=1, source_target_pairs={{0,8},{4,12},{8,0},{12,4},{1,9},{5,13},{9,1},{13,5},{2,10},{6,14},... | collective-permute-start | bytes 245768 | tf_op jit(solution)/shard_map/ppermute | solution.py:342
  51.1 1.3 %collective-permute-start.19 = (bf16[80,512]{1,0:T(8,128)(2,1)S(1)}, bf16[80,512]{1,0:T(8,128)(2,1)S(1)}, u32[]{:S(2)}, u32[]{:S(2)}) collective-permute-start(bf16[80,512]{1,0:T(8,128)(2,1)S(1)} %get-tuple-element.45), channel_id=1, source_target_pairs={{0,12},{4,8},{8,4},{12,0},{1,13},{5,9},{9,5},{13,1},{2,14},{6,10},... | collective-permute-start | bytes 245768 | tf_op jit(solution)/shard_map/ppermute | solution.py:342
  52.5 1.9 %collective-permute-done.16.refs_0_ = bf16[40,3584]{1,0:T(8,128)(2,1)S(1)} collective-permute-done((bf16[40,3584]{1,0:T(8,128)(2,1)S(1)}, bf16[40,3584]{1,0:T(8,128)(2,1)S(1)}, u32[]{:S(2)}, u32[]{:S(2)}) %collective-permute-start.16) | collective-permute-done | bytes 286752 | tf_op jit(solution)/shard_map/ppermute | solution.py:342
  54.4 4.5 %collective-permute-done.18.refs_2_.refs_3_ = bf16[80,512]{1,0:T(8,128)(2,1)S(1)} collective-permute-done((bf16[80,512]{1,0:T(8,128)(2,1)S(1)}, bf16[80,512]{1,0:T(8,128)(2,1)S(1)}, u32[]{:S(2)}, u32[]{:S(2)}) %collective-permute-start.18) | collective-permute-done | bytes 81952 | tf_op jit(solution)/shard_map/ppermute | solution.py:342
  63.1 1.0 %collective-permute-start.23 = (f32[8,128]{1,0:T(8,128)S(1)}, f32[8,128]{1,0:T(8,128)S(1)}, u32[]{:S(2)}, u32[]{:S(2)}) collective-permute-start(f32[8,128]{1,0:T(8,128)S(1)} %get-tuple-element.47.refs_0_), channel_id=1, source_target_pairs={{0,3},{1,2},{2,1},{3,0},{4,7},{5,6},{6,5},{7,4},{8,11},{9,10},{10,... | collective-permute-start | bytes 12296 | tf_op jit(solution)/shard_map/ppermute | solution.py:342
  64.1 1.9 %collective-permute-done.22.refs_2_ = f32[8,128]{1,0:T(8,128)S(1)} collective-permute-done((f32[8,128]{1,0:T(8,128)S(1)}, f32[8,128]{1,0:T(8,128)S(1)}, u32[]{:S(2)}, u32[]{:S(2)}) %collective-permute-start.22) | collective-permute-done | bytes 4128 | tf_op jit(solution)/shard_map/ppermute | solution.py:342
  (72 shorter events, 13.0 us)
Async XLA Ops:
  1.8 8.7 %collective-permute-start = (bf16[80,512]{1,0:T(8,128)(2,1)S(1)}, bf16[80,512]{1,0:T(8,128)(2,1)S(1)}, u32[]{:S(2)}, u32[]{:S(2)}) collective-permute-start(bf16[80,512]{1,0:T(8,128)(2,1)S(1)} %get-tuple-element.27), channel_id=1, source_target_pairs={{0,4},{4,0},{8,12},{12,8},{1,5},{5,1},{9,13},{13,9},{2,6},{6,2},{1... | collective-permute-start | bytes 245768 | tf_op jit(solution)/shard_map/ppermute | solution.py:342
  4.9 9.2 %collective-permute-start.1 = (bf16[80,512]{1,0:T(8,128)(2,1)S(1)}, bf16[80,512]{1,0:T(8,128)(2,1)S(1)}, u32[]{:S(2)}, u32[]{:S(2)}) collective-permute-start(bf16[80,512]{1,0:T(8,128)(2,1)S(1)} %get-tuple-element.28), channel_id=1, source_target_pairs={{0,8},{4,12},{8,0},{12,4},{1,9},{5,13},{9,1},{13,5},{2,10},{6,14},... | collective-permute-start | bytes 245768 | tf_op jit(solution)/shard_map/ppermute | solution.py:342
  7.5 6.6 %collective-permute-start.2 = (bf16[80,512]{1,0:T(8,128)(2,1)S(1)}, bf16[80,512]{1,0:T(8,128)(2,1)S(1)}, u32[]{:S(2)}, u32[]{:S(2)}) collective-permute-start(bf16[80,512]{1,0:T(8,128)(2,1)S(1)} %get-tuple-element.29), channel_id=1, source_target_pairs={{0,12},{4,8},{8,4},{12,0},{1,13},{5,9},{9,5},{13,1},{2,14},{6,10},... | collective-permute-start | bytes 245768 | tf_op jit(solution)/shard_map/ppermute | solution.py:342
  14.1 5.4 %collective-permute-start.4 = (bf16[160,512]{1,0:T(8,128)(2,1)S(1)}, bf16[160,512]{1,0:T(8,128)(2,1)S(1)}, u32[]{:S(2)}, u32[]{:S(2)}) collective-permute-start(bf16[160,512]{1,0:T(8,128)(2,1)S(1)} %get-tuple-element.31), channel_id=1, source_target_pairs={{0,2},{1,3},{2,0},{3,1},{4,6},{5,7},{6,4},{7,5},{8,10},{9,11},{10,... | collective-permute-start | bytes 491528 | tf_op jit(solution)/shard_map/ppermute | solution.py:342
  15.7 5.3 %collective-permute-start.3 = (bf16[160,512]{1,0:T(8,128)(2,1)S(1)}, bf16[160,512]{1,0:T(8,128)(2,1)S(1)}, u32[]{:S(2)}, u32[]{:S(2)}) collective-permute-start(bf16[160,512]{1,0:T(8,128)(2,1)S(1)} %get-tuple-element.30.refs_1_.refs_0_), channel_id=1, source_target_pairs={{0,1},{1,0},{2,3},{3,2},{4,5},{5,4},{6,7},{7,6},{8,9},{9,8},{10,11... | collective-permute-start | bytes 491528 | tf_op jit(solution)/shard_map/ppermute | solution.py:342
  19.5 1.4 %collective-permute-start.5 = (bf16[160,512]{1,0:T(8,128)(2,1)S(1)}, bf16[160,512]{1,0:T(8,128)(2,1)S(1)}, u32[]{:S(2)}, u32[]{:S(2)}) collective-permute-start(bf16[160,512]{1,0:T(8,128)(2,1)S(1)} %hold.6.refs_2_), channel_id=1, source_target_pairs={{0,1},{1,0},{2,3},{3,2},{4,5},{5,4},{6,7},{7,6},{8,9},{9,8},{10,11... | collective-permute-start | bytes 491528 | tf_op jit(solution)/shard_map/ppermute | solution.py:342
  19.5 8.7 %collective-permute-start.6 = (f32[4,128,128]{2,1,0:T(8,128)S(1)}, f32[4,128,128]{2,1,0:T(8,128)S(1)}, u32[]{:S(2)}, u32[]{:S(2)}) collective-permute-start(f32[4,128,128]{2,1,0:T(8,128)S(1)} %hold.7.refs_0_), channel_id=1, source_target_pairs={{0,4},{4,0},{8,12},{12,8},{1,5},{5,1},{9,13},{13,9},{2,6},{6,2},{1... | collective-permute-start | bytes 786440 | tf_op jit(solution)/shard_map/ppermute | solution.py:342
  23.2 13.3 %collective-permute-start.10 = (bf16[120,1408]{1,0:T(8,128)(2,1)S(1)}, bf16[120,1408]{1,0:T(8,128)(2,1)S(1)}, u32[]{:S(2)}, u32[]{:S(2)}) collective-permute-start(bf16[120,1408]{1,0:T(8,128)(2,1)S(1)} %get-tuple-element.39), channel_id=1, source_target_pairs={{0,2},{1,3},{2,0},{3,1},{4,6},{5,7},{6,4},{7,5},{8,10},{9,11},{10,... | collective-permute-start | bytes 1013768 | tf_op jit(solution)/shard_map/ppermute | solution.py:342
  29.9 10.8 %collective-permute-start.8 = (bf16[120,1024]{1,0:T(8,128)(2,1)S(1)}, bf16[120,1024]{1,0:T(8,128)(2,1)S(1)}, u32[]{:S(2)}, u32[]{:S(2)}) collective-permute-start(bf16[120,1024]{1,0:T(8,128)(2,1)S(1)} %get-tuple-element.38), channel_id=1, source_target_pairs={{0,2},{1,3},{2,0},{3,1},{4,6},{5,7},{6,4},{7,5},{8,10},{9,11},{10,... | collective-permute-start | bytes 737288 | tf_op jit(solution)/shard_map/ppermute | solution.py:342
  31.4 8.6 %collective-permute-start.9 = (bf16[4,128,128]{2,1,0:T(8,128)(2,1)S(1)}, bf16[4,128,128]{2,1,0:T(8,128)(2,1)S(1)}, u32[]{:S(2)}, u32[]{:S(2)}) collective-permute-start(bf16[4,128,128]{2,1,0:T(8,128)(2,1)S(1)} %pair_sum.1.refs_6_.refs_0_), channel_id=1, source_target_pairs={{0,8},{4,12},{8,0},{12,4},{1,9},{5,13},{9,1},{13,5},{2,10},{6,14},... | collective-permute-start | bytes 393224 | tf_op jit(solution)/shard_map/ppermute | solution.py:342
  35.9 11.2 %collective-permute-start.14 = (bf16[160,1792]{1,0:T(8,128)(2,1)S(1)}, bf16[160,1792]{1,0:T(8,128)(2,1)S(1)}, u32[]{:S(2)}, u32[]{:S(2)}) collective-permute-start(bf16[160,1792]{1,0:T(8,128)(2,1)S(1)} %get-tuple-element.36.refs_0_), channel_id=1, source_target_pairs={{0,1},{1,0},{2,3},{3,2},{4,5},{5,4},{6,7},{7,6},{8,9},{9,8},{10,11... | collective-permute-start | bytes 1720328 | tf_op jit(solution)/shard_map/ppermute | solution.py:342
  36.0 11.2 %collective-permute-start.15 = (bf16[160,1792]{1,0:T(8,128)(2,1)S(1)}, bf16[160,1792]{1,0:T(8,128)(2,1)S(1)}, u32[]{:S(2)}, u32[]{:S(2)}) collective-permute-start(bf16[160,1792]{1,0:T(8,128)(2,1)S(1)} %get-tuple-element.37.refs_1_), channel_id=1, source_target_pairs={{0,1},{1,0},{2,3},{3,2},{4,5},{5,4},{6,7},{7,6},{8,9},{9,8},{10,11... | collective-permute-start | bytes 1720328 | tf_op jit(solution)/shard_map/ppermute | solution.py:342
  36.5 8.6 %collective-permute-start.7 = (bf16[120,1152]{1,0:T(8,128)(2,1)S(1)}, bf16[120,1152]{1,0:T(8,128)(2,1)S(1)}, u32[]{:S(2)}, u32[]{:S(2)}) collective-permute-start(bf16[120,1152]{1,0:T(8,128)(2,1)S(1)} %get-tuple-element.34), channel_id=1, source_target_pairs={{0,2},{1,3},{2,0},{3,1},{4,6},{5,7},{6,4},{7,5},{8,10},{9,11},{10,... | collective-permute-start | bytes 829448 | tf_op jit(solution)/shard_map/ppermute | solution.py:342
  40.7 1.5 %collective-permute-start.11 = (bf16[120,1024]{1,0:T(8,128)(2,1)S(1)}, bf16[120,1024]{1,0:T(8,128)(2,1)S(1)}, u32[]{:S(2)}, u32[]{:S(2)}) collective-permute-start(bf16[120,1024]{1,0:T(8,128)(2,1)S(1)} %hold.9.refs_0_), channel_id=1, source_target_pairs={{0,1},{1,0},{2,3},{3,2},{4,5},{5,4},{6,7},{7,6},{8,9},{9,8},{10,11... | collective-permute-start | bytes 737288 | tf_op jit(solution)/shard_map/ppermute | solution.py:342
  40.7 5.7 %collective-permute-start.13 = (bf16[120,1408]{1,0:T(8,128)(2,1)S(1)}, bf16[120,1408]{1,0:T(8,128)(2,1)S(1)}, u32[]{:S(2)}, u32[]{:S(2)}) collective-permute-start(bf16[120,1408]{1,0:T(8,128)(2,1)S(1)} %hold.8.refs_0_), channel_id=1, source_target_pairs={{0,1},{1,0},{2,3},{3,2},{4,5},{5,4},{6,7},{7,6},{8,9},{9,8},{10,11... | collective-permute-start | bytes 1013768 | tf_op jit(solution)/shard_map/ppermute | solution.py:342
  45.1 1.7 %collective-permute-start.12 = (bf16[120,1152]{1,0:T(8,128)(2,1)S(1)}, bf16[120,1152]{1,0:T(8,128)(2,1)S(1)}, u32[]{:S(2)}, u32[]{:S(2)}) collective-permute-start(bf16[120,1152]{1,0:T(8,128)(2,1)S(1)} %hold.10.refs_0_), channel_id=1, source_target_pairs={{0,1},{1,0},{2,3},{3,2},{4,5},{5,4},{6,7},{7,6},{8,9},{9,8},{10,11... | collective-permute-start | bytes 829448 | tf_op jit(solution)/shard_map/ppermute | solution.py:342
  45.1 9.2 %collective-permute-start.16 = (bf16[40,3584]{1,0:T(8,128)(2,1)S(1)}, bf16[40,3584]{1,0:T(8,128)(2,1)S(1)}, u32[]{:S(2)}, u32[]{:S(2)}) collective-permute-start(bf16[40,3584]{1,0:T(8,128)(2,1)S(1)} %get-tuple-element.40.refs_1_), channel_id=1, source_target_pairs={{0,2},{1,3},{2,0},{3,1},{4,6},{5,7},{6,4},{7,5},{8,10},{9,11},{10,... | collective-permute-start | bytes 860168 | tf_op jit(solution)/shard_map/ppermute | solution.py:342
  48.0 6.3 %collective-permute-start.17 = (bf16[80,512]{1,0:T(8,128)(2,1)S(1)}, bf16[80,512]{1,0:T(8,128)(2,1)S(1)}, u32[]{:S(2)}, u32[]{:S(2)}) collective-permute-start(bf16[80,512]{1,0:T(8,128)(2,1)S(1)} %get-tuple-element.43), channel_id=1, source_target_pairs={{0,4},{4,0},{8,12},{12,8},{1,5},{5,1},{9,13},{13,9},{2,6},{6,2},{1... | collective-permute-start | bytes 245768 | tf_op jit(solution)/shard_map/ppermute | solution.py:342
  49.4 9.5 %collective-permute-start.18 = (bf16[80,512]{1,0:T(8,128)(2,1)S(1)}, bf16[80,512]{1,0:T(8,128)(2,1)S(1)}, u32[]{:S(2)}, u32[]{:S(2)}) collective-permute-start(bf16[80,512]{1,0:T(8,128)(2,1)S(1)} %get-tuple-element.44), channel_id=1, source_target_pairs={{0,8},{4,12},{8,0},{12,4},{1,9},{5,13},{9,1},{13,5},{2,10},{6,14},... | collective-permute-start | bytes 245768 | tf_op jit(solution)/shard_map/ppermute | solution.py:342
  51.1 7.8 %collective-permute-start.19 = (bf16[80,512]{1,0:T(8,128)(2,1)S(1)}, bf16[80,512]{1,0:T(8,128)(2,1)S(1)}, u32[]{:S(2)}, u32[]{:S(2)}) collective-permute-start(bf16[80,512]{1,0:T(8,128)(2,1)S(1)} %get-tuple-element.45), channel_id=1, source_target_pairs={{0,12},{4,8},{8,4},{12,0},{1,13},{5,9},{9,5},{13,1},{2,14},{6,10},... | collective-permute-start | bytes 245768 | tf_op jit(solution)/shard_map/ppermute | solution.py:342
  58.9 1.6 %collective-permute-start.20 = (bf16[40,3584]{1,0:T(8,128)(2,1)S(1)}, bf16[40,3584]{1,0:T(8,128)(2,1)S(1)}, u32[]{:S(2)}, u32[]{:S(2)}) collective-permute-start(bf16[40,3584]{1,0:T(8,128)(2,1)S(1)} %hold.11.refs_0_), channel_id=1, source_target_pairs={{0,1},{1,0},{2,3},{3,2},{4,5},{5,4},{6,7},{7,6},{8,9},{9,8},{10,11... | collective-permute-start | bytes 860168 | tf_op jit(solution)/shard_map/ppermute | solution.py:342
  62.2 1.9 %collective-permute-start.21 = (f32[8,128]{1,0:T(8,128)S(1)}, f32[8,128]{1,0:T(8,128)S(1)}, u32[]{:S(2)}, u32[]{:S(2)}) collective-permute-start(f32[8,128]{1,0:T(8,128)S(1)} %get-tuple-element.47.refs_0_), channel_id=1, source_target_pairs={{0,1},{1,0},{2,3},{3,2},{4,5},{5,4},{6,7},{7,6},{8,9},{9,8},{10,11... | collective-permute-start | bytes 12296 | tf_op jit(solution)/shard_map/ppermute | solution.py:342
  62.3 3.6 %collective-permute-start.22 = (f32[8,128]{1,0:T(8,128)S(1)}, f32[8,128]{1,0:T(8,128)S(1)}, u32[]{:S(2)}, u32[]{:S(2)}) collective-permute-start(f32[8,128]{1,0:T(8,128)S(1)} %get-tuple-element.47.refs_0_), channel_id=1, source_target_pairs={{0,2},{1,3},{2,0},{3,1},{4,6},{5,7},{6,4},{7,5},{8,10},{9,11},{10,... | collective-permute-start | bytes 12296 | tf_op jit(solution)/shard_map/ppermute | solution.py:342
  63.1 3.0 %collective-permute-start.23 = (f32[8,128]{1,0:T(8,128)S(1)}, f32[8,128]{1,0:T(8,128)S(1)}, u32[]{:S(2)}, u32[]{:S(2)}) collective-permute-start(f32[8,128]{1,0:T(8,128)S(1)} %get-tuple-element.47.refs_0_), channel_id=1, source_target_pairs={{0,3},{1,2},{2,1},{3,0},{4,7},{5,6},{6,5},{7,4},{8,11},{9,10},{10,... | collective-permute-start | bytes 12296 | tf_op jit(solution)/shard_map/ppermute | solution.py:342
  (9 other events, 58.5 us)

commit v4 on v3

--- a/solution.py
+++ b/solution.py
@@ -134,11 +134,12 @@
 LISTS = 8
 ROWS = OWNERS * MOST
 REMOTE = ROWS - MOST
-CHUNKS = (1408, 1024, 1152)
-STARTS = (0, 1408, 2432)
+CHUNKS = (1152, 1024, 1408)
+STARTS = (0, 1152, 2176)
 HALF = FF // 2
 BLOCK = 256
-FLUSH = ((), (1,), (0, 2))
+SEND_ORDER = (2, 3, 1)
+FLUSH = ((), (0, 1), (2,))
 OWN_NEAR = ((0, 0, 0), (HALF // 2, 0, 0))
 OWN_FAR = ((0, 0, 1), (HALF // 2, 0, 1))
 ANY = pl.BlockSpec(memory_space=pl.ANY)
@@ -201,7 +202,7 @@
     )
 
 
-def pack_kernel(place, ids_ref, tokens_ref, *refs):
+def pack_kernel(place, ids_ref, tokens_ref, gate_hbm, up_hbm, *refs):
     outs, (ids, tokens, sems) = refs[:OWNERS], refs[OWNERS:]
     copies = [
         pltpu.make_async_copy(ids_ref, ids, sems.at[0]),
@@ -230,12 +231,12 @@
 
 def split_kernel(place, *refs):
     own_ref, other_ref = refs[OWNERS:]
-    order = [refs[s][...].astype(jnp.float32) for s in (1, 2, 3, 0)]
+    order = [ref[...].astype(jnp.float32) for ref in (*reversed(refs[: OWNERS - 1]), refs[OWNERS - 1])]
     own_ref[...] = jnp.concatenate([d[:MOST] for d in order], axis=0).astype(jnp.bfloat16)
     other_ref[...] = jnp.concatenate([d[MOST:] for d in order], axis=0).astype(jnp.bfloat16)
 
 
-def masked_kernel(place, context_hbm, grad_hbm, kept_hbm, gate_hbm, up_hbm, out_ref, *scratch):
+def masked_kernel(place, context_hbm, grad_hbm, kept_hbm, out_ref, *scratch):
     context, grad, kept_ref, sems = scratch
     pairs = ((context_hbm, context), (grad_hbm, grad), (kept_hbm, kept_ref))
     copies = [pltpu.make_async_copy(*pair, sems.at[i]) for i, pair in enumerate(pairs)]
@@ -271,16 +272,32 @@
     token_ref[...] = jnp.zeros_like(token_ref)
 
 
-def hidden_kernel(first, place, a0, a1, a2, a3, gate_ref, up_ref, out_ref, remote_ref, rows):
-    for j, piece in enumerate((a0, a1, a2, a3)):
-        width = piece.shape[1]
-        start = pl.multiple_of((place[1] ^ j) * width, width)
-        rows[:, pl.ds(start, width)] = piece[...]
+def features_of(place, by, width):
+    return pl.ds(pl.multiple_of((place[1] ^ by) * width, width), width)
+
+
+def begun_kernel(place, own, gate_ref, up_ref, gate_out, up_out):
+    features = features_of(place, 0, own.shape[1])
+    for start in range(0, gate_out.shape[1], BLOCK):
+        units = slice(start, min(start + BLOCK, gate_out.shape[1]))
+        gate_out[:, units] = product(own[...], gate_ref[features, units])
+        up_out[:, units] = product(own[...], up_ref[features, units])
+
+
+def hidden_kernel(first, place, a0, a1, a2, a3, *refs):
+    begun, (gate_ref, up_ref, out_ref, remote_ref) = refs[:-4], refs[-4:]
+    pieces = [(by, piece[...]) for by, piece in enumerate((a0, a1, a2, a3)) if by or not begun]
     for start in range(0, out_ref.shape[1], BLOCK):
         columns = slice(start, min(start + BLOCK, out_ref.shape[1]))
         units = slice(first + columns.start, first + columns.stop)
-        gate = product(rows[...], gate_ref[:, units])
-        up = product(rows[...], up_ref[:, units])
+        acts = []
+        for i, weight_ref in enumerate((gate_ref, up_ref)):
+            act = begun[i][:, columns] if begun else None
+            for by, piece in pieces:
+                term = product(piece, weight_ref[features_of(place, by, piece.shape[1]), units])
+                act = term if act is None else act + term
+            acts.append(act)
+        gate, up = acts
         hidden = gate / (1.0 + jnp.exp(-gate)) * up
         out_ref[:, columns] = hidden.astype(jnp.bfloat16)
         remote_ref[:, columns] = hidden[:REMOTE].astype(jnp.bfloat16)
@@ -319,7 +336,7 @@
     outs[-1][...] = mine_ref[REMOTE:, :].astype(jnp.bfloat16)
 
 
-def combine_kernel(place, own, other, b1, b2, b3, route_ref, grad_ref, layer_ref, router_ref):
+def combine_kernel(place, own, other, b3, b2, b1, route_ref, grad_ref, layer_ref, router_ref):
     count, columns = grad_ref.shape
     stacked = [ref[...].astype(jnp.float32) for ref in (own, other, b1, b2, b3)]
     stacked.append(jnp.zeros((64, columns), jnp.float32))
@@ -362,20 +379,21 @@
     packed = call(
         pack_kernel,
         "pack",
-        (ids, tokens),
+        (ids, tokens, gate_weight, up_weight),
         [shape(2 * MOST, columns)] * OWNERS,
-        far=(0, 1),
+        far=(0, 1, 2, 3),
         scratch=[pltpu.VMEM(ids.shape, ids.dtype), pltpu.VMEM(tokens.shape, tokens.dtype), dma((2,))],
     )
-    arrived = [packed[0]] + [swap(packed[s], "rank", s) for s in (1, 2, 3)]
+    sent = {s: swap(packed[s], "rank", s) for s in SEND_ORDER}
+    arrived = [sent[3], sent[2], sent[1], packed[0]]
     blocks = (kept_rows.shape[0], kept_rows.shape[1], 128)
     partial = call(
         masked_kernel,
         "masked",
-        (context, out_grad, kept_rows, gate_weight, up_weight),
+        (context, out_grad, kept_rows),
         [shape(*blocks, dtype=f32)],
         after=(packed[0],),
-        far=(0, 1, 2, 3, 4),
+        far=(0, 1, 2),
         limit=4,
         scratch=[
             pltpu.VMEM(context.shape, context.dtype),
@@ -397,7 +415,10 @@
         return call(pass_kernel, "hold", (value,), [value], after=after, aliases={0: 0})[0]
 
     held = hold(partial, own)
-    crossed = hold(crossed, own)
+    begun = call(
+        begun_kernel, "begun", (own, gate_weight, up_weight), [shape(ROWS, CHUNKS[0], dtype=f32)] * 2
+    )
+    crossed = hold(crossed, begun[0])
     crossed_far = swap(crossed, "tensor", 1)
     pieces = (own, own_far, crossed, crossed_far)
 
@@ -406,16 +427,15 @@
         made = call(
             functools.partial(hidden_kernel, STARTS[k]),
             "hidden",
-            (*pieces, gate_weight, up_weight),
+            (*pieces, *(begun if k == 0 else ()), gate_weight, up_weight),
             [shape(ROWS, width), shape(REMOTE, width)],
             after=(last,),
-            scratch=[pltpu.VMEM((ROWS, depth), jnp.bfloat16)],
             cost=20 if k == 0 else 0,
         )
         hidden.append(made[0])
         remote.append(made[1])
         last = made[0]
-        if k == 0:
+        if k == 1:
             last = pair = call(
                 sum_kernel, "pair_sum", (held, swap(held, "rank", 1)), [shape(*blocks)], after=(last,)
             )[0]
@@ -474,18 +494,20 @@
         (total, mine),
         [shape(2 * MOST, columns)] * 3 + [shape(MOST, columns)],
     )
-    lists = [swap(backs[s - 1], "rank", s) for s in (1, 2, 3)]
-    near = hold(own_across, *lists)
+    back = {s: swap(backs[s - 1], "rank", s) for s in SEND_ORDER}
+    lists = [back[s] for s in (1, 2, 3)]
+    near = hold(own_across, *reversed(lists))
     far = swap(near, "tensor", 1)
     last = add(((0, 1, 0),), (near,), None)
     last = add(((0, 1, 1),), (far,), last)
     layer_output, router = call(
         combine_kernel,
         "combine",
-        (own, last, *lists, route, out_grad),
+        (own, last, *reversed(lists), route, out_grad),
         [shape(token_count, columns), shape(8, token_count, dtype=f32)],
     )
-    routers = [router] + [swap(router, "tensor", t) for t in (1, 2, 3)]
+    scores = {t: swap(router, "tensor", t) for t in (2, 3, 1)}
+    routers = [router] + [scores[t] for t in (1, 2, 3)]
     router_grad = call(router_kernel, "router", tuple(routers), [shape(2, token_count, dtype=f32)])[0]
     return (layer_output, router_grad.T, masked_grad)
 

time: 66.8 us -> 65.3 us (0.978)
  waiting for transfers between devices: 25.2 us -> 23.8 us
  starting transfers between devices: 23.1 us -> 21.9 us
  Pallas kernels: 17.4 us -> 18.4 us
    ppermute x24, waiting for transfers between devices: 25.2 us -> 23.8 us  [swap(): return lax.ppermute(value, axis, [(i, i ^ by) for i in range(4)])]
    ppermute x24, starting transfers between devices: 23.1 us -> 21.9 us  [swap(): return lax.ppermute(value, axis, [(i, i ^ by) for i in range(4)])]
    pallas_call x29 -> x30, Pallas kernels: 17.4 us -> 18.4 us  [call(): pl.pallas_call(body, out_shape=outs, in_specs=[HBM if i in far else VMEM...]
  transfers between devices with their start and end apart: 24 -> 24, of which waited for: 11 -> 13; matrix products, arithmetic and copies ran while one was open for 0% -> 0% of each run, Pallas kernels for 21% -> 23%
where the time goes in v4:
time: 65.3 us; the launch traced here: 65.2 us
  waiting for transfers between devices  23.8 us (36%)
  starting transfers between devices  21.9 us (34%)
  Pallas kernels  18.4 us (28%)
  between operations  0.97 us (1%)
    ppermute x24, waiting for transfers between devices, swap(): return lax.ppermute(value, axis, [(i, i ^ by) for i in range(4)])  23.8 us
    ppermute x24, starting transfers between devices, swap(): return lax.ppermute(value, axis, [(i, i ^ by) for i in range(4)])  21.9 us
    pallas_call x30, Pallas kernels, call(): pl.pallas_call(body, out_shape=outs, in_specs=[HBM if i in far else VMEM...  18.4 us
  transfers between devices with their start and end apart: 24, of which 13 were waited for; matrix products, arithmetic and copies ran while one was open for 0% of the time, Pallas kernels for 23%

profile of v4, /device:TPU:0, one launch (start us, length us, event | category | flops | bytes accessed | tf_op | source)
XLA Modules:
  0.0 65.2 jit_solution(12258077184444786718)
XLA Ops:
  0.7 1.3 %pack.1 = (bf16[80,512]{1,0:T(8,128)(2,1)S(1)}, bf16[80,512]{1,0:T(8,128)(2,1)S(1)}, bf16[80,512]{1,0:T(8,128)(2,1)S(1)}, bf16[80,512]{1,0:T(8,128)(2,1)S(1)}) custom-call(s32[2,128]{1,0:T(2,128)} %bitcast.5, bf16[128,512]{1,0:T(8,128)(2,1)} %refs_1_.11, bf16[2048,3584]{1,0:T(8,128)(2,1)} %refs_4_.3, bf16[2048,3584]{1,0:T(8,128)(2,1)} %refs_5_.3), custom_call_target="tpu_custom_call" | custom-call | tf_op jit(solution)/shard_map/pack/pallas_call | solution.py:161
  2.0 5.1 %collective-permute-start = (bf16[80,512]{1,0:T(8,128)(2,1)S(1)}, bf16[80,512]{1,0:T(8,128)(2,1)S(1)}, u32[]{:S(2)}, u32[]{:S(2)}) collective-permute-start(bf16[80,512]{1,0:T(8,128)(2,1)S(1)} %get-tuple-element.28), channel_id=1, source_target_pairs={{0,12},{4,8},{8,4},{12,0},{1,13},{5,9},{9,5},{13,1},{2,14},{6,10},... | collective-permute-start | bytes 245768 | tf_op jit(solution)/shard_map/ppermute | solution.py:359
  7.8 3.2 %masked.1.refs_2_.refs_0_ = f32[4,128,128]{2,1,0:T(8,128)S(1)} custom-call(bf16[128,2048]{1,0:T(8,128)(2,1)} %refs_0_.1, bf16[128,512]{1,0:T(8,128)(2,1)} %refs_6_.3, s32[4,128]{1,0:T(4,128)} %refs_2_.6, bf16[80,512]{1,0:T(8,128)(2,1)S(1)} %get-tuple-element.31.refs_3_), custom_call_target="tpu_custom_call" | custom-call | tf_op jit(solution)/shard_map/masked/pallas_call | solution.py:161
  11.4 2.6 %collective-permute-done.1.refs_1_ = bf16[80,512]{1,0:T(8,128)(2,1)S(1)} collective-permute-done((bf16[80,512]{1,0:T(8,128)(2,1)S(1)}, bf16[80,512]{1,0:T(8,128)(2,1)S(1)}, u32[]{:S(2)}, u32[]{:S(2)}) %collective-permute-start.1) | collective-permute-done | bytes 81952 | tf_op jit(solution)/shard_map/ppermute | solution.py:359
  14.0 1.6 %collective-permute-start.4 = (bf16[160,512]{1,0:T(8,128)(2,1)S(1)}, bf16[160,512]{1,0:T(8,128)(2,1)S(1)}, u32[]{:S(2)}, u32[]{:S(2)}) collective-permute-start(bf16[160,512]{1,0:T(8,128)(2,1)S(1)} %get-tuple-element.33), channel_id=1, source_target_pairs={{0,2},{1,3},{2,0},{3,1},{4,6},{5,7},{6,4},{7,5},{8,10},{9,11},{10,... | collective-permute-start | bytes 491528 | tf_op jit(solution)/shard_map/ppermute | solution.py:359
  16.2 3.3 %collective-permute-done.4.refs_0_ = bf16[160,512]{1,0:T(8,128)(2,1)S(1)} collective-permute-done((bf16[160,512]{1,0:T(8,128)(2,1)S(1)}, bf16[160,512]{1,0:T(8,128)(2,1)S(1)}, u32[]{:S(2)}, u32[]{:S(2)}) %collective-permute-start.4) | collective-permute-done | bytes 163872 | tf_op jit(solution)/shard_map/ppermute | solution.py:359
  20.9 1.5 %hidden.3 = (bf16[160,1152]{1,0:T(8,128)(2,1)S(1)}, bf16[120,1152]{1,0:T(8,128)(2,1)S(1)}) custom-call(bf16[160,512]{1,0:T(8,128)(2,1)S(1)} %get-tuple-element.32.refs_0_.refs_1_, bf16[160,512]{1,0:T(8,128)(2,1)S(1)} %collective-permute-done.3.refs_1_, bf16[160,512]{1,0:T(8,128)(2,1)S(1)} %hold.6.refs_2_, ...), custom_call_target="tpu_custom_call" | custom-call | bytes 60000000 | tf_op jit(solution)/shard_map/hidden/pallas_call | solution.py:161
  22.4 1.7 %collective-permute-start.10 = (bf16[120,1152]{1,0:T(8,128)(2,1)S(1)}, bf16[120,1152]{1,0:T(8,128)(2,1)S(1)}, u32[]{:S(2)}, u32[]{:S(2)}) collective-permute-start(bf16[120,1152]{1,0:T(8,128)(2,1)S(1)} %get-tuple-element.43), channel_id=1, source_target_pairs={{0,2},{1,3},{2,0},{3,1},{4,6},{5,7},{6,4},{7,5},{8,10},{9,11},{10,... | collective-permute-start | bytes 829448 | tf_op jit(solution)/shard_map/ppermute | solution.py:359
  24.1 1.6 %hidden.4 = (bf16[160,1024]{1,0:T(8,128)(2,1)S(1)}, bf16[120,1024]{1,0:T(8,128)(2,1)S(1)}) custom-call(bf16[160,512]{1,0:T(8,128)(2,1)S(1)} %get-tuple-element.32.refs_0_.refs_1_, bf16[160,512]{1,0:T(8,128)(2,1)S(1)} %collective-permute-done.3.refs_1_, bf16[160,512]{1,0:T(8,128)(2,1)S(1)} %hold.6.refs_2_, ...), custom_call_target="tpu_custom_call" | custom-call | tf_op jit(solution)/shard_map/hidden/pallas_call | solution.py:161
  26.1 2.1 %collective-permute-done.6.refs_1_ = f32[4,128,128]{2,1,0:T(8,128)S(1)} collective-permute-done((f32[4,128,128]{2,1,0:T(8,128)S(1)}, f32[4,128,128]{2,1,0:T(8,128)S(1)}, u32[]{:S(2)}, u32[]{:S(2)}) %collective-permute-start.6) | collective-permute-done | bytes 262176 | tf_op jit(solution)/shard_map/ppermute | solution.py:359
  28.3 1.5 %collective-permute-start.9 = (bf16[4,128,128]{2,1,0:T(8,128)(2,1)S(1)}, bf16[4,128,128]{2,1,0:T(8,128)(2,1)S(1)}, u32[]{:S(2)}, u32[]{:S(2)}) collective-permute-start(bf16[4,128,128]{2,1,0:T(8,128)(2,1)S(1)} %pair_sum.1.refs_6_.refs_0_), channel_id=1, source_target_pairs={{0,8},{4,12},{8,0},{12,4},{1,9},{5,13},{9,1},{13,5},{2,10},{6,14},... | collective-permute-start | bytes 393224 | tf_op jit(solution)/shard_map/ppermute | solution.py:359
  29.8 2.2 %hidden.5 = (bf16[160,1408]{1,0:T(8,128)(2,1)S(1)}, bf16[120,1408]{1,0:T(8,128)(2,1)S(1)}) custom-call(bf16[160,512]{1,0:T(8,128)(2,1)S(1)} %get-tuple-element.32.refs_0_.refs_1_, bf16[160,512]{1,0:T(8,128)(2,1)S(1)} %collective-permute-done.3.refs_1_, bf16[160,512]{1,0:T(8,128)(2,1)S(1)} %hold.6.refs_2_, ...), custom_call_target="tpu_custom_call" | custom-call | tf_op jit(solution)/shard_map/hidden/pallas_call | solution.py:161
  32.0 1.6 %collective-permute-start.7 = (bf16[120,1408]{1,0:T(8,128)(2,1)S(1)}, bf16[120,1408]{1,0:T(8,128)(2,1)S(1)}, u32[]{:S(2)}, u32[]{:S(2)}) collective-permute-start(bf16[120,1408]{1,0:T(8,128)(2,1)S(1)} %get-tuple-element.38), channel_id=1, source_target_pairs={{0,2},{1,3},{2,0},{3,1},{4,6},{5,7},{6,4},{7,5},{8,10},{9,11},{10,... | collective-permute-start | bytes 1013768 | tf_op jit(solution)/shard_map/ppermute | solution.py:359
  34.2 3.0 %collective-permute-done.9.refs_1_ = bf16[4,128,128]{2,1,0:T(8,128)(2,1)S(1)} collective-permute-done((bf16[4,128,128]{2,1,0:T(8,128)(2,1)S(1)}, bf16[4,128,128]{2,1,0:T(8,128)(2,1)S(1)}, u32[]{:S(2)}, u32[]{:S(2)}) %collective-permute-start.9) | collective-permute-done | bytes 131104 | tf_op jit(solution)/shard_map/ppermute | solution.py:359
  40.5 3.1 %collective-permute-done.7.refs_0_ = bf16[120,1408]{1,0:T(8,128)(2,1)S(1)} collective-permute-done((bf16[120,1408]{1,0:T(8,128)(2,1)S(1)}, bf16[120,1408]{1,0:T(8,128)(2,1)S(1)}, u32[]{:S(2)}, u32[]{:S(2)}) %collective-permute-start.7) | collective-permute-done | bytes 337952 | tf_op jit(solution)/shard_map/ppermute | solution.py:359
  43.7 1.6 %collective-permute-start.16 = (bf16[40,3584]{1,0:T(8,128)(2,1)S(1)}, bf16[40,3584]{1,0:T(8,128)(2,1)S(1)}, u32[]{:S(2)}, u32[]{:S(2)}) collective-permute-start(bf16[40,3584]{1,0:T(8,128)(2,1)S(1)} %get-tuple-element.44.refs_1_), channel_id=1, source_target_pairs={{0,2},{1,3},{2,0},{3,1},{4,6},{5,7},{6,4},{7,5},{8,10},{9,11},{10,... | collective-permute-start | bytes 860168 | tf_op jit(solution)/shard_map/ppermute | solution.py:359
  46.9 2.5 %collective-permute-start.17 = (bf16[80,512]{1,0:T(8,128)(2,1)S(1)}, bf16[80,512]{1,0:T(8,128)(2,1)S(1)}, u32[]{:S(2)}, u32[]{:S(2)}) collective-permute-start(bf16[80,512]{1,0:T(8,128)(2,1)S(1)} %get-tuple-element.47), channel_id=1, source_target_pairs={{0,12},{4,8},{8,4},{12,0},{1,13},{5,9},{9,5},{13,1},{2,14},{6,10},... | collective-permute-start | bytes 245768 | tf_op jit(solution)/shard_map/ppermute | solution.py:359
  49.5 1.9 %collective-permute-start.19 = (bf16[80,512]{1,0:T(8,128)(2,1)S(1)}, bf16[80,512]{1,0:T(8,128)(2,1)S(1)}, u32[]{:S(2)}, u32[]{:S(2)}) collective-permute-start(bf16[80,512]{1,0:T(8,128)(2,1)S(1)} %get-tuple-element.49), channel_id=1, source_target_pairs={{0,4},{4,0},{8,12},{12,8},{1,5},{5,1},{9,13},{13,9},{2,6},{6,2},{1... | collective-permute-start | bytes 245768 | tf_op jit(solution)/shard_map/ppermute | solution.py:359
  51.4 1.5 %collective-permute-done.16.refs_0_ = bf16[40,3584]{1,0:T(8,128)(2,1)S(1)} collective-permute-done((bf16[40,3584]{1,0:T(8,128)(2,1)S(1)}, bf16[40,3584]{1,0:T(8,128)(2,1)S(1)}, u32[]{:S(2)}, u32[]{:S(2)}) %collective-permute-start.16) | collective-permute-done | bytes 286752 | tf_op jit(solution)/shard_map/ppermute | solution.py:359
  52.9 1.3 %collective-permute-done.17.refs_1_.refs_2_ = bf16[80,512]{1,0:T(8,128)(2,1)S(1)} collective-permute-done((bf16[80,512]{1,0:T(8,128)(2,1)S(1)}, bf16[80,512]{1,0:T(8,128)(2,1)S(1)}, u32[]{:S(2)}, u32[]{:S(2)}) %collective-permute-start.17) | collective-permute-done | bytes 81952 | tf_op jit(solution)/shard_map/ppermute | solution.py:359
  54.2 2.8 %collective-permute-done.18.refs_2_.refs_3_ = bf16[80,512]{1,0:T(8,128)(2,1)S(1)} collective-permute-done((bf16[80,512]{1,0:T(8,128)(2,1)S(1)}, bf16[80,512]{1,0:T(8,128)(2,1)S(1)}, u32[]{:S(2)}, u32[]{:S(2)}) %collective-permute-start.18) | collective-permute-done | bytes 81952 | tf_op jit(solution)/shard_map/ppermute | solution.py:359
  59.3 1.0 %combine.1 = (bf16[128,512]{1,0:T(8,128)(2,1)}, f32[8,128]{1,0:T(8,128)S(1)}) custom-call(bf16[40,512]{1,0:T(8,128)(2,1)S(1)} %get-tuple-element.46.refs_0_, f32[40,512]{1,0:T(8,128)S(1)} %down_add.19.refs_1_, bf16[80,512]{1,0:T(8,128)(2,1)S(1)} %collective-permute-done.17.refs_1_.refs_2_, bf16[80,512]{1,0:T(8,128)(2,1)S(1)} %collective-permute-done.18.refs_2_.refs_3_, ...), custom_call_target="tpu_custom_call" | custom-call | tf_op jit(solution)/shard_map/combine/pallas_call | solution.py:161
  60.4 1.2 %collective-permute-start.22 = (f32[8,128]{1,0:T(8,128)S(1)}, f32[8,128]{1,0:T(8,128)S(1)}, u32[]{:S(2)}, u32[]{:S(2)}) collective-permute-start(f32[8,128]{1,0:T(8,128)S(1)} %get-tuple-element.51.refs_0_), channel_id=1, source_target_pairs={{0,2},{1,3},{2,0},{3,1},{4,6},{5,7},{6,4},{7,5},{8,10},{9,11},{10,... | collective-permute-start | bytes 12296 | tf_op jit(solution)/shard_map/ppermute | solution.py:359
  62.1 1.9 %collective-permute-done.22.refs_2_ = f32[8,128]{1,0:T(8,128)S(1)} collective-permute-done((f32[8,128]{1,0:T(8,128)S(1)}, f32[8,128]{1,0:T(8,128)S(1)}, u32[]{:S(2)}, u32[]{:S(2)}) %collective-permute-start.22) | collective-permute-done | bytes 4128 | tf_op jit(solution)/shard_map/ppermute | solution.py:359
  (73 shorter events, 13.1 us)
Async XLA Ops:
  2.0 9.3 %collective-permute-start = (bf16[80,512]{1,0:T(8,128)(2,1)S(1)}, bf16[80,512]{1,0:T(8,128)(2,1)S(1)}, u32[]{:S(2)}, u32[]{:S(2)}) collective-permute-start(bf16[80,512]{1,0:T(8,128)(2,1)S(1)} %get-tuple-element.28), channel_id=1, source_target_pairs={{0,12},{4,8},{8,4},{12,0},{1,13},{5,9},{9,5},{13,1},{2,14},{6,10},... | collective-permute-start | bytes 245768 | tf_op jit(solution)/shard_map/ppermute | solution.py:359
  7.1 6.9 %collective-permute-start.1 = (bf16[80,512]{1,0:T(8,128)(2,1)S(1)}, bf16[80,512]{1,0:T(8,128)(2,1)S(1)}, u32[]{:S(2)}, u32[]{:S(2)}) collective-permute-start(bf16[80,512]{1,0:T(8,128)(2,1)S(1)} %get-tuple-element.29), channel_id=1, source_target_pairs={{0,8},{4,12},{8,0},{12,4},{1,9},{5,13},{9,1},{13,5},{2,10},{6,14},... | collective-permute-start | bytes 245768 | tf_op jit(solution)/shard_map/ppermute | solution.py:359
  7.1 6.9 %collective-permute-start.2 = (bf16[80,512]{1,0:T(8,128)(2,1)S(1)}, bf16[80,512]{1,0:T(8,128)(2,1)S(1)}, u32[]{:S(2)}, u32[]{:S(2)}) collective-permute-start(bf16[80,512]{1,0:T(8,128)(2,1)S(1)} %get-tuple-element.30), channel_id=1, source_target_pairs={{0,4},{4,0},{8,12},{12,8},{1,5},{5,1},{9,13},{13,9},{2,6},{6,2},{1... | collective-permute-start | bytes 245768 | tf_op jit(solution)/shard_map/ppermute | solution.py:359
  14.0 5.5 %collective-permute-start.4 = (bf16[160,512]{1,0:T(8,128)(2,1)S(1)}, bf16[160,512]{1,0:T(8,128)(2,1)S(1)}, u32[]{:S(2)}, u32[]{:S(2)}) collective-permute-start(bf16[160,512]{1,0:T(8,128)(2,1)S(1)} %get-tuple-element.33), channel_id=1, source_target_pairs={{0,2},{1,3},{2,0},{3,1},{4,6},{5,7},{6,4},{7,5},{8,10},{9,11},{10,... | collective-permute-start | bytes 491528 | tf_op jit(solution)/shard_map/ppermute | solution.py:359
  15.6 4.7 %collective-permute-start.3 = (bf16[160,512]{1,0:T(8,128)(2,1)S(1)}, bf16[160,512]{1,0:T(8,128)(2,1)S(1)}, u32[]{:S(2)}, u32[]{:S(2)}) collective-permute-start(bf16[160,512]{1,0:T(8,128)(2,1)S(1)} %get-tuple-element.32.refs_0_.refs_1_), channel_id=1, source_target_pairs={{0,1},{1,0},{2,3},{3,2},{4,5},{5,4},{6,7},{7,6},{8,9},{9,8},{10,11... | collective-permute-start | bytes 491528 | tf_op jit(solution)/shard_map/ppermute | solution.py:359
  19.5 1.4 %collective-permute-start.5 = (bf16[160,512]{1,0:T(8,128)(2,1)S(1)}, bf16[160,512]{1,0:T(8,128)(2,1)S(1)}, u32[]{:S(2)}, u32[]{:S(2)}) collective-permute-start(bf16[160,512]{1,0:T(8,128)(2,1)S(1)} %hold.6.refs_2_), channel_id=1, source_target_pairs={{0,1},{1,0},{2,3},{3,2},{4,5},{5,4},{6,7},{7,6},{8,9},{9,8},{10,11... | collective-permute-start | bytes 491528 | tf_op jit(solution)/shard_map/ppermute | solution.py:359
  19.5 8.7 %collective-permute-start.6 = (f32[4,128,128]{2,1,0:T(8,128)S(1)}, f32[4,128,128]{2,1,0:T(8,128)S(1)}, u32[]{:S(2)}, u32[]{:S(2)}) collective-permute-start(f32[4,128,128]{2,1,0:T(8,128)S(1)} %hold.7.refs_0_), channel_id=1, source_target_pairs={{0,4},{4,0},{8,12},{12,8},{1,5},{5,1},{9,13},{13,9},{2,6},{6,2},{1... | collective-permute-start | bytes 786440 | tf_op jit(solution)/shard_map/ppermute | solution.py:359
  22.4 11.3 %collective-permute-start.10 = (bf16[120,1152]{1,0:T(8,128)(2,1)S(1)}, bf16[120,1152]{1,0:T(8,128)(2,1)S(1)}, u32[]{:S(2)}, u32[]{:S(2)}) collective-permute-start(bf16[120,1152]{1,0:T(8,128)(2,1)S(1)} %get-tuple-element.43), channel_id=1, source_target_pairs={{0,2},{1,3},{2,0},{3,1},{4,6},{5,7},{6,4},{7,5},{8,10},{9,11},{10,... | collective-permute-start | bytes 829448 | tf_op jit(solution)/shard_map/ppermute | solution.py:359
  25.7 12.2 %collective-permute-start.8 = (bf16[120,1024]{1,0:T(8,128)(2,1)S(1)}, bf16[120,1024]{1,0:T(8,128)(2,1)S(1)}, u32[]{:S(2)}, u32[]{:S(2)}) collective-permute-start(bf16[120,1024]{1,0:T(8,128)(2,1)S(1)} %get-tuple-element.42), channel_id=1, source_target_pairs={{0,2},{1,3},{2,0},{3,1},{4,6},{5,7},{6,4},{7,5},{8,10},{9,11},{10,... | collective-permute-start | bytes 737288 | tf_op jit(solution)/shard_map/ppermute | solution.py:359
  28.3 8.9 %collective-permute-start.9 = (bf16[4,128,128]{2,1,0:T(8,128)(2,1)S(1)}, bf16[4,128,128]{2,1,0:T(8,128)(2,1)S(1)}, u32[]{:S(2)}, u32[]{:S(2)}) collective-permute-start(bf16[4,128,128]{2,1,0:T(8,128)(2,1)S(1)} %pair_sum.1.refs_6_.refs_0_), channel_id=1, source_target_pairs={{0,8},{4,12},{8,0},{12,4},{1,9},{5,13},{9,1},{13,5},{2,10},{6,14},... | collective-permute-start | bytes 393224 | tf_op jit(solution)/shard_map/ppermute | solution.py:359
  32.0 11.6 %collective-permute-start.7 = (bf16[120,1408]{1,0:T(8,128)(2,1)S(1)}, bf16[120,1408]{1,0:T(8,128)(2,1)S(1)}, u32[]{:S(2)}, u32[]{:S(2)}) collective-permute-start(bf16[120,1408]{1,0:T(8,128)(2,1)S(1)} %get-tuple-element.38), channel_id=1, source_target_pairs={{0,2},{1,3},{2,0},{3,1},{4,6},{5,7},{6,4},{7,5},{8,10},{9,11},{10,... | collective-permute-start | bytes 1013768 | tf_op jit(solution)/shard_map/ppermute | solution.py:359
  33.7 5.1 %collective-permute-start.12 = (bf16[120,1152]{1,0:T(8,128)(2,1)S(1)}, bf16[120,1152]{1,0:T(8,128)(2,1)S(1)}, u32[]{:S(2)}, u32[]{:S(2)}) collective-permute-start(bf16[120,1152]{1,0:T(8,128)(2,1)S(1)} %hold.8.refs_0_), channel_id=1, source_target_pairs={{0,1},{1,0},{2,3},{3,2},{4,5},{5,4},{6,7},{7,6},{8,9},{9,8},{10,11... | collective-permute-start | bytes 829448 | tf_op jit(solution)/shard_map/ppermute | solution.py:359
  37.9 1.5 %collective-permute-start.11 = (bf16[120,1024]{1,0:T(8,128)(2,1)S(1)}, bf16[120,1024]{1,0:T(8,128)(2,1)S(1)}, u32[]{:S(2)}, u32[]{:S(2)}) collective-permute-start(bf16[120,1024]{1,0:T(8,128)(2,1)S(1)} %hold.9.refs_0_), channel_id=1, source_target_pairs={{0,1},{1,0},{2,3},{3,2},{4,5},{5,4},{6,7},{7,6},{8,9},{9,8},{10,11... | collective-permute-start | bytes 737288 | tf_op jit(solution)/shard_map/ppermute | solution.py:359
  37.9 8.2 %collective-permute-start.14 = (bf16[160,1792]{1,0:T(8,128)(2,1)S(1)}, bf16[160,1792]{1,0:T(8,128)(2,1)S(1)}, u32[]{:S(2)}, u32[]{:S(2)}) collective-permute-start(bf16[160,1792]{1,0:T(8,128)(2,1)S(1)} %get-tuple-element.40.refs_0_), channel_id=1, source_target_pairs={{0,1},{1,0},{2,3},{3,2},{4,5},{5,4},{6,7},{7,6},{8,9},{9,8},{10,11... | collective-permute-start | bytes 1720328 | tf_op jit(solution)/shard_map/ppermute | solution.py:359
  38.4 7.7 %collective-permute-start.15 = (bf16[160,1792]{1,0:T(8,128)(2,1)S(1)}, bf16[160,1792]{1,0:T(8,128)(2,1)S(1)}, u32[]{:S(2)}, u32[]{:S(2)}) collective-permute-start(bf16[160,1792]{1,0:T(8,128)(2,1)S(1)} %get-tuple-element.41.refs_1_), channel_id=1, source_target_pairs={{0,1},{1,0},{2,3},{3,2},{4,5},{5,4},{6,7},{7,6},{8,9},{9,8},{10,11... | collective-permute-start | bytes 1720328 | tf_op jit(solution)/shard_map/ppermute | solution.py:359
  43.6 2.0 %collective-permute-start.13 = (bf16[120,1408]{1,0:T(8,128)(2,1)S(1)}, bf16[120,1408]{1,0:T(8,128)(2,1)S(1)}, u32[]{:S(2)}, u32[]{:S(2)}) collective-permute-start(bf16[120,1408]{1,0:T(8,128)(2,1)S(1)} %hold.10.refs_0_), channel_id=1, source_target_pairs={{0,1},{1,0},{2,3},{3,2},{4,5},{5,4},{6,7},{7,6},{8,9},{9,8},{10,11... | collective-permute-start | bytes 1013768 | tf_op jit(solution)/shard_map/ppermute | solution.py:359
  43.7 9.2 %collective-permute-start.16 = (bf16[40,3584]{1,0:T(8,128)(2,1)S(1)}, bf16[40,3584]{1,0:T(8,128)(2,1)S(1)}, u32[]{:S(2)}, u32[]{:S(2)}) collective-permute-start(bf16[40,3584]{1,0:T(8,128)(2,1)S(1)} %get-tuple-element.44.refs_1_), channel_id=1, source_target_pairs={{0,2},{1,3},{2,0},{3,1},{4,6},{5,7},{6,4},{7,5},{8,10},{9,11},{10,... | collective-permute-start | bytes 860168 | tf_op jit(solution)/shard_map/ppermute | solution.py:359
  46.9 7.2 %collective-permute-start.17 = (bf16[80,512]{1,0:T(8,128)(2,1)S(1)}, bf16[80,512]{1,0:T(8,128)(2,1)S(1)}, u32[]{:S(2)}, u32[]{:S(2)}) collective-permute-start(bf16[80,512]{1,0:T(8,128)(2,1)S(1)} %get-tuple-element.47), channel_id=1, source_target_pairs={{0,12},{4,8},{8,4},{12,0},{1,13},{5,9},{9,5},{13,1},{2,14},{6,10},... | collective-permute-start | bytes 245768 | tf_op jit(solution)/shard_map/ppermute | solution.py:359
  49.5 7.5 %collective-permute-start.18 = (bf16[80,512]{1,0:T(8,128)(2,1)S(1)}, bf16[80,512]{1,0:T(8,128)(2,1)S(1)}, u32[]{:S(2)}, u32[]{:S(2)}) collective-permute-start(bf16[80,512]{1,0:T(8,128)(2,1)S(1)} %get-tuple-element.48), channel_id=1, source_target_pairs={{0,8},{4,12},{8,0},{12,4},{1,9},{5,13},{9,1},{13,5},{2,10},{6,14},... | collective-permute-start | bytes 245768 | tf_op jit(solution)/shard_map/ppermute | solution.py:359
  49.5 7.5 %collective-permute-start.19 = (bf16[80,512]{1,0:T(8,128)(2,1)S(1)}, bf16[80,512]{1,0:T(8,128)(2,1)S(1)}, u32[]{:S(2)}, u32[]{:S(2)}) collective-permute-start(bf16[80,512]{1,0:T(8,128)(2,1)S(1)} %get-tuple-element.49), channel_id=1, source_target_pairs={{0,4},{4,0},{8,12},{12,8},{1,5},{5,1},{9,13},{13,9},{2,6},{6,2},{1... | collective-permute-start | bytes 245768 | tf_op jit(solution)/shard_map/ppermute | solution.py:359
  57.0 1.6 %collective-permute-start.20 = (bf16[40,3584]{1,0:T(8,128)(2,1)S(1)}, bf16[40,3584]{1,0:T(8,128)(2,1)S(1)}, u32[]{:S(2)}, u32[]{:S(2)}) collective-permute-start(bf16[40,3584]{1,0:T(8,128)(2,1)S(1)} %hold.11.refs_0_), channel_id=1, source_target_pairs={{0,1},{1,0},{2,3},{3,2},{4,5},{5,4},{6,7},{7,6},{8,9},{9,8},{10,11... | collective-permute-start | bytes 860168 | tf_op jit(solution)/shard_map/ppermute | solution.py:359
  60.3 1.9 %collective-permute-start.21 = (f32[8,128]{1,0:T(8,128)S(1)}, f32[8,128]{1,0:T(8,128)S(1)}, u32[]{:S(2)}, u32[]{:S(2)}) collective-permute-start(f32[8,128]{1,0:T(8,128)S(1)} %get-tuple-element.51.refs_0_), channel_id=1, source_target_pairs={{0,1},{1,0},{2,3},{3,2},{4,5},{5,4},{6,7},{7,6},{8,9},{9,8},{10,11... | collective-permute-start | bytes 12296 | tf_op jit(solution)/shard_map/ppermute | solution.py:359
  60.4 3.6 %collective-permute-start.22 = (f32[8,128]{1,0:T(8,128)S(1)}, f32[8,128]{1,0:T(8,128)S(1)}, u32[]{:S(2)}, u32[]{:S(2)}) collective-permute-start(f32[8,128]{1,0:T(8,128)S(1)} %get-tuple-element.51.refs_0_), channel_id=1, source_target_pairs={{0,2},{1,3},{2,0},{3,1},{4,6},{5,7},{6,4},{7,5},{8,10},{9,11},{10,... | collective-permute-start | bytes 12296 | tf_op jit(solution)/shard_map/ppermute | solution.py:359
  61.6 3.0 %collective-permute-start.23 = (f32[8,128]{1,0:T(8,128)S(1)}, f32[8,128]{1,0:T(8,128)S(1)}, u32[]{:S(2)}, u32[]{:S(2)}) collective-permute-start(f32[8,128]{1,0:T(8,128)S(1)} %get-tuple-element.51.refs_0_), channel_id=1, source_target_pairs={{0,3},{1,2},{2,1},{3,0},{4,7},{5,6},{6,5},{7,4},{8,11},{9,10},{10,... | collective-permute-start | bytes 12296 | tf_op jit(solution)/shard_map/ppermute | solution.py:359
  (9 other events, 75.1 us)
